TPU v7x, 32 devices: a whole 2x2x4 slice. The times are simulated.
32 devices in a mesh: head: 4 (over y, core), seq: 8 (over z, x).
Axes of the slice: x: 2, y: 2, z: 4, core: 2. Of those that a mesh axis runs over, the one named last changes fastest.
Arguments:
- block_in: bfloat16 [4096, 2048], P(('seq', 'head')), may hold values from -6 to 6
- out_cot: bfloat16 [4096, 2048], P(('seq', 'head')), may hold values from -6 to 6
- gain_one: bfloat16 [2048], replicated, may hold values from 0.5 to 1.5
- qkv_weight: bfloat16 [2048, 16, 512], P(None, 'head'), may hold values from -0.125 to 0.125
- conv_weight: bfloat16 [4, 16, 512], P(None, 'head'), may hold values from -3 to 3
- gate_weight: bfloat16 [2048, 16, 256], P(None, 'head'), may hold values from -0.125 to 0.125
- gain_out: bfloat16 [256], replicated, may hold values from 0.5 to 1.5
- out_weight: bfloat16 [16, 256, 2048], P('head'), may hold values from -0.09375 to 0.09375
- gain_two: bfloat16 [2048], replicated, may hold values from 0.5 to 1.5
- mlp_gate: bfloat16 [2048, 5632], P(None, 'seq'), may hold values from -0.125 to 0.125
- mlp_up: bfloat16 [2048, 5632], P(None, 'seq'), may hold values from -0.125 to 0.125
- mlp_down: bfloat16 [5632, 2048], P('seq'), may hold values from -0.078125 to 0.078125
- decay_code: int32 [4096, 16], P('seq', 'head'), may hold values from 0 to 1024, as said below
- beta_code: int32 [4096, 16], P('seq', 'head'), may hold values from 0 to 256
Outputs:
- output: bfloat16 [4096, 2048], P(('seq', 'head'))
- d_input: bfloat16 [4096, 2048], P(('seq', 'head'))
- grad_gain_one: float32 [2048], P(('head', 'seq'))
- grad_qkv: float32 [2048, 16, 512], P('seq', 'head')
- grad_conv: float32 [4, 16, 512], P(None, 'head', 'seq')
- grad_gate: float32 [2048, 16, 256], P('seq', 'head')
- grad_gain_out: float32 [256], P(('head', 'seq'))
- grad_out: float32 [16, 256, 2048], P('head', None, 'seq')
- grad_gain_two: float32 [2048], P(('head', 'seq'))
- grad_mlp_gate: float32 [2048, 5632], P('head', 'seq')
- grad_mlp_up: float32 [2048, 5632], P('head', 'seq')
- grad_mlp_down: float32 [5632, 2048], P('seq', 'head')
Inputs may be any that keep to these rules, and one draw needn't show every extreme that they name: `decay_code`: values to 1023 grade a head's forgetting at a token; 1024 marks a token at which the head's state loses a fixed share at once.
All inputs are finite; a program needn't handle non-finite values.
Results may differ from a plain program's by a relative error of at most 0.025.
Values may be sent and summed in bfloat16 or wider, within the bound.
A program may use at most 256 MiB of HBM per device.

v0:
```python
import math

import jax
import jax.numpy as jnp
from jax import lax
from jax.sharding import PartitionSpec as P

DK = 128
DV = 256
STRETCH = 64


epsilon = 1e-06
exact_mode = lax.Precision.HIGHEST


def passed_along(value, axis, steps):
    count = lax.axis_size(axis)
    first, last = (max(0, -steps), min(count, count - steps))
    return lax.ppermute(value, axis, [(source, source + steps) for source in range(first, last)])


def carried_in(shard, axis, join, neutral, backward):
    count = lax.axis_size(axis)
    place = lax.axis_index(axis)
    ahead = count - 1 - place if backward else place
    gathered = jax.tree.map(
        lambda a, kind: lax.all_gather(a.astype(kind), axis), shard, (jnp.bfloat16, jnp.bfloat16)
    )
    state = jax.tree.map(lambda a, e: jnp.zeros_like(a) + jnp.asarray(e, a.dtype), shard, neutral)

    def one(turn, state):
        source = count - 1 - turn if backward else turn
        return join(
            state,
            jax.tree.map(
                lambda a, own: lax.dynamic_index_in_dim(a, source, 0, False).astype(own.dtype),
                gathered,
                shard,
            ),
        )

    return lax.fori_loop(0, ahead, one, state)


def exact_dot(form, left, right):
    return jnp.einsum(form, left, right, precision=exact_mode)


def rms_scale(tensor):
    return lax.rsqrt(jnp.mean(tensor * tensor, axis=-1, keepdims=True) + epsilon)


def unit_rows(tensor):
    return tensor * lax.rsqrt(jnp.sum(tensor * tensor, axis=-1, keepdims=True) + epsilon)


def log_rates(decay_code, total_len):
    code_level = decay_code.astype(jnp.float32) / 1023.0
    smooth = -jnp.exp(-code_level * math.log(total_len / 32.0)) / 32.0
    return jnp.where(decay_code == 1024, -0.25, smooth)


def conv_features(padded, conv_f):
    row_total = padded.shape[0] - conv_f.shape[0] + 1
    summed = conv_f[0] * padded[0:row_total]
    for tap_index in range(1, conv_f.shape[0]):
        summed = summed + conv_f[tap_index] * padded[tap_index : tap_index + row_total]
    activated = jax.nn.silu(summed)
    queries = unit_rows(activated[..., :DK]) * DK ** (-0.5)
    key_rows = unit_rows(activated[..., DK : 2 * DK])
    return (queries, key_rows, activated[..., 2 * DK :])


def decay_masks(decay_log):
    block_size = decay_log.shape[-1]
    row_ids = lax.broadcasted_iota(jnp.int32, (block_size, block_size), 0)
    col_ids = lax.broadcasted_iota(jnp.int32, (block_size, block_size), 1)
    causal = (row_ids >= col_ids).astype(jnp.float32)
    strict = (row_ids > col_ids).astype(jnp.float32)
    log_gaps = decay_log[..., :, None] - decay_log[..., None, :]
    within = jnp.exp(log_gaps * causal) * causal
    return (within, strict)


def solve_parts(key_blk, value_blk, decay_log, beta_blk):
    within, strict = decay_masks(decay_log)
    key_dots = exact_dot("...ik,...jk->...ij", key_blk, key_blk)
    lower_part = within * strict * key_dots * beta_blk[..., :, None]
    block_size = decay_log.shape[-1]
    system = jnp.eye(block_size, dtype=jnp.float32) + lower_part
    decay_run = jnp.exp(decay_log)
    right_side = jnp.concatenate(
        [beta_blk[..., None] * value_blk, (beta_blk * decay_run)[..., None] * key_blk], axis=-1
    )
    solved = jax.scipy.linalg.solve_triangular(system, right_side, lower=True, unit_diagonal=True)
    width_v = value_blk.shape[-1]
    return (solved[..., :width_v], solved[..., width_v:])


def piece_maps(key_blk, value_blk, decay_log, beta_blk):
    new_values, new_keys = solve_parts(key_blk, value_blk, decay_log, beta_blk)
    last_log = decay_log[..., -1:]
    tail_decay = jnp.exp(last_log - decay_log)
    key_width = key_blk.shape[-1]
    transit = jnp.exp(last_log)[..., None] * jnp.eye(key_width, dtype=jnp.float32) - exact_dot(
        "...ck,...cj->...kj", new_keys * tail_decay[..., None], key_blk
    )
    offsets = exact_dot("...cv,...ck->...vk", new_values * tail_decay[..., None], key_blk)
    return (new_values, new_keys, transit, offsets)


def stretch_out(query_blk, key_blk, decay_log, new_values, new_keys, states):
    within, strict = decay_masks(decay_log)
    decay_run = jnp.exp(decay_log)
    fresh_values = new_values - exact_dot("...ck,...vk->...cv", new_keys, states)
    scores = exact_dot("...ik,...jk->...ij", query_blk, key_blk) * within
    return decay_run[..., None] * exact_dot("...ck,...vk->...cv", query_blk, states) + exact_dot(
        "...ij,...jv->...iv", scores, fresh_values
    )


def head_branch(core, gate_pre, gain_head):
    return core * rms_scale(core) * gain_head * jax.nn.silu(gate_pre)


def compose(earlier, later):
    return (
        exact_dot("hij,hjk->hik", earlier[0], later[0]),
        exact_dot("hvj,hjk->hvk", earlier[1], later[0]) + later[1],
    )


def to_stretches(tensor):
    block_count = tensor.shape[0] // STRETCH
    return tensor.reshape((block_count, STRETCH) + tensor.shape[1:]).swapaxes(1, 2)


def from_stretches(tensor):
    moved = tensor.swapaxes(1, 2)
    return moved.reshape((moved.shape[0] * moved.shape[1],) + moved.shape[2:])


def chain_back(end_grad, transit, states, d_states):

    def retreat(state_grad, inputs):
        transit_blk, state_blk, d_state_blk = inputs
        d_transit = exact_dot("hvk,hvj->hkj", state_blk, state_grad)
        earlier_grad = exact_dot("hvj,hkj->hvk", state_grad, transit_blk) + d_state_blk
        return (earlier_grad, (d_transit, state_grad))

    return lax.scan(retreat, end_grad, (transit, states, d_states), reverse=True)


def silu_slope(tensor):
    sigmoid_part = jax.nn.sigmoid(tensor)
    return sigmoid_part * (1.0 + tensor * (1.0 - sigmoid_part))


def on_device(
    block_in,
    out_cot,
    gain_one,
    qkv_weight,
    conv_weight,
    gate_weight,
    gain_out,
    out_weight,
    gain_two,
    mlp_gate,
    mlp_up,
    mlp_down,
    decay_code,
    beta_code,
):
    span_rows = decay_code.shape[0]
    heads_here = qkv_weight.shape[1]
    total_len = span_rows * lax.axis_size("seq")
    input_f = block_in.astype(jnp.float32)
    gain_first = gain_one.astype(jnp.float32)
    gain_head = gain_out.astype(jnp.float32)
    gain_second = gain_two.astype(jnp.float32)
    conv_f = conv_weight.astype(jnp.float32)
    lead_rows = conv_f.shape[0] - 1
    gathered_in = lax.all_gather(block_in, "head", axis=0, tiled=True)
    wide_in = gathered_in.astype(jnp.float32)
    hat_first = wide_in * rms_scale(wide_in)
    normed_first = (hat_first * gain_first).astype(jnp.bfloat16)
    mixed_in = jnp.einsum(
        "td,dhc->thc", normed_first, qkv_weight, preferred_element_type=jnp.float32
    ).astype(jnp.bfloat16)
    gate_pre = jnp.einsum(
        "td,dhv->thv", normed_first, gate_weight, preferred_element_type=jnp.float32
    )
    tail_in = passed_along(mixed_in[span_rows - lead_rows :], "seq", 1)
    padded = jnp.concatenate([tail_in, mixed_in], 0).astype(jnp.float32)
    queries, key_rows, values = conv_features(padded, conv_f)
    rates = log_rates(decay_code, total_len)
    betas = 0.5 + beta_code.astype(jnp.float32) / 512.0
    query_ch = to_stretches(queries)
    key_ch = to_stretches(key_rows)
    value_ch = to_stretches(values)
    decay_ch = jnp.cumsum(to_stretches(rates), axis=-1)
    beta_ch = to_stretches(betas)
    new_values, new_keys, transit, offsets = piece_maps(key_ch, value_ch, decay_ch, beta_ch)
    eye_keys = jnp.broadcast_to(jnp.eye(DK, dtype=jnp.float32), (heads_here, DK, DK))
    zero_state = jnp.zeros((heads_here, DV, DK), jnp.float32)

    def fold_maps(carried, map_pair):
        return (compose(carried, map_pair), None)

    (whole_map, whole_shift), _ = lax.scan(fold_maps, (eye_keys, zero_state), (transit, offsets))
    start_state = carried_in(
        (whole_map, whole_shift), "seq", compose, (eye_keys, zero_state), False
    )[1]

    def advance(carried, map_pair):
        return (exact_dot("hvj,hjk->hvk", carried, map_pair[0]) + map_pair[1], carried)

    _, states = lax.scan(advance, start_state, (transit, offsets))
    core = from_stretches(stretch_out(query_ch, key_ch, decay_ch, new_values, new_keys, states))
    branch = head_branch(core, gate_pre, gain_head).astype(jnp.bfloat16)
    row_block = branch
    middle = input_f + lax.psum_scatter(
        jnp.einsum("thv,hvd->td", row_block, out_weight, preferred_element_type=jnp.float32).astype(
            jnp.bfloat16
        ),
        "head",
        scatter_dimension=0,
        tiled=True,
    ).astype(jnp.float32)
    scale_two = rms_scale(middle)
    hat_two = middle * scale_two
    normed_two = (hat_two * gain_second).astype(jnp.bfloat16)
    weight_gate, weight_up, weight_down = (mlp_gate, mlp_up, mlp_down)
    rows_out = lax.all_gather(normed_two, "seq", axis=0, tiled=True)
    gate_part = jnp.dot(rows_out, weight_gate, preferred_element_type=jnp.float32)
    up_part = jnp.dot(rows_out, weight_up, preferred_element_type=jnp.float32)
    hidden = (jax.nn.silu(gate_part) * up_part).astype(jnp.bfloat16)
    row_block = hidden
    mlp_out = lax.psum_scatter(
        jnp.dot(row_block, weight_down, preferred_element_type=jnp.float32).astype(jnp.bfloat16),
        "seq",
        scatter_dimension=0,
        tiled=True,
    ).astype(jnp.float32)
    output = (middle + mlp_out).astype(jnp.bfloat16)
    cot_f = out_cot.astype(jnp.float32)
    cot_all = lax.all_gather(out_cot, "seq", axis=0, tiled=True)
    grad_down = jnp.einsum("tf,td->fd", hidden, cot_all, preferred_element_type=jnp.float32)
    d_hidden = jnp.einsum("td,fd->tf", cot_all, weight_down, preferred_element_type=jnp.float32)
    d_gate_mlp = (d_hidden * up_part * silu_slope(gate_part)).astype(jnp.bfloat16)
    d_up_mlp = (d_hidden * jax.nn.silu(gate_part)).astype(jnp.bfloat16)
    grad_mgate = jnp.einsum("td,tf->df", rows_out, d_gate_mlp, preferred_element_type=jnp.float32)
    grad_mup = jnp.einsum("td,tf->df", rows_out, d_up_mlp, preferred_element_type=jnp.float32)
    d_normed_two = lax.psum_scatter(
        (
            jnp.einsum("tf,df->td", d_gate_mlp, weight_gate, preferred_element_type=jnp.float32)
            + jnp.einsum("tf,df->td", d_up_mlp, weight_up, preferred_element_type=jnp.float32)
        ).astype(jnp.bfloat16),
        "seq",
        scatter_dimension=0,
        tiled=True,
    ).astype(jnp.float32)
    gain_two_part = jnp.sum(d_normed_two * hat_two, 0)
    e_two = d_normed_two * gain_second
    d_middle = cot_f + scale_two * (
        e_two - hat_two * jnp.mean(e_two * hat_two, axis=-1, keepdims=True)
    )
    d_mix_all = lax.all_gather(d_middle.astype(jnp.bfloat16), "head", axis=0, tiled=True)
    grad_out_w = jnp.einsum("thv,td->hvd", branch, d_mix_all, preferred_element_type=jnp.float32)
    d_branch = jnp.einsum("td,hvd->thv", d_mix_all, out_weight, preferred_element_type=jnp.float32)
    _, branch_back = jax.vjp(head_branch, core, gate_pre, gain_head)
    d_core, d_gate_pre, gain_out_part = branch_back(d_branch)
    d_gate_low = d_gate_pre.astype(jnp.bfloat16)
    _, out_back = jax.vjp(stretch_out, query_ch, key_ch, decay_ch, new_values, new_keys, states)
    d_query_ch, d_key_one, d_decay_one, d_new_values, d_new_keys, d_states = out_back(
        to_stretches(d_core)
    )
    local_grad, _ = chain_back(zero_state, transit, states, d_states)
    end_grad = carried_in(
        (jnp.swapaxes(whole_map, 1, 2), local_grad), "seq", compose, (eye_keys, zero_state), True
    )[1]
    _, (d_transit, d_offsets) = chain_back(end_grad, transit, states, d_states)
    _, maps_back = jax.vjp(piece_maps, key_ch, value_ch, decay_ch, beta_ch)
    d_key_two, d_value_ch, d_decay_two, d_beta_two = maps_back(
        (d_new_values, d_new_keys, d_transit, d_offsets)
    )
    _, conv_back = jax.vjp(conv_features, padded, conv_f)
    d_padded, grad_conv = conv_back(
        (
            from_stretches(d_query_ch),
            from_stretches(d_key_one + d_key_two),
            from_stretches(d_value_ch),
        )
    )
    from_next = passed_along(d_padded[:lead_rows], "seq", -1)
    d_mixed = d_padded[lead_rows:].at[span_rows - lead_rows :].add(from_next).astype(jnp.bfloat16)
    grad_qkv = jnp.einsum("td,thc->dhc", normed_first, d_mixed, preferred_element_type=jnp.float32)
    grad_gate = jnp.einsum(
        "td,thv->dhv", normed_first, d_gate_low, preferred_element_type=jnp.float32
    )
    d_normed_part = jnp.einsum(
        "thc,dhc->td", d_mixed, qkv_weight, preferred_element_type=jnp.float32
    ) + jnp.einsum("thv,dhv->td", d_gate_low, gate_weight, preferred_element_type=jnp.float32)
    gain_one_part = jnp.sum(d_normed_part * hat_first, 0)
    d_normed_one, grad_mgate_h, grad_mup_h, grad_down_h, gain_one_h, gain_two_h, gain_out_h = (
        lax.psum_scatter(
            d_normed_part.astype(jnp.bfloat16), "head", scatter_dimension=0, tiled=True
        ).astype(jnp.float32),
        lax.psum_scatter(
            grad_mgate.astype(jnp.bfloat16), "head", scatter_dimension=0, tiled=True
        ).astype(jnp.float32),
        lax.psum_scatter(
            grad_mup.astype(jnp.bfloat16), "head", scatter_dimension=0, tiled=True
        ).astype(jnp.float32),
        lax.psum_scatter(
            grad_down.astype(jnp.bfloat16), "head", scatter_dimension=1, tiled=True
        ).astype(jnp.float32),
        lax.psum_scatter(
            gain_one_part.astype(jnp.bfloat16), "head", scatter_dimension=0, tiled=True
        ).astype(jnp.float32),
        lax.psum_scatter(
            gain_two_part.astype(jnp.bfloat16), "head", scatter_dimension=0, tiled=True
        ).astype(jnp.float32),
        lax.psum_scatter(
            gain_out_part.astype(jnp.bfloat16), "head", scatter_dimension=0, tiled=True
        ).astype(jnp.float32),
    )
    scale_own = rms_scale(input_f)
    hat_own = input_f * scale_own
    e_one = d_normed_one * gain_first
    d_input = (
        d_middle + scale_own * (e_one - hat_own * jnp.mean(e_one * hat_own, axis=-1, keepdims=True))
    ).astype(jnp.bfloat16)
    grad_qkv_s, grad_gate_s, grad_out_s, grad_conv_s, gain_one_g, gain_two_g, gain_out_g = (
        lax.psum_scatter(
            grad_qkv.astype(jnp.bfloat16), "seq", scatter_dimension=0, tiled=True
        ).astype(jnp.float32),
        lax.psum_scatter(
            grad_gate.astype(jnp.bfloat16), "seq", scatter_dimension=0, tiled=True
        ).astype(jnp.float32),
        lax.psum_scatter(
            grad_out_w.astype(jnp.bfloat16), "seq", scatter_dimension=2, tiled=True
        ).astype(jnp.float32),
        lax.psum_scatter(
            grad_conv.astype(jnp.bfloat16), "seq", scatter_dimension=2, tiled=True
        ).astype(jnp.float32),
        lax.psum_scatter(
            gain_one_h.astype(jnp.bfloat16), "seq", scatter_dimension=0, tiled=True
        ).astype(jnp.float32),
        lax.psum_scatter(
            gain_two_h.astype(jnp.bfloat16), "seq", scatter_dimension=0, tiled=True
        ).astype(jnp.float32),
        lax.psum_scatter(
            gain_out_h.astype(jnp.bfloat16), "seq", scatter_dimension=0, tiled=True
        ).astype(jnp.float32),
    )
    return (
        output,
        d_input,
        gain_one_g,
        grad_qkv_s,
        grad_conv_s,
        grad_gate_s,
        gain_out_g,
        grad_out_s,
        gain_two_g,
        grad_mgate_h,
        grad_mup_h,
        grad_down_h,
    )


def solution(mesh):
    in_specs = (
        P(("seq", "head"), None),
        P(("seq", "head"), None),
        P(),
        P(None, "head", None),
        P(None, "head", None),
        P(None, "head", None),
        P(),
        P("head", None, None),
        P(),
        P(None, "seq"),
        P(None, "seq"),
        P("seq", None),
        P("seq", "head"),
        P("seq", "head"),
    )
    out_specs = (
        P(("seq", "head"), None),
        P(("seq", "head"), None),
        P(("head", "seq")),
        P("seq", "head", None),
        P(None, "head", "seq"),
        P("seq", "head", None),
        P(("head", "seq")),
        P("head", None, "seq"),
        P(("head", "seq")),
        P("head", "seq"),
        P("head", "seq"),
        P("seq", "head"),
    )
    return jax.shard_map(
        on_device, mesh=mesh, in_specs=in_specs, out_specs=out_specs, check_vma=False
    )
```

profile of v0, /device:TPU:0, one launch (start us, length us, event | category | flops | bytes accessed | tf_op | source)
XLA Modules:
  0.0 1547.4 jit_solution(7451590957412185047)
XLA Ops:
  15.9 19.0 %all-gather.13.cloned.1.call-done = bf16[512,2048]{1,0:T(8,128)(2,1)} async-done(((bf16[128,2048]{1,0:T(8,128)(2,1)}), bf16[512,2048]{1,0:T(8,128)(2,1)}) %all-gather.13.cloned.1.call-update) | async-done | bytes 2097168 | tf_op jit(solution)/shard_map/all_gather | solution.py:185
  37.0 8.8 fusion.88
  46.5 4.5 collective-permute-start
  58.2 3.8 fusion.50
  70.2 158.7 %custom-call.13 = f32[8,4,1,64,64]{3,4,2,1,0:T(8,128)} custom-call(f32[8,4,1,64,64]{4,3,2,1,0:T(8,128)} %fusion.115), custom_call_target="InvertDiagBlocksLowerTriangular" | custom-call | tf_op jit(solution)/shard_map/jit(_solve_triangular)/vmap(vmap())/triangular_solve/custom-call.1 | solution.py:96
  232.5 3.4 fusion.57
  235.9 5.7 fusion.92
  241.6 5.3 multiply_subtract_fusion
  250.6 38.3 %while.89 = (s32[]{:T(128)}, f32[4,128,128]{1,2,0:T(8,128)}, f32[4,256,128]{1,2,0:T(8,128)S(1)}, f32[8,4,128,128]{2,3,1,0:T(8,128)}, f32[8,4,256,128]{2,3,1,0:T(8,128)}, /*index=5*/s32[]{:T(128)}, s32[]{:T(128)}) while((s32[]{:T(128)}, f32[4,128,128]{1,2,0:T(8,128)}, f32[4,256,128]{1,2,0:T(8,128)S(1)}, ...), condition=%wide.region_5.7_spmd.clone, body=%wide.region_4.6_spmd.clone.sunk | while | flops 302252032 | bytes 4195938 | solution.py:212
  291.7 4.3 convolution_multiply_fusion
  296.0 33.5 %all-gather.21.cloned.1.call-done = bf16[32,128,128]{2,1,0:T(8,128)(2,1)} async-done(((bf16[4,128,128]{2,1,0:T(8,128)(2,1)}), bf16[32,128,128]{2,1,0:T(8,128)(2,1)}) %all-gather.21.cloned.1.call-update) | async-done | bytes 1048592 | tf_op jit(solution)/shard_map/all_gather | solution.py:28
  329.5 50.8 %all-gather.23.cloned.1.call-done = bf16[32,256,128]{2,1,0:T(8,128)(2,1)} async-done(((bf16[4,256,128]{2,1,0:T(8,128)(2,1)}), bf16[32,256,128]{2,1,0:T(8,128)(2,1)}) %all-gather.23.cloned.1.call-update) | async-done | bytes 2097168 | tf_op jit(solution)/shard_map/all_gather | solution.py:28
  382.8 21.5 %while.86 = (s32[]{:T(128)}, f32[4,256,128]{1,2,0:T(8,128)S(1)}, f32[8,4,256,128]{2,3,1,0:T(8,128)}, f32[8,4,128,128]{2,3,1,0:T(8,128)}, f32[8,4,256,128]{2,3,1,0:T(8,128)}, /*index=5*/s32[]{:T(128)}) while((s32[]{:T(128)}, f32[4,256,128]{1,2,0:T(8,128)S(1)}, f32[8,4,256,128]{2,3,1,0:T(8,128)}, f32[8,4,128,128]{2,3,1,0:T(8,128)}, ...), condition=%wide.region_9.11_spmd, body=%wide.region_8.10_spmd.sunk | while | flops 201457664 | bytes 3933265 | solution.py:220
  404.3 5.9 slice_subtract_fusion
  412.8 3.6 multiply_reduce_fusion.5
  418.6 7.0 multiply_convert_fusion.3
  426.6 3.7 bitcast_convert_fusion
  430.6 59.3 %reduce-scatter.14.cloned.1.call-done = bf16[128,2048]{1,0:T(8,128)(2,1)} async-done(((bf16[512,2048]{1,0:T(8,128)(2,1)}), bf16[128,2048]{1,0:T(8,128)(2,1)}) %reduce-scatter.14.cloned.1.call-update) | async-done | bytes 524304 | tf_op jit(solution)/shard_map/reduce_scatter | solution.py:224
  493.8 72.9 %all-gather.15.cloned.1.call-done = bf16[1024,2048]{1,0:T(8,128)(2,1)} async-done(((bf16[128,2048]{1,0:T(8,128)(2,1)}), bf16[1024,2048]{1,0:T(8,128)(2,1)}) %all-gather.15.cloned.1.call-update) | async-done | bytes 4194320 | tf_op jit(solution)/shard_map/all_gather | solution.py:236
  566.8 8.0 fusion.203
  574.8 4.8 fusion.202
  579.6 61.1 %all-gather.17.cloned.1.call-done = bf16[1024,2048]{1,0:T(8,128)(2,1)} async-done(((bf16[128,2048]{1,0:T(8,128)(2,1)}), bf16[1024,2048]{1,0:T(8,128)(2,1)}) %all-gather.17.cloned.1.call-update) | async-done | bytes 4194320 | tf_op jit(solution)/shard_map/all_gather | solution.py:249
  640.7 8.4 multiply_convert_fusion
  649.1 3.5 fusion.204
  652.7 5.4 add_convert_fusion
  658.2 86.3 %reduce-scatter.18.cloned.1.call-done = bf16[128,2048]{1,0:T(8,128)(2,1)} async-done(((bf16[1024,2048]{1,0:T(8,128)(2,1)}), bf16[128,2048]{1,0:T(8,128)(2,1)}) %reduce-scatter.18.cloned.1.call-update) | async-done | bytes 524304 | tf_op jit(solution)/shard_map/reduce_scatter | solution.py:256
  752.1 20.3 %all-gather.19.cloned.1.call-done = bf16[512,2048]{1,0:T(8,128)(2,1)} async-done(((bf16[128,2048]{1,0:T(8,128)(2,1)}), bf16[512,2048]{1,0:T(8,128)(2,1)}) %all-gather.19.cloned.1.call-update) | async-done | bytes 2097168 | tf_op jit(solution)/shard_map/all_gather | solution.py:270
  772.4 7.7 multiply_reduce_fusion.4
  785.3 7.6 fusion.80
  793.0 10.2 convolution_add_fusion
  803.1 5.4 copy.298
  808.5 14.3 while.90
  823.8 7.3 convolution_convert_fusion.6
  831.2 7.4 convolution_convert_fusion.4
  838.7 7.3 convolution_convert_fusion.5
  846.8 4.5 fusion.106
  855.4 4.7 fusion.102
  861.1 4.4 fusion.51
  865.5 7.8 all-gather.27.cloned.1.call-done
  873.4 29.6 %while.87 = (s32[]{:T(128)}, f32[4,256,128]{1,2,0:T(8,128)S(1)}, s32[]{:T(128)}, bf16[8,4,128,128]{3,2,1,0:T(8,128)(2,1)}, bf16[8,4,256,128]{3,2,1,0:T(8,128)(2,...) while((s32[]{:T(128)}, f32[4,256,128]{1,2,0:T(8,128)S(1)}, s32[]{:T(128)}, ...), condition=%wide.region_21.23_spmd, body=%wide.region_20.22_spmd.sunk | while | flops 201588736 | bytes 3539099 | solution.py:43
  907.0 40.6 %while.88 = (s32[]{:T(128)}, f32[4,256,128]{1,2,0:T(8,128)S(1)}, f32[8,4,128,128]{3,2,1,0:T(8,128)}, f32[8,4,256,128]{2,3,1,0:T(8,128)}, f32[8,4,128,128]{3,2,1,...) while((s32[]{:T(128)}, f32[4,256,128]{1,2,0:T(8,128)S(1)}, ...), condition=%wide.region_23.25_spmd, body=%wide.region_22.24_spmd.sunk | while | flops 402784256 | bytes 5245037 | solution.py:152
  947.6 6.2 fusion.103
  953.9 6.3 fusion.98
  962.8 3.0 fusion.63
  968.4 3.8 fusion.62
  975.9 4.6 fusion.119
  988.3 4.9 multiply_reduce_fusion.3
  993.2 7.9 broadcast_multiply_fusion
  1004.3 7.0 pad_add_fusion
  1012.7 3.4 slice.136
  1018.7 12.0 fusion.46
  1030.7 6.4 convolution_convert_fusion.3
  1037.3 6.3 convolution_convert_fusion.1
  1044.3 6.3 convolution_convert_fusion.2
  1050.8 10.2 convolution_convert_fusion
  1072.9 5.9 all-reduce.20
  1079.0 18.9 %all-reduce.19 = (bf16[512]{0:T(512)(128)(2,1)S(1)}, bf16[64]{0:T(256)(128)(2,1)S(1)}, bf16[512]{0:T(512)(128)(2,1)S(1)}) all-reduce(bf16[512]{0:T(512)(128)(2,1)S(1)} %dynamic-slice.9, bf16[64]{0:T(256)(128)(2,1)S(1)} %dynamic-slice.13, bf16[512]{0:T(512)(128)(2,1)S(1)} %dynamic-slice.17), channel_id=11, replica_groups=mesh['head'=4,'seq'=8] {'seq'}, use_global_device_ids=true, to_apply=%region_30.32.clone | all-reduce | flops 1088 | bytes 4352
  1101.2 7.5 reduce-scatter.20.cloned.1.call-done
  1110.1 90.2 %reduce-scatter.16.cloned.1.call-done = bf16[128,2048]{1,0:T(8,128)(2,1)} async-done(((bf16[1024,2048]{1,0:T(8,128)(2,1)}), bf16[128,2048]{1,0:T(8,128)(2,1)}) %reduce-scatter.16.cloned.1.call-update) | async-done | bytes 524304 | tf_op jit(solution)/shard_map/reduce_scatter | solution.py:241
  1200.3 3.5 fusion.128
  1203.8 88.5 %reduce-scatter.26.cloned.1.call-done = bf16[4,256,256]{2,1,0:T(8,128)(2,1)} async-done(((bf16[4,256,2048]{2,1,0:T(8,128)(2,1)}), bf16[4,256,256]{2,1,0:T(8,128)(2,1)}) %reduce-scatter.26.cloned.1.call-update) | async-done | bytes 524304 | tf_op jit(solution)/shard_map/reduce_scatter | solution.py:343
  1294.4 89.6 %reduce-scatter.24.cloned.1.call-done = bf16[256,4,256]{2,0,1:T(8,128)(2,1)} async-done(((bf16[2048,4,256]{2,0,1:T(8,128)(2,1)}), bf16[256,4,256]{2,0,1:T(8,128)(2,1)}) %reduce-scatter.24.cloned.1.call-update) | async-done | bytes 524304 | tf_op jit(solution)/shard_map/reduce_scatter | solution.py:340
  1386.4 150.8 %reduce-scatter.22.cloned.1.call-done = bf16[256,4,512]{2,0,1:T(8,128)(2,1)} async-done(((bf16[2048,4,512]{2,0,1:T(8,128)(2,1)}), bf16[256,4,512]{2,0,1:T(8,128)(2,1)}) %reduce-scatter.22.cloned.1.call-update) | async-done | bytes 1048592 | tf_op jit(solution)/shard_map/reduce_scatter | solution.py:337
  1537.2 3.4 copy.316
  (501 shorter events, 258.5 us)
Async XLA Ops:
  7.2 633.5 %copy-start = (bf16[704,2048]{1,0:T(8,128)(2,1)S(1)}, bf16[704,2048]{1,0:T(8,128)(2,1)}, u32[]{:S(2)}) copy-start(bf16[704,2048]{1,0:T(8,128)(2,1)} %param.41) | copy-start | bytes 8650756
  7.2 27.7 %all-gather.13.cloned.1.call-start = ((), (), s32[]{:S(2)}) async-start(), calls=%async_computation.11 | async-start | bytes 2621440 | tf_op jit(solution)/shard_map/all_gather | solution.py:185
  7.9 321.5 %all-gather.21.cloned.1.call-start = ((), (), s32[]{:S(2)}) async-start(), calls=%async_computation.25 | async-start | bytes 1179648 | tf_op jit(solution)/shard_map/all_gather | solution.py:28
  8.7 37.1 %copy-start.62 = (f32[2048]{0:T(1024)}, f32[2048]{0:T(1024)S(1)}, u32[]{:S(2)}) copy-start(f32[2048]{0:T(1024)S(1)} %convert_element_type.232) | copy-start | bytes 24580
  12.0 279.7 %copy-start.43 = (f32[64,64]{1,0:T(8,128)}, f32[64,64]{1,0:T(8,128)S(1)}, u32[]{:S(2)}) copy-start(f32[64,64]{1,0:T(8,128)S(1)} %fusion.188) | copy-start | bytes 49156
  37.0 8.8 copy-start.85
  45.8 5.8 copy-start.36
  46.5 9.4 collective-permute-start
  51.6 240.0 %copy-start.41 = (f32[8,4,64]{2,1,0:T(4,128)}, f32[8,4,64]{2,1,0:T(4,128)S(1)}, u32[]{:S(2)}) copy-start(f32[8,4,64]{2,1,0:T(4,128)S(1)} %copy.269) | copy-start | bytes 24580
  51.7 178.8 %copy-start.45 = (f32[8,4,64]{2,1,0:T(4,128)}, f32[8,4,64]{2,1,0:T(4,128)S(1)}, u32[]{:S(2)}) copy-start(f32[8,4,64]{2,1,0:T(4,128)S(1)} %copy.272) | copy-start | bytes 24580
  235.8 5.8 copy-start.9
  250.6 41.0 %copy-start.100 = (bf16[256]{0:T(256)(128)(2,1)S(1)}, bf16[256]{0:T(256)(128)(2,1)}, u32[]{:S(2)}) copy-start(bf16[256]{0:T(256)(128)(2,1)} %param.36) | copy-start | bytes 1540
  250.6 41.1 %copy-start.73 = (f32[8,64,4]{1,0,2:T(8,128)S(1)}, f32[8,64,4]{1,0,2:T(8,128)}, u32[]{:S(2)}) copy-start(f32[8,64,4]{1,0,2:T(8,128)} %get-tuple-element.786) | copy-start | bytes 24580
  290.6 89.6 %all-gather.23.cloned.1.call-start = ((), (), s32[]{:S(2)}) async-start(), calls=%async_computation.26 | async-start | bytes 2359296 | tf_op jit(solution)/shard_map/all_gather | solution.py:28
  291.5 198.3 %reduce-scatter.14.cloned.1.call-start = ((), (), s32[]{:S(2)}) async-start(), calls=%async_computation.12 | async-start | bytes 2621440 | tf_op jit(solution)/shard_map/reduce_scatter | solution.py:224
  291.6 126.7 %copy-start.90 = (f32[256]{0:T(256)}, f32[256]{0:T(256)S(1)}, u32[]{:S(2)}) copy-start(f32[256]{0:T(256)S(1)} %convert_element_type.243) | copy-start | bytes 3076
  404.2 6.0 copy-start.2
  404.3 6.0 copy-start.20
  416.4 9.2 copy-start.71
  416.4 9.2 copy-start.76
  418.6 7.0 copy-start.33
  418.6 8.0 copy-start.94
  426.6 63.2 %copy-start.23 = (bf16[128,2048]{1,0:T(8,128)(2,1)S(1)}, bf16[128,2048]{1,0:T(8,128)(2,1)}, u32[]{:S(2)}) copy-start(bf16[128,2048]{1,0:T(8,128)(2,1)} %param.30) | copy-start | bytes 1572868
  430.3 136.5 %all-gather.15.cloned.1.call-start = ((), (), s32[]{:S(2)}) async-start(), calls=%async_computation.13 | async-start | bytes 4718592 | tf_op jit(solution)/shard_map/all_gather | solution.py:236
  430.6 144.2 %copy-start.48 = (f32[2048]{0:T(1024)}, f32[2048]{0:T(1024)S(1)}, u32[]{:S(2)}) copy-start(f32[2048]{0:T(1024)S(1)} %convert_element_type.247) | copy-start | bytes 24580
  491.1 83.6 %copy-start.82 = (f32[128]{0:T(128)}, f32[128]{0:T(128)S(1)}, u32[]{:S(2)}) copy-start(f32[128]{0:T(128)S(1)} %add_rsqrt_fusion.4) | copy-start | bytes 1540
  493.2 147.4 %all-gather.17.cloned.1.call-start = ((), (), s32[]{:S(2)}) async-start(), calls=%async_computation.15 | async-start | bytes 4718592 | tf_op jit(solution)/shard_map/all_gather | solution.py:249
  493.8 250.7 %reduce-scatter.18.cloned.1.call-start = ((), (), s32[]{:S(2)}) async-start(), calls=%async_computation.16 | async-start | bytes 4718592 | tf_op jit(solution)/shard_map/reduce_scatter | solution.py:256
  566.8 8.0 copy-start.96
  566.8 8.0 copy-start.97
  640.7 8.4 copy-start.98
  658.1 93.2 %copy-start.39 = (bf16[4,128,128]{2,1,0:T(8,128)(2,1)S(1)}, bf16[4,128,128]{2,1,0:T(8,128)(2,1)}, u32[]{:S(2)}) copy-start(bf16[4,128,128]{2,1,0:T(8,128)(2,1)} %copy.282) | copy-start | bytes 393220
  658.1 114.3 %all-gather.19.cloned.1.call-start = ((), (), s32[]{:S(2)}) async-start(), calls=%async_computation.17 | async-start | bytes 2621440 | tf_op jit(solution)/shard_map/all_gather | solution.py:270
  749.9 115.6 %all-gather.25.cloned.1.call-start = ((), (), s32[]{:S(2)}) async-start(), calls=%async_computation.27 | async-start | bytes 1179648 | tf_op jit(solution)/shard_map/all_gather | solution.py:28
  752.1 121.2 %all-gather.27.cloned.1.call-start = ((), (), s32[]{:S(2)}) async-start(), calls=%async_computation.28 | async-start | bytes 2359296 | tf_op jit(solution)/shard_map/all_gather | solution.py:28
  772.4 7.8 copy-start.72
  772.4 7.8 copy-start.34
  772.4 7.8 copy-start.37
  772.4 7.8 copy-start.77
  772.4 7.8 copy-start.91
  785.3 7.7 copy-start.18
  823.7 241.8 %reduce-scatter.32.cloned.1.call-start = ((), (), s32[]{:S(2)}) async-start(), calls=%async_computation.24 | async-start | bytes 3604480 | tf_op jit(solution)/shard_map/reduce_scatter | solution.py:317
  831.1 236.9 %reduce-scatter.30.cloned.1.call-start = ((), (), s32[]{:S(2)}) async-start(), calls=%async_computation.23 | async-start | bytes 3604480 | tf_op jit(solution)/shard_map/reduce_scatter | solution.py:314
  838.6 231.8 %reduce-scatter.28.cloned.1.call-start = ((), (), s32[]{:S(2)}) async-start(), calls=%async_computation.22 | async-start | bytes 3604480 | tf_op jit(solution)/shard_map/reduce_scatter | solution.py:311
  846.0 253.6 %reduce-scatter.34.cloned.1.call-start = ((), (), s32[]{:S(2)}) async-start(), calls=%async_computation.29 | async-start | bytes 147456
  947.6 6.3 copy-start.4
  953.9 6.3 copy-start.8
  953.9 6.3 copy-start.17
  953.9 6.3 copy-start.19
  975.9 7.0 copy-start.35
  980.5 7.0 slice-start
  1002.1 14.0 collective-permute-start.1
  1016.1 92.6 %reduce-scatter.20.cloned.1.call-start = ((), (), s32[]{:S(2)}) async-start(), calls=%async_computation.18 | async-start | bytes 2621440 | tf_op jit(solution)/shard_map/reduce_scatter | solution.py:308
  1030.7 169.6 %reduce-scatter.16.cloned.1.call-start = ((), (), s32[]{:S(2)}) async-start(), calls=%async_computation.14 | async-start | bytes 4718592 | tf_op jit(solution)/shard_map/reduce_scatter | solution.py:241
  1037.2 255.1 %reduce-scatter.26.cloned.1.call-start = ((), (), s32[]{:S(2)}) async-start(), calls=%async_computation.21 | async-start | bytes 4718592 | tf_op jit(solution)/shard_map/reduce_scatter | solution.py:343
  1043.6 340.4 %reduce-scatter.24.cloned.1.call-start = ((), (), s32[]{:S(2)}) async-start(), calls=%async_computation.20 | async-start | bytes 4718592 | tf_op jit(solution)/shard_map/reduce_scatter | solution.py:340
  1050.6 486.7 %reduce-scatter.22.cloned.1.call-start = ((), (), s32[]{:S(2)}) async-start(), calls=%async_computation.19 | async-start | bytes 9437184 | tf_op jit(solution)/shard_map/reduce_scatter | solution.py:337
  1065.5 7.4 copy-start.92
  1065.5 7.4 copy-start.81
  1065.5 7.4 copy-start.93
  1065.5 43.2 %copy-start.24 = (bf16[128,2048]{1,0:T(8,128)(2,1)S(1)}, bf16[128,2048]{1,0:T(8,128)(2,1)}, u32[]{:S(2)}) copy-start(bf16[128,2048]{1,0:T(8,128)(2,1)} %param.30) | copy-start | bytes 1572868
  1068.0 132.3 %copy-start.49 = (f32[2048]{0:T(1024)S(1)}, f32[2048]{0:T(1024)}, u32[]{:S(2)}) copy-start(f32[2048]{0:T(1024)} %copy-done.48) | copy-start | bytes 24580
  1068.0 132.3 %copy-start.83 = (f32[128]{0:T(128)S(1)}, f32[128]{0:T(128)}, u32[]{:S(2)}) copy-start(f32[128]{0:T(128)} %copy-done.82) | copy-start | bytes 1540
  1068.0 132.3 %copy-start.89 = (f32[128]{0:T(128)S(1)}, f32[128]{0:T(128)}, u32[]{:S(2)}) copy-start(f32[128]{0:T(128)} %copy-done.88) | copy-start | bytes 1540
  (65 other events, 186.1 us)
Sparse Core Ops, SparseCore 0:
  9.6 25.2 all-gather.12
  290.8 38.6 all-gather.20
  332.2 48.0 all-gather.22
  430.4 59.3 reduce-scatter.13
  493.3 73.3 all-gather.14
  569.0 71.6 all-gather.16
  658.2 86.1 reduce-scatter.17
  750.0 22.3 all-gather.18
  775.1 40.1 all-gather.24
  823.8 49.4 all-gather.26
  875.9 34.8 reduce-scatter.31
  913.3 36.3 reduce-scatter.29
  952.2 36.2 reduce-scatter.27
  1016.2 59.4 reduce-scatter.33
  1078.3 30.3 reduce-scatter.19
  1112.2 88.0 reduce-scatter.15
  1204.2 88.0 reduce-scatter.25
  1295.8 88.1 reduce-scatter.23
  1388.1 149.0 reduce-scatter.21
where the time goes:
time: 1560 us; the launch traced here: 1550 us
  waiting for transfers between devices  839 us (54%)
  matrix products  327 us (21%)
  other arithmetic  232 us (15%)
  local copies, waits for them, and re-layouts  97.1 us (6%)
  blocking collectives  24.8 us (2%)
  between operations  18.3 us (1%)
    dot_general x76, matrix products, exact_dot(): return jnp.einsum(form, left, right, precision=exact_mode)  190 us
    another operation x4, other arithmetic, solve_parts(): jax.scipy.linalg.solve_triangular(system, right_side, lower=True, unit_di...  160 us
    reduce_scatter x1, waiting for transfers between devices, on_device(): lax.psum_scatter(grad_qkv.astype(jnp.bfloat16), 'seq', scatter_dimension=...  151 us
    all_gather x4, waiting for transfers between devices, carried_in(): lax.all_gather(a.astype(kind), axis)  92.1 us
    reduce_scatter x1, waiting for transfers between devices, on_device(): lax.psum_scatter(jnp.dot(row_block, weight_down, preferred_element_type=j...  90.2 us
    reduce_scatter x1, waiting for transfers between devices, on_device(): lax.psum_scatter(grad_gate.astype(jnp.bfloat16), 'seq', scatter_dimension...  89.6 us
    reduce_scatter x1, waiting for transfers between devices, on_device(): lax.psum_scatter(grad_out_w.astype(jnp.bfloat16), 'seq', scatter_dimensio...  88.5 us
    reduce_scatter x1, waiting for transfers between devices, on_device(): lax.psum_scatter((jnp.einsum('tf,df->td', d_gate_mlp, weight_gate, prefer...  86.3 us
  transfers between devices with their start and end apart: 21, of which 14 were waited for; matrix products, arithmetic and copies ran while one was open for 21% of the time, Pallas kernels for 0%

commit v1 on v0

v1 whole, which is shorter than its diff:
```python
import functools
import math

import jax
import jax.numpy as jnp
from jax import lax
from jax.experimental import pallas as pl
from jax.experimental.pallas import tpu as pltpu
from jax.sharding import PartitionSpec as P

DK = 128
DV = 256
STRETCH = 64
GROUP = 4 * STRETCH
INNER = 2 * DK + DV
BETA, GAMMA, BETA_GAMMA, TAIL, LAST, RUN = range(6)

epsilon = 1e-06
bf16 = jnp.bfloat16
f32 = jnp.float32
VMEM_BYTES = 48 * 2**20


def passed_along(value, axis, steps):
    count = lax.axis_size(axis)
    first, last = (max(0, -steps), min(count, count - steps))
    return lax.ppermute(value, axis, [(source, source + steps) for source in range(first, last)])


def rms_scale(tensor):
    return lax.rsqrt(jnp.mean(tensor * tensor, axis=-1, keepdims=True) + epsilon)


def log_rates(decay_code, total_len):
    code_level = decay_code.astype(f32) / 1023.0
    smooth = -jnp.exp(-code_level * math.log(total_len / 32.0)) / 32.0
    return jnp.where(decay_code == 1024, -0.25, smooth)


def token_columns(decay_code, beta_code, total_len):
    rows, heads = decay_code.shape
    rates = log_rates(decay_code, total_len)
    run = jnp.cumsum(rates.reshape(rows // STRETCH, STRETCH, heads), axis=1)
    last = jnp.broadcast_to(run[:, -1:], run.shape).reshape(rows, heads)
    run = run.reshape(rows, heads)
    beta = 0.5 + beta_code.astype(f32) / 512.0
    gamma = jnp.exp(run)
    columns = jnp.concatenate(
        [beta, gamma, beta * gamma, jnp.exp(last - run), jnp.exp(last), run], axis=1
    )
    columns = jnp.pad(columns, ((0, 0), (0, 128 - columns.shape[1])))
    run_rows = jnp.pad(run.T, ((0, 8 - heads % 8), (0, 0)))
    return columns, run_rows


def mm(left, right):
    return jnp.dot(left, right, preferred_element_type=f32)


def mm_nt(left, right):
    return lax.dot_general(left, right, (((1,), (1,)), ((), ())), preferred_element_type=f32)


def mm_tn(left, right):
    return lax.dot_general(left, right, (((0,), (0,)), ((), ())), preferred_element_type=f32)


def column(columns_ref, kind, head, heads):
    block = columns_ref[...]
    lanes = lax.broadcasted_iota(jnp.int32, block.shape, 1)
    return jnp.sum(jnp.where(lanes == kind * heads + head, block, 0.0), axis=1, keepdims=True)


def square_ids():
    return (
        lax.broadcasted_iota(jnp.int32, (GROUP, GROUP), 0),
        lax.broadcasted_iota(jnp.int32, (GROUP, GROUP), 1),
    )


def convolved(padded_ref, tail_ref, mixed_ref, taps_ref):
    rows = mixed_ref.shape[0]
    count = taps_ref.shape[0]
    padded_ref[0:8, :] = tail_ref[...]
    padded_ref[8 : 8 + rows, :] = mixed_ref[...].astype(f32)
    taps = taps_ref[...].astype(f32)
    start = 9 - count
    total = taps[0:1] * padded_ref[start : start + rows, :]
    for tap in range(1, count):
        total += taps[tap : tap + 1] * padded_ref[start + tap : start + tap + rows, :]
    return total


def chunk_masks_stack(transposed):
    lanes = lax.broadcasted_iota(jnp.int32, transposed.shape, 1) // STRETCH
    parts = [jnp.where(lanes == part, transposed, 0.0) for part in range(GROUP // STRETCH)]
    return jnp.concatenate(parts, axis=0).astype(bf16)


def local_forward(
    mixed_ref,
    tail_ref,
    taps_ref,
    columns_ref,
    run_rows_ref,
    solve_ref,
    score_ref,
    fresh_ref,
    reach_ref,
    inner_ref,
    turn_ref,
    local_ref,
    end_ref,
    padded,
    turn_t,
    offsets,
):
    head = pl.program_id(0)
    heads = pl.num_programs(0)
    rows = mixed_ref.shape[0]
    per_group = GROUP // STRETCH
    stretches = rows // STRETCH
    total = convolved(padded, tail_ref, mixed_ref, taps_ref)
    activated = total * jax.nn.sigmoid(total)
    raw_q, raw_k = activated[:, :DK], activated[:, DK : 2 * DK]
    queries = raw_q * (
        lax.rsqrt(jnp.sum(raw_q * raw_q, axis=1, keepdims=True) + epsilon) * DK ** (-0.5)
    )
    keys = raw_k * lax.rsqrt(jnp.sum(raw_k * raw_k, axis=1, keepdims=True) + epsilon)
    values = activated[:, 2 * DK :]
    beta = column(columns_ref, BETA, head, heads)
    gamma = column(columns_ref, GAMMA, head, heads)
    beta_gamma = column(columns_ref, BETA_GAMMA, head, heads)
    tail_decay = column(columns_ref, TAIL, head, heads)
    last = column(columns_ref, LAST, head, heads)
    run = column(columns_ref, RUN, head, heads)
    row_id, col_id = square_ids()
    same = row_id // STRETCH == col_id // STRETCH
    causal = same & (row_id >= col_id)
    diagonal = row_id == col_id
    eye = jnp.where(
        lax.broadcasted_iota(jnp.int32, (DK, DK), 0) == lax.broadcasted_iota(jnp.int32, (DK, DK), 1),
        1.0,
        0.0,
    )
    for group in range(rows // GROUP):
        span = slice(group * GROUP, (group + 1) * GROUP)
        key_b = keys[span].astype(bf16)
        query_b = queries[span].astype(bf16)
        gaps = run[span] - run_rows_ref[pl.ds(head, 1), span]
        within = jnp.exp(jnp.where(causal, gaps, -1e30))
        lower = jnp.where(diagonal, 0.0, beta[span] * within * mm_nt(key_b, key_b))
        solve = jnp.where(diagonal, 1.0, jnp.where(row_id // 2 == col_id // 2, -lower, 0.0))
        size = 2
        while size < STRETCH:
            crossing = (row_id // (2 * size) == col_id // (2 * size)) & (
                row_id // size != col_id // size
            )
            solve_b = solve.astype(bf16)
            half = mm(solve_b, jnp.where(crossing, lower, 0.0).astype(bf16))
            solve = solve - mm(half.astype(bf16), solve_b)
            size *= 2
        solve_b = solve.astype(bf16)
        right = jnp.concatenate([beta[span] * values[span], beta_gamma[span] * keys[span]], axis=1)
        fresh_b = mm(solve_b, right.astype(bf16)).astype(bf16)
        score_b = (within * mm_nt(query_b, key_b)).astype(bf16)
        scored = mm(score_b, fresh_b)
        solve_ref[group] = solve_b
        score_ref[group] = score_b
        fresh_ref[span, :] = fresh_b
        inner_ref[span, :] = scored[:, :DV]
        reach_ref[span, :] = (gamma[span] * queries[span] - scored[:, DV:]).astype(bf16)
        tail_keys = (tail_decay[span] * keys[span]).T
        moved = mm(chunk_masks_stack(tail_keys), fresh_b)
        for part in range(per_group):
            at = group * per_group + part
            block = moved[part * DK : (part + 1) * DK]
            stay = last[at * STRETCH : at * STRETCH + 1]
            turned = stay * eye - block[:, DV:]
            turn_t[head, at] = turned.astype(bf16)
            turn_ref[at] = turned.T.astype(bf16)
            offsets[head, at] = block[:, :DV]

    @pl.when(head == heads - 1)
    def _():
        states = [
            jnp.concatenate([jnp.zeros((DK, DV), f32), eye], axis=1)
            for _ in range(local_ref.shape[0])
        ]
        for at in range(stretches):
            for h in range(len(states)):
                state_b = states[h].astype(bf16)
                local_ref[h, at] = state_b
                moved = mm(turn_t[h, at], state_b)
                states[h] = jnp.concatenate(
                    [moved[:, :DV] + offsets[h, at], moved[:, DV:]], axis=1
                )
        for h in range(len(states)):
            end_ref[h] = states[h].astype(bf16)


def finish_forward(
    ends_ref, local_ref, reach_ref, inner_ref, gate_ref, gain_ref, state_ref, core_ref, branch_ref, start
):
    head = pl.program_id(0)
    heads, stretches = start.shape[0], local_ref.shape[0]

    @pl.when(head == 0)
    def _():
        start[...] = jnp.zeros_like(start)

        def one(source, carry):
            for h in range(heads):
                start[h] = (
                    mm(ends_ref[source, h, :, DV:], start[h].astype(bf16))
                    + ends_ref[source, h, :, :DV].astype(f32)
                )
            return carry

        lax.fori_loop(0, lax.axis_index("seq"), one, 0)

    start_b = start[head].astype(bf16)
    cores = []
    for at in range(stretches):
        state_b = (
            local_ref[at, :, :DV].astype(f32) + mm(local_ref[at, :, DV:], start_b)
        ).astype(bf16)
        state_ref[at] = state_b
        span = slice(at * STRETCH, (at + 1) * STRETCH)
        cores.append(inner_ref[span, :] + mm(reach_ref[span, :], state_b))
    core = jnp.concatenate(cores, axis=0)
    core_ref[...] = core
    gate = gate_ref[...]
    branch = core * rms_scale(core) * gain_ref[...].astype(f32) * (gate * jax.nn.sigmoid(gate))
    branch_ref[...] = branch.astype(bf16)


def local_backward(
    d_branch_ref,
    core_ref,
    gate_ref,
    gain_ref,
    reach_ref,
    turn_ref,
    d_core_ref,
    d_gate_ref,
    gain_part_ref,
    local_ref,
    end_ref,
    pulls,
):
    head = pl.program_id(0)
    heads = pl.num_programs(0)
    rows = core_ref.shape[0]
    per_group = GROUP // STRETCH
    stretches = rows // STRETCH
    core = core_ref[...]
    gate = gate_ref[...]
    gain = gain_ref[...].astype(f32)
    d_branch = d_branch_ref[...]
    scale = rms_scale(core)
    nhat = core * scale
    sig = jax.nn.sigmoid(gate)
    gated = d_branch * (gate * sig)

    @pl.when(head == 0)
    def _():
        gain_part_ref[...] = jnp.zeros_like(gain_part_ref)

    gain_part_ref[...] += jnp.sum(gated * nhat, axis=0, keepdims=True)
    f = gated * gain
    d_core = scale * (f - nhat * jnp.mean(f * nhat, axis=1, keepdims=True))
    d_gate_ref[...] = (d_branch * nhat * gain * sig * (1.0 + gate * (1.0 - sig))).astype(bf16)
    d_core_b = d_core.astype(bf16)
    d_core_ref[...] = d_core_b
    for group in range(rows // GROUP):
        span = slice(group * GROUP, (group + 1) * GROUP)
        pulled = mm(chunk_masks_stack(reach_ref[span, :].astype(f32).T), d_core_b[span])
        for part in range(per_group):
            pulls[head, group * per_group + part] = pulled[part * DK : (part + 1) * DK]

    @pl.when(head == heads - 1)
    def _():
        eye = jnp.where(
            lax.broadcasted_iota(jnp.int32, (DK, DK), 0)
            == lax.broadcasted_iota(jnp.int32, (DK, DK), 1),
            1.0,
            0.0,
        )
        grads = [
            jnp.concatenate([jnp.zeros((DK, DV), f32), eye], axis=1)
            for _ in range(local_ref.shape[0])
        ]
        for at in reversed(range(stretches)):
            for h in range(len(grads)):
                grad_b = grads[h].astype(bf16)
                local_ref[h, at] = grad_b
                moved = mm(turn_ref[h, at], grad_b)
                grads[h] = jnp.concatenate([moved[:, :DV] + pulls[h, at], moved[:, DV:]], axis=1)
        for h in range(len(grads)):
            end_ref[h] = grads[h][:, :DV].astype(bf16)


def finish_backward(
    ends_ref,
    grad_ends_ref,
    mixed_ref,
    tail_ref,
    taps_ref,
    columns_ref,
    run_rows_ref,
    solve_ref,
    score_ref,
    fresh_ref,
    state_ref,
    d_core_ref,
    local_ref,
    d_mixed_ref,
    tail_out_ref,
    lead_ref,
    grad_taps_ref,
    padded,
    spread,
    end,
):
    head = pl.program_id(0)
    heads = pl.num_programs(0)
    rows = mixed_ref.shape[0]
    per_group = GROUP // STRETCH

    @pl.when(head == 0)
    def _():
        end[...] = jnp.zeros_like(end)
        count = ends_ref.shape[0]

        def one(turn, carry):
            source = count - 1 - turn
            for h in range(end.shape[0]):
                end[h] = (
                    mm_tn(ends_ref[source, h, :, DV:], end[h].astype(bf16))
                    + grad_ends_ref[source, h].astype(f32)
                )
            return carry

        lax.fori_loop(0, count - 1 - lax.axis_index("seq"), one, 0)

    end_b = end[head].astype(bf16)
    total = convolved(padded, tail_ref, mixed_ref, taps_ref)
    sig = jax.nn.sigmoid(total)
    activated = total * sig
    raw_q, raw_k = activated[:, :DK], activated[:, DK : 2 * DK]
    scale_q = lax.rsqrt(jnp.sum(raw_q * raw_q, axis=1, keepdims=True) + epsilon)
    scale_k = lax.rsqrt(jnp.sum(raw_k * raw_k, axis=1, keepdims=True) + epsilon)
    unit_q = raw_q * scale_q
    keys = raw_k * scale_k
    beta = column(columns_ref, BETA, head, heads)
    gamma = column(columns_ref, GAMMA, head, heads)
    beta_gamma = column(columns_ref, BETA_GAMMA, head, heads)
    tail_decay = column(columns_ref, TAIL, head, heads)
    run = column(columns_ref, RUN, head, heads)
    row_id, col_id = square_ids()
    causal = (row_id // STRETCH == col_id // STRETCH) & (row_id >= col_id)
    diagonal = row_id == col_id
    d_queries, d_keys, d_values = [], [], []
    for group in range(rows // GROUP):
        span = slice(group * GROUP, (group + 1) * GROUP)
        key_b = keys[span].astype(bf16)
        query_b = (unit_q[span] * DK ** (-0.5)).astype(bf16)
        tail_keys = (tail_decay[span] * keys[span]).astype(bf16)
        d_core_b = d_core_ref[span, :]
        grad_bs, from_grad, fresh_parts, from_state = [], [], [], []
        for part in range(per_group):
            at = group * per_group + part
            own = slice(part * STRETCH, (part + 1) * STRETCH)
            rows_at = slice(at * STRETCH, (at + 1) * STRETCH)
            grad_b = (
                local_ref[at, :, :DV].astype(f32) + mm(local_ref[at, :, DV:], end_b)
            ).astype(bf16)
            grad_bs.append(grad_b)
            from_grad.append(mm(tail_keys[own], grad_b))
            fresh_parts.append(mm(fresh_ref[rows_at, DV:], state_ref[at]))
            from_state.append(mm_nt(d_core_b[own], state_ref[at]))
        d_fresh = mm_tn(score_ref[group], d_core_b) + jnp.concatenate(from_grad, axis=0)
        d_right = mm_tn(solve_ref[group], d_fresh.astype(bf16))
        d_right_b = d_right.astype(bf16)
        fresh = fresh_ref[span, :DV].astype(f32) - jnp.concatenate(fresh_parts, axis=0)
        fresh_b = fresh.astype(bf16)
        gaps = run[span] - run_rows_ref[pl.ds(head, 1), span]
        within = jnp.exp(jnp.where(causal, gaps, -1e30))
        d_score = (within * mm_nt(d_core_b, fresh_b)).astype(bf16)
        d_lower = jnp.where(
            diagonal, 0.0, -beta[span] * within * mm_nt(d_right_b, fresh_b)
        ).astype(bf16)
        state_keys, grad_keys = [], []
        for part in range(per_group):
            at = group * per_group + part
            own = slice(part * STRETCH, (part + 1) * STRETCH)
            state_keys.append(mm_nt(d_right_b[own], state_ref[at]))
            grad_keys.append(mm_nt(fresh_b[own], grad_bs[part]))
        d_queries.append(gamma[span] * jnp.concatenate(from_state, axis=0) + mm(d_score, key_b))
        d_keys.append(
            mm_tn(d_score, query_b)
            + mm_tn(d_lower, key_b)
            + mm(d_lower, key_b)
            + tail_decay[span] * jnp.concatenate(grad_keys, axis=0)
            - beta_gamma[span] * jnp.concatenate(state_keys, axis=0)
        )
        d_values.append(beta[span] * d_right)
    g_q = jnp.concatenate(d_queries, axis=0) * DK ** (-0.5)
    g_k = jnp.concatenate(d_keys, axis=0)
    d_act = jnp.concatenate(
        [
            scale_q * (g_q - unit_q * jnp.sum(unit_q * g_q, axis=1, keepdims=True)),
            scale_k * (g_k - keys * jnp.sum(keys * g_k, axis=1, keepdims=True)),
            jnp.concatenate(d_values, axis=0),
        ],
        axis=1,
    )
    d_conv = d_act * (sig * (1.0 + total * (1.0 - sig)))
    taps = taps_ref[...].astype(f32)
    count = taps_ref.shape[0]
    start = 9 - count
    grad_taps_ref[...] = jnp.concatenate(
        [
            jnp.sum(padded[start + tap : start + tap + rows, :] * d_conv, axis=0, keepdims=True)
            for tap in range(count)
        ],
        axis=0,
    )
    spread[0:8, :] = jnp.zeros((8, d_conv.shape[1]), f32)
    spread[8 : 8 + rows, :] = d_conv
    spread[8 + rows : 16 + rows, :] = jnp.zeros((8, d_conv.shape[1]), f32)
    lead = taps[0:1] * spread[8:16, :]
    d_mixed = taps[0:1] * spread[7 + count : 7 + count + rows, :]
    for tap in range(1, count):
        lead += taps[tap : tap + 1] * spread[8 - tap : 16 - tap, :]
        begin = 7 + count - tap
        d_mixed += taps[tap : tap + 1] * spread[begin : begin + rows, :]
    lead_ref[...] = lead
    d_mixed_ref[...] = d_mixed.astype(bf16)
    tail_out_ref[...] = d_mixed[rows - 8 :]


def whole(shape):
    return pl.BlockSpec(shape, lambda h: (0,) * len(shape))


def by_head(shape):
    return pl.BlockSpec((None,) + shape, lambda h: (h,) + (0,) * len(shape))


def by_columns(rows, width):
    return pl.BlockSpec((rows, width), lambda h: (0, h))


def kernel_call(body, heads, ins, outs, out_shapes, scratch, flops, moved):
    return pl.pallas_call(
        body,
        grid=(heads,),
        in_specs=ins,
        out_specs=outs,
        out_shape=out_shapes,
        scratch_shapes=scratch,
        compiler_params=pltpu.CompilerParams(
            dimension_semantics=("arbitrary",), vmem_limit_bytes=VMEM_BYTES
        ),
        cost_estimate=pl.CostEstimate(flops=flops, bytes_accessed=moved, transcendentals=0),
    )


def shaped(shape, kind):
    return jax.ShapeDtypeStruct(shape, kind)


def run_local_forward(mixed, tail, taps, columns, run_rows, heads):
    rows = mixed.shape[0]
    count = taps.shape[0]
    groups, stretches = rows // GROUP, rows // STRETCH
    return kernel_call(
        local_forward,
        heads,
        [
            by_columns(rows, INNER),
            by_columns(8, INNER),
            by_columns(count, INNER),
            whole(columns.shape),
            whole(run_rows.shape),
        ],
        [
            by_head((groups, GROUP, GROUP)),
            by_head((groups, GROUP, GROUP)),
            by_head((rows, DV + DK)),
            by_head((rows, DK)),
            by_columns(rows, DV),
            by_head((stretches, DK, DK)),
            whole((heads, stretches, DK, DV + DK)),
            whole((heads, DK, DV + DK)),
        ],
        [
            shaped((heads, groups, GROUP, GROUP), bf16),
            shaped((heads, groups, GROUP, GROUP), bf16),
            shaped((heads, rows, DV + DK), bf16),
            shaped((heads, rows, DK), bf16),
            shaped((rows, heads * DV), f32),
            shaped((heads, stretches, DK, DK), bf16),
            shaped((heads, stretches, DK, DV + DK), bf16),
            shaped((heads, DK, DV + DK), bf16),
        ],
        [
            pltpu.VMEM((rows + 8, INNER), f32),
            pltpu.VMEM((heads, stretches, DK, DK), bf16),
            pltpu.VMEM((heads, stretches, DK, DV), f32),
        ],
        12_000_000_000,
        20_000_000,
    )(mixed, tail, taps, columns, run_rows)


def run_finish_forward(ends, local, reach, inner, gate_pre, gain):
    heads, stretches = local.shape[:2]
    rows = inner.shape[0]
    return kernel_call(
        finish_forward,
        heads,
        [
            whole(ends.shape),
            by_head((stretches, DK, DV + DK)),
            by_head((rows, DK)),
            by_columns(rows, DV),
            by_columns(rows, DV),
            whole(gain.shape),
        ],
        [by_head((stretches, DK, DV)), by_columns(rows, DV), by_columns(rows, DV)],
        [
            shaped((heads, stretches, DK, DV), bf16),
            shaped((rows, heads * DV), f32),
            shaped((rows, heads * DV), bf16),
        ],
        [pltpu.VMEM((heads, DK, DV), f32)],
        3_000_000_000,
        20_000_000,
    )(ends, local, reach, inner, gate_pre, gain)


def run_local_backward(d_branch, core, gate_pre, gain, reach, turn):
    heads, stretches = turn.shape[:2]
    rows = core.shape[0]
    return kernel_call(
        local_backward,
        heads,
        [
            by_columns(rows, DV),
            by_columns(rows, DV),
            by_columns(rows, DV),
            whole(gain.shape),
            by_head((rows, DK)),
            whole(turn.shape),
        ],
        [
            by_columns(rows, DV),
            by_columns(rows, DV),
            whole((1, DV)),
            whole((heads, stretches, DK, DV + DK)),
            whole((heads, DK, DV)),
        ],
        [
            shaped((rows, heads * DV), bf16),
            shaped((rows, heads * DV), bf16),
            shaped((1, DV), f32),
            shaped((heads, stretches, DK, DV + DK), bf16),
            shaped((heads, DK, DV), bf16),
        ],
        [pltpu.VMEM((heads, stretches, DK, DV), f32)],
        4_000_000_000,
        20_000_000,
    )(d_branch, core, gate_pre, gain, reach, turn)


def run_finish_backward(
    ends, grad_ends, mixed, tail, taps, columns, run_rows, solve, score, fresh, states, d_core, local
):
    heads, stretches = local.shape[:2]
    rows = mixed.shape[0]
    groups = rows // GROUP
    count = taps.shape[0]
    return kernel_call(
        finish_backward,
        heads,
        [
            whole(ends.shape),
            whole(grad_ends.shape),
            by_columns(rows, INNER),
            by_columns(8, INNER),
            by_columns(count, INNER),
            whole(columns.shape),
            whole(run_rows.shape),
            by_head((groups, GROUP, GROUP)),
            by_head((groups, GROUP, GROUP)),
            by_head((rows, DV + DK)),
            by_head((stretches, DK, DV)),
            by_columns(rows, DV),
            by_head((stretches, DK, DV + DK)),
        ],
        [
            by_columns(rows, INNER),
            by_columns(8, INNER),
            by_columns(8, INNER),
            by_columns(count, INNER),
        ],
        [
            shaped((rows, heads * INNER), bf16),
            shaped((8, heads * INNER), f32),
            shaped((8, heads * INNER), f32),
            shaped((count, heads * INNER), f32),
        ],
        [
            pltpu.VMEM((rows + 8, INNER), f32),
            pltpu.VMEM((rows + 16, INNER), f32),
            pltpu.VMEM((heads, DK, DV), f32),
        ],
        12_000_000_000,
        20_000_000,
    )(ends, grad_ends, mixed, tail, taps, columns, run_rows, solve, score, fresh, states, d_core, local)


def silu_slope(tensor):
    sigmoid_part = jax.nn.sigmoid(tensor)
    return sigmoid_part * (1.0 + tensor * (1.0 - sigmoid_part))


def gathered(value, axis):
    return lax.all_gather(value, axis, axis=0, tiled=True)


def scattered(value, axis, dimension=0):
    return lax.psum_scatter(
        value.astype(bf16), axis, scatter_dimension=dimension, tiled=True
    ).astype(f32)


def on_device(
    block_in,
    out_cot,
    gain_one,
    qkv_weight,
    conv_weight,
    gate_weight,
    gain_out,
    out_weight,
    gain_two,
    mlp_gate,
    mlp_up,
    mlp_down,
    decay_code,
    beta_code,
):
    span_rows = decay_code.shape[0]
    width, heads, inner = qkv_weight.shape
    total_len = span_rows * lax.axis_size("seq")
    lead_rows = conv_weight.shape[0] - 1
    input_f = block_in.astype(f32)
    gain_first = gain_one.astype(f32)
    gain_second = gain_two.astype(f32)
    gain_head = gain_out.reshape(1, -1)
    taps = conv_weight.reshape(conv_weight.shape[0], heads * inner)
    qkv_flat = qkv_weight.reshape(width, heads * inner)
    gate_flat = gate_weight.reshape(width, heads * DV)
    out_flat = out_weight.reshape(heads * DV, width)
    columns, run_rows = token_columns(decay_code, beta_code, total_len)

    wide_in = gathered(block_in, "head").astype(f32)
    hat_first = wide_in * rms_scale(wide_in)
    normed_first = (hat_first * gain_first).astype(bf16)
    mixed_in = mm(normed_first, qkv_flat).astype(bf16)
    tail_in = passed_along(mixed_in[span_rows - 8 :], "seq", 1)
    tail_in = jnp.where(jnp.arange(8)[:, None] >= 8 - lead_rows, tail_in.astype(f32), 0.0)
    solve, score, fresh, reach, inner_part, turn, local_states, piece_end = run_local_forward(
        mixed_in, tail_in, taps, columns, run_rows, heads
    )
    ends = lax.all_gather(piece_end, "seq")
    gate_pre = mm(normed_first, gate_flat)
    states, core, branch = run_finish_forward(
        ends, local_states, reach, inner_part, gate_pre, gain_head
    )
    middle = input_f + scattered(mm(branch, out_flat), "head")
    scale_two = rms_scale(middle)
    hat_two = middle * scale_two
    normed_two = (hat_two * gain_second).astype(bf16)

    rows_out = gathered(normed_two, "seq")
    gate_part = mm(rows_out, mlp_gate)
    up_part = mm(rows_out, mlp_up)
    hidden = (jax.nn.silu(gate_part) * up_part).astype(bf16)
    mlp_out = scattered(mm(hidden, mlp_down), "seq")
    output = (middle + mlp_out).astype(bf16)
    cot_f = out_cot.astype(f32)
    cot_all = gathered(out_cot, "seq")
    d_hidden = mm_nt(cot_all, mlp_down)
    d_gate_mlp = (d_hidden * up_part * silu_slope(gate_part)).astype(bf16)
    d_up_mlp = (d_hidden * jax.nn.silu(gate_part)).astype(bf16)
    d_normed_two = scattered(mm_nt(d_gate_mlp, mlp_gate) + mm_nt(d_up_mlp, mlp_up), "seq")
    grad_down = mm_tn(hidden, cot_all)
    grad_mgate = mm_tn(rows_out, d_gate_mlp)
    grad_mup = mm_tn(rows_out, d_up_mlp)
    gain_two_part = jnp.sum(d_normed_two * hat_two, 0)
    e_two = d_normed_two * gain_second
    d_middle = cot_f + scale_two * (
        e_two - hat_two * jnp.mean(e_two * hat_two, axis=-1, keepdims=True)
    )
    d_mix_all = gathered(d_middle.astype(bf16), "head")
    d_branch = mm_nt(d_mix_all, out_flat)
    d_core, d_gate_low, gain_out_part, local_grads, grad_end = run_local_backward(
        d_branch, core, gate_pre, gain_head, reach, turn
    )
    grad_ends = lax.all_gather(grad_end, "seq")
    grad_out_w = mm_tn(branch, d_mix_all)
    d_mixed, d_tail, d_lead, grad_conv = run_finish_backward(
        ends,
        grad_ends,
        mixed_in,
        tail_in,
        taps,
        columns,
        run_rows,
        solve,
        score,
        fresh,
        states,
        d_core,
        local_grads,
    )
    from_next = passed_along(d_lead[:lead_rows], "seq", -1)
    d_tail = d_tail.at[8 - lead_rows :].add(from_next).astype(bf16)
    d_mixed = lax.dynamic_update_slice(d_mixed, d_tail, (span_rows - 8, 0))
    d_normed_part = mm_nt(d_mixed, qkv_flat) + mm_nt(d_gate_low, gate_flat)
    d_normed_one = scattered(d_normed_part, "head")
    grad_qkv = mm_tn(normed_first, d_mixed)
    grad_gate = mm_tn(normed_first, d_gate_low)
    gain_one_part = jnp.sum(d_normed_part * hat_first, 0)

    grad_mgate_h = scattered(grad_mgate, "head")
    grad_mup_h = scattered(grad_mup, "head")
    grad_down_h = scattered(grad_down, "head", 1)
    gain_parts = [
        scattered(scattered(part, "head"), "seq")
        for part in (gain_one_part, gain_two_part, gain_out_part.reshape(-1))
    ]
    scale_own = rms_scale(input_f)
    hat_own = input_f * scale_own
    e_one = d_normed_one * gain_first
    d_input = (
        d_middle + scale_own * (e_one - hat_own * jnp.mean(e_one * hat_own, axis=-1, keepdims=True))
    ).astype(bf16)
    grad_qkv_s = scattered(grad_qkv, "seq").reshape(-1, heads, inner)
    grad_gate_s = scattered(grad_gate, "seq").reshape(-1, heads, DV)
    grad_out_s = scattered(grad_out_w, "seq", 1).reshape(heads, DV, -1)
    grad_conv_s = scattered(grad_conv.reshape(-1, heads, inner), "seq", 2)
    return (
        output,
        d_input,
        gain_parts[0],
        grad_qkv_s,
        grad_conv_s,
        grad_gate_s,
        gain_parts[2],
        grad_out_s,
        gain_parts[1],
        grad_mgate_h,
        grad_mup_h,
        grad_down_h,
    )


def solution(mesh):
    in_specs = (
        P(("seq", "head"), None),
        P(("seq", "head"), None),
        P(),
        P(None, "head", None),
        P(None, "head", None),
        P(None, "head", None),
        P(),
        P("head", None, None),
        P(),
        P(None, "seq"),
        P(None, "seq"),
        P("seq", None),
        P("seq", "head"),
        P("seq", "head"),
    )
    out_specs = (
        P(("seq", "head"), None),
        P(("seq", "head"), None),
        P(("head", "seq")),
        P("seq", "head", None),
        P(None, "head", "seq"),
        P("seq", "head", None),
        P(("head", "seq")),
        P("head", None, "seq"),
        P(("head", "seq")),
        P("head", "seq"),
        P("head", "seq"),
        P("seq", "head"),
    )
    return jax.shard_map(
        on_device, mesh=mesh, in_specs=in_specs, out_specs=out_specs, check_vma=False
    )
```

time: 1560 us -> 1200 us (0.77)
  matrix products: 327 us -> 120 us
  other arithmetic: 232 us -> 35.1 us
  Pallas kernels: 0 us -> 68.9 us
  local copies, waits for them, and re-layouts: 97.1 us -> 46.3 us
  waiting for transfers between devices: 839 us -> 867 us
    dot_general x95 -> x18, matrix products: 319 us -> 120 us  [the longest x6 45.1 us: mm_tn(): lax.dot_general(left, right, (((0,), (0,)), ((), ())), preferred_element_...]
    another operation x5 -> x1, other arithmetic: 161 us -> 6.33 us  [token_columns(): run = jnp.cumsum(rates.reshape(rows // STRETCH, STRETCH, heads), axis=1)]
    pallas_call x0 -> x4, Pallas kernels: none -> 68.9 us  [the longest x1 27.7 us: run_finish_backward(): kernel_call(finish_backward, heads, [whole(ends.shape), whole(grad_ends.s...]
    unnamed x20 -> x18, waiting for transfers between devices: 1.48 us -> 34.7 us
    all_gather x8 -> x6, waiting for transfers between devices: 265 us -> 243 us  [the longest x4 164 us: gathered(): return lax.all_gather(value, axis, axis=0, tiled=True)]
    while x50 -> x0, local copies, waits for them, and re-layouts: 17.7 us -> none
    mul x6 -> x0, other arithmetic: 16.8 us -> none  [the longest x1 7.88 us: conv_features(): conv_f[tap_index] * padded[tap_index:tap_index + row_total]]
    reduce_scatter x10, waiting for transfers between devices: 572 us -> 588 us  [scattered(): lax.psum_scatter(value.astype(bf16), axis, scatter_dimension=dimension, t...]
  transfers between devices with their start and end apart: 21 -> 19, of which waited for: 14 -> 16; matrix products, arithmetic and copies ran while one was open for 21% -> 11% of each run, Pallas kernels for 0% -> 2%
where the time goes in v1:
time: 1200 us; the launch traced here: 1190 us
  waiting for transfers between devices  867 us (72%)
  matrix products  120 us (10%)
  Pallas kernels  68.9 us (6%)
  local copies, waits for them, and re-layouts  46.3 us (4%)
  other arithmetic  35.1 us (3%)
  blocking collectives  27.9 us (2%)
  between operations  17.5 us (1%)
    reduce_scatter x10, waiting for transfers between devices, scattered(): lax.psum_scatter(value.astype(bf16), axis, scatter_dimension=dimension, t...  588 us
    all_gather x4, waiting for transfers between devices, gathered(): return lax.all_gather(value, axis, axis=0, tiled=True)  164 us
    all_gather x1, waiting for transfers between devices, on_device(): ends = lax.all_gather(piece_end, 'seq')  52.3 us
    dot_general x6, matrix products, mm_tn(): lax.dot_general(left, right, (((0,), (0,)), ((), ())), preferred_element_...  45.1 us
    dot_general x6, matrix products, mm_nt(): lax.dot_general(left, right, (((1,), (1,)), ((), ())), preferred_element_...  39.9 us
    unnamed x87, local copies, waits for them, and re-layouts  39 us
    dot_general x6, matrix products, mm(): return jnp.dot(left, right, preferred_element_type=f32)  35.4 us
    unnamed x18, waiting for transfers between devices  34.7 us
  transfers between devices with their start and end apart: 19, of which 16 were waited for; matrix products, arithmetic and copies ran while one was open for 11% of the time, Pallas kernels for 2%

profile of v1, /device:TPU:0, one launch (start us, length us, event | category | flops | bytes accessed | tf_op | source)
XLA Modules:
  0.0 1189.4 jit_solution(3650406586728080548)
XLA Ops:
  9.0 6.3 fusion.28
  16.6 10.7 copy.39
  27.3 7.7 all-gather.9.cloned.1.call-done
  34.9 2.1 fusion.4
  37.0 8.6 convolution_convert_fusion.8.mixed_ref
  45.6 3.6 collective-permute-start
  50.6 22.3 %shard_map.229 = (bf16[4,2,256,256]{3,2,1,0:T(8,128)(2,1)S(1)}, bf16[4,2,256,256]{3,2,1,0:T(8,128)(2,1)S(1)}, bf16[4,512,384]{2,1,0:T(8,128)(2,1)S(1)}, bf16[4,5...) custom-call(bf16[512,2048]{1,0:T(8,128)(2,1)} %copy-done.26, ...), custom_call_target="tpu_custom_call" | custom-call | flops 12000000000 | bytes 20000000 | tf_op jit(solution)/shard_map/pallas_call | solution.py:479
  78.0 3.4 copy.41
  81.4 1.9 copy-done.20
  83.3 3.7 fusion.24.gate_ref
  87.0 52.3 %all-gather.17.cloned.1.call-done = bf16[32,128,384]{2,1,0:T(8,128)(2,1)} async-done(((bf16[4,128,384]{2,1,0:T(8,128)(2,1)}), bf16[32,128,384]{2,1,0:T(8,128)(2,1)}) %all-gather.17.cloned.1.call-update) | async-done | bytes 3145744 | tf_op jit(solution)/shard_map/all_gather | solution.py:680
  140.4 9.4 shard_map.230
  149.8 1.3 copy-done.1
  151.2 1.3 copy-done.2
  153.5 3.6 convolution_convert_fusion.7
  157.3 31.6 %reduce-scatter.14.cloned.1.call-done = bf16[128,2048]{1,0:T(8,128)(2,1)} async-done(((bf16[512,2048]{1,0:T(8,128)(2,1)}), bf16[128,2048]{1,0:T(8,128)(2,1)}) %reduce-scatter.14.cloned.1.call-update) | async-done | bytes 524304 | tf_op jit(solution)/shard_map/reduce_scatter | solution.py:636
  188.9 1.5 multiply_reduce_fusion
  190.4 2.2 multiply_convert_fusion.3
  193.6 72.5 %all-gather.11.cloned.1.call-done = bf16[1024,2048]{1,0:T(8,128)(2,1)} async-done(((bf16[128,2048]{1,0:T(8,128)(2,1)}), bf16[1024,2048]{1,0:T(8,128)(2,1)}) %all-gather.11.cloned.1.call-update) | async-done | bytes 4194320 | tf_op jit(solution)/shard_map/all_gather | solution.py:632
  266.2 8.0 fusion.30
  274.2 4.7 fusion.29
  278.9 61.1 %all-gather.13.cloned.1.call-done = bf16[1024,2048]{1,0:T(8,128)(2,1)} async-done(((bf16[128,2048]{1,0:T(8,128)(2,1)}), bf16[1024,2048]{1,0:T(8,128)(2,1)}) %all-gather.13.cloned.1.call-update) | async-done | bytes 4194320 | tf_op jit(solution)/shard_map/all_gather | solution.py:632
  340.1 8.4 multiply_convert_fusion
  348.5 3.5 fusion.31
  352.1 5.3 add_convert_fusion
  357.5 86.3 %reduce-scatter.18.cloned.1.call-done = bf16[128,2048]{1,0:T(8,128)(2,1)} async-done(((bf16[1024,2048]{1,0:T(8,128)(2,1)}), bf16[128,2048]{1,0:T(8,128)(2,1)}) %reduce-scatter.18.cloned.1.call-update) | async-done | bytes 524304 | tf_op jit(solution)/shard_map/reduce_scatter | solution.py:636
  443.7 1.9 fusion.18
  445.6 2.8 fusion.21
  448.5 22.5 %all-gather.15.cloned.1.call-done = bf16[512,2048]{1,0:T(8,128)(2,1)} async-done(((bf16[128,2048]{1,0:T(8,128)(2,1)}), bf16[512,2048]{1,0:T(8,128)(2,1)}) %all-gather.15.cloned.1.call-update) | async-done | bytes 2097168 | tf_op jit(solution)/shard_map/all_gather | solution.py:632
  470.9 5.3 fusion.32.d_branch_ref
  476.2 9.5 shard_map.231
  487.8 7.4 convolution_convert_fusion.6
  495.3 7.5 convolution_convert_fusion.4
  502.9 7.3 convolution_convert_fusion.5
  510.3 26.9 %all-gather.19.cloned.1.call-done = bf16[32,128,256]{2,1,0:T(8,128)(2,1)} async-done(((bf16[4,128,256]{2,1,0:T(8,128)(2,1)}), bf16[32,128,256]{2,1,0:T(8,128)(2,1)}) %all-gather.19.cloned.1.call-update) | async-done | bytes 2097168 | tf_op jit(solution)/shard_map/all_gather | solution.py:715
  538.4 1.4 copy-done.14
  539.8 1.2 copy-done.16
  541.0 1.2 copy-done.18
  542.3 27.7 %shard_map.232 = (bf16[512,2048]{1,0:T(8,128)(2,1)}, f32[8,2048]{1,0:T(8,128)S(1)}, f32[8,2048]{1,0:T(8,128)S(1)}, f32[4,2048]{1,0:T(4,128)S(1)}) custom-call(bf16[8,4,128,384]{3,2,1,0:T(8,128)(2,1)} %bitcast.73, bf16[8,4,128,256]{3,2,1,0:T(8,128)(2,1)} %bitcast.74, bf16[512,2048]{1,0:T(8,128)(2,1)} %copy-done.26, ...), custom_call_target="tpu_custom_call" | custom-call | flops 12000000000 | bytes 20000000 | tf_op jit(solution)/shard_map/pallas_call | solution.py:586
  569.9 1.3 collective-permute-start.1
  571.3 4.3 fusion.33
  576.7 2.0 reshape.157
  579.8 13.0 %fusion.3 = (bf16[2048]{0:T(1024)(128)(2,1)S(1)}, bf16[512,2048]{1,0:T(8,128)(2,1)}) fusion(bf16[512,2048]{1,0:T(8,128)(2,1)} %all-gather.9.cloned.1.call-done, f32[512]{0:T(512)S(1)} %add_rsqrt_fusion, f32[512,2048]{1,0:T(8,128)} %fusion.33, bf16[512,2048]{1,0:T(8,128)(2,1)} %convert_dynamic-update-slice_fusion, bf16[2048,2048]{1,0:T(8,128)(2,1)} %bitcast.60), kind=kOutput, calls=%fused_computation.7 | convolution fusion | flops 4301256704 | bytes 18880512 | tf_op jit(solution)/shard_map/dot_general | solution.py:61
  592.8 6.7 convolution_convert_fusion.3
  599.6 6.2 convolution_convert_fusion.1
  605.9 6.3 convolution_convert_fusion.2
  612.4 10.3 convolution_convert_fusion
  627.2 2.5 convert_element_type.192
  629.6 2.4 convert_element_type.190
  632.0 20.4 %reduce-scatter.28.cloned.1.call-done = bf16[512,704]{0,1:T(8,128)(2,1)} async-done(((bf16[2048,704]{0,1:T(8,128)(2,1)}), bf16[512,704]{0,1:T(8,128)(2,1)}) %reduce-scatter.28.cloned.1.call-update) | async-done | bytes 720912 | tf_op jit(solution)/shard_map/reduce_scatter | solution.py:636
  652.4 2.4 convert_element_type.188
  654.8 6.0 all-reduce.9
  661.1 22.0 %all-reduce.8 = (bf16[512]{0:T(512)(128)(2,1)S(1)}, bf16[64]{0:T(256)(128)(2,1)S(1)}, bf16[512]{0:T(512)(128)(2,1)S(1)}) all-reduce(bf16[512]{0:T(512)(128)(2,1)S(1)} %dynamic-slice.9, bf16[64]{0:T(256)(128)(2,1)S(1)} %dynamic-slice.13, bf16[512]{0:T(512)(128)(2,1)S(1)} %dynamic-slice.17), channel_id=9, replica_groups=mesh['head'=4,'seq'=8] {'seq'}, use_global_device_ids=true, to_apply=%region_12.13.clone | all-reduce | flops 1088 | bytes 4352
  684.2 33.2 %reduce-scatter.34.cloned.1.call-done = bf16[64,16]{1,0:T(8,128)(2,1)} async-done(((bf16[512,16]{1,0:T(8,128)(2,1)}), bf16[64,16]{1,0:T(8,128)(2,1)}) %reduce-scatter.34.cloned.1.call-update) | async-done | bytes 2064
  719.0 32.2 %reduce-scatter.20.cloned.1.call-done = bf16[128,2048]{1,0:T(8,128)(2,1)} async-done(((bf16[512,2048]{1,0:T(8,128)(2,1)}), bf16[128,2048]{1,0:T(8,128)(2,1)}) %reduce-scatter.20.cloned.1.call-update) | async-done | bytes 524304 | tf_op jit(solution)/shard_map/reduce_scatter | solution.py:636
  751.2 1.4 fusion.10
  752.6 90.0 %reduce-scatter.16.cloned.1.call-done = bf16[128,2048]{1,0:T(8,128)(2,1)} async-done(((bf16[1024,2048]{1,0:T(8,128)(2,1)}), bf16[128,2048]{1,0:T(8,128)(2,1)}) %reduce-scatter.16.cloned.1.call-update) | async-done | bytes 524304 | tf_op jit(solution)/shard_map/reduce_scatter | solution.py:636
  842.6 3.5 fusion.14
  846.1 88.5 %reduce-scatter.26.cloned.1.call-done = bf16[1024,256]{1,0:T(8,128)(2,1)} async-done(((bf16[1024,2048]{1,0:T(8,128)(2,1)}), bf16[1024,256]{1,0:T(8,128)(2,1)}) %reduce-scatter.26.cloned.1.call-update) | async-done | bytes 524304 | tf_op jit(solution)/shard_map/reduce_scatter | solution.py:636
  934.6 2.1 convert.3
  936.7 89.2 %reduce-scatter.24.cloned.1.call-done = bf16[256,1024]{1,0:T(8,128)(2,1)} async-done(((bf16[2048,1024]{1,0:T(8,128)(2,1)}), bf16[256,1024]{1,0:T(8,128)(2,1)}) %reduce-scatter.24.cloned.1.call-update) | async-done | bytes 524304 | tf_op jit(solution)/shard_map/reduce_scatter | solution.py:636
  1025.9 2.5 reshape.152
  1028.4 150.2 %reduce-scatter.22.cloned.1.call-done = bf16[256,2048]{1,0:T(8,128)(2,1)} async-done(((bf16[2048,2048]{1,0:T(8,128)(2,1)}), bf16[256,2048]{1,0:T(8,128)(2,1)}) %reduce-scatter.22.cloned.1.call-update) | async-done | bytes 1048592 | tf_op jit(solution)/shard_map/reduce_scatter | solution.py:636
  1178.6 3.7 reshape.150
  (150 shorter events, 23.3 us)
Async XLA Ops:
  7.2 332.9 %copy-start = (bf16[704,2048]{1,0:T(8,128)(2,1)S(1)}, bf16[704,2048]{1,0:T(8,128)(2,1)}, u32[]{:S(2)}) copy-start(bf16[704,2048]{1,0:T(8,128)(2,1)} %param.27) | copy-start | bytes 8650756
  7.2 27.7 %all-gather.9.cloned.1.call-start = ((), (), s32[]{:S(2)}) async-start(), calls=%async_computation.11 | async-start | bytes 2621440 | tf_op jit(solution)/shard_map/all_gather | solution.py:632
  7.9 131.4 %all-gather.17.cloned.1.call-start = ((), (), s32[]{:S(2)}) async-start(), calls=%async_computation.25 | async-start | bytes 3538944 | tf_op jit(solution)/shard_map/all_gather | solution.py:680
  16.6 10.7 copy-start.24
  37.0 12.2 %copy-start.23 = (bf16[4,4,512]{2,1,0:T(4,128)(2,1)S(1)}, bf16[4,4,512]{2,1,0:T(4,128)(2,1)}, u32[]{:S(2)}) copy-start(bf16[4,4,512]{2,1,0:T(4,128)(2,1)} %param.20) | copy-start | bytes 49156
  45.6 3.7 copy-start.26
  45.6 5.0 collective-permute-start
  50.6 27.3 %copy-start.32 = (bf16[256]{0:T(256)(128)(2,1)S(1)}, bf16[256]{0:T(256)(128)(2,1)}, u32[]{:S(2)}) copy-start(bf16[256]{0:T(256)(128)(2,1)} %param.22) | copy-start | bytes 1540
  73.0 0.8 copy-start.4
  73.8 1.0 copy-start.9
  74.7 1.2 copy-start.13
  75.9 1.0 copy-start.15
  76.9 1.0 copy-start.17
  77.9 111.0 %reduce-scatter.14.cloned.1.call-start = ((), (), s32[]{:S(2)}) async-start(), calls=%async_computation.12 | async-start | bytes 2621440 | tf_op jit(solution)/shard_map/reduce_scatter | solution.py:636
  78.0 5.3 copy-start.22
  81.4 1.9 copy-start.20
  139.4 1.0 copy-start.5
  140.4 13.1 %copy-start.27 = (bf16[4,256,2048]{2,1,0:T(8,128)(2,1)S(1)}, bf16[4,256,2048]{2,1,0:T(8,128)(2,1)}, u32[]{:S(2)}) copy-start(bf16[4,256,2048]{2,1,0:T(8,128)(2,1)} %param.23) | copy-start | bytes 12582916
  149.8 1.3 copy-start.1
  151.2 1.3 copy-start.2
  152.5 1.0 copy-start.3
  153.5 3.7 copy-start.25
  157.2 109.0 %all-gather.11.cloned.1.call-start = ((), (), s32[]{:S(2)}) async-start(), calls=%async_computation.13 | async-start | bytes 4718592 | tf_op jit(solution)/shard_map/all_gather | solution.py:632
  192.6 147.5 %all-gather.13.cloned.1.call-start = ((), (), s32[]{:S(2)}) async-start(), calls=%async_computation.15 | async-start | bytes 4718592 | tf_op jit(solution)/shard_map/all_gather | solution.py:632
  193.2 250.5 %reduce-scatter.18.cloned.1.call-start = ((), (), s32[]{:S(2)}) async-start(), calls=%async_computation.16 | async-start | bytes 4718592 | tf_op jit(solution)/shard_map/reduce_scatter | solution.py:636
  266.2 8.0 copy-start.28
  266.2 8.0 copy-start.29
  340.0 8.4 copy-start.30
  348.4 3.6 copy-start.35
  348.5 3.6 copy-start.36
  348.5 3.6 copy-start.31
  357.4 113.5 %all-gather.15.cloned.1.call-start = ((), (), s32[]{:S(2)}) async-start(), calls=%async_computation.17 | async-start | bytes 2621440 | tf_op jit(solution)/shard_map/all_gather | solution.py:632
  448.4 88.8 %all-gather.19.cloned.1.call-start = ((), (), s32[]{:S(2)}) async-start(), calls=%async_computation.26 | async-start | bytes 2359296 | tf_op jit(solution)/shard_map/all_gather | solution.py:715
  470.9 5.3 copy-start.6
  470.9 5.3 copy-start.10
  485.7 1.0 copy-start.7
  486.7 1.0 copy-start.11
  487.7 139.4 %reduce-scatter.32.cloned.1.call-start = ((), (), s32[]{:S(2)}) async-start(), calls=%async_computation.24 | async-start | bytes 3604480 | tf_op jit(solution)/shard_map/reduce_scatter | solution.py:636
  495.2 134.4 %reduce-scatter.30.cloned.1.call-start = ((), (), s32[]{:S(2)}) async-start(), calls=%async_computation.23 | async-start | bytes 3604480 | tf_op jit(solution)/shard_map/reduce_scatter | solution.py:636
  502.8 149.6 %reduce-scatter.28.cloned.1.call-start = ((), (), s32[]{:S(2)}) async-start(), calls=%async_computation.22 | async-start | bytes 3604480 | tf_op jit(solution)/shard_map/reduce_scatter | solution.py:636
  510.2 207.2 %reduce-scatter.34.cloned.1.call-start = ((), (), s32[]{:S(2)}) async-start(), calls=%async_computation.27 | async-start | bytes 147456
  537.2 1.2 copy-start.12
  538.4 1.4 copy-start.14
  539.8 1.2 copy-start.16
  541.0 1.2 copy-start.18
  542.3 29.0 %copy-start.8 = (bf16[512,1024]{1,0:T(8,128)(2,1)S(1)}, bf16[512,1024]{1,0:T(8,128)(2,1)}, u32[]{:S(2)}) copy-start(bf16[512,1024]{1,0:T(8,128)(2,1)} %copy-done.7) | copy-start | bytes 3145732
  542.3 29.0 %copy-start.21 = (bf16[256,8,4,256]{3,1,2,0:T(8,128)(2,1)S(1)}, bf16[256,8,4,256]{3,1,2,0:T(8,128)(2,1)}, u32[]{:S(2)}) copy-start(bf16[256,8,4,256]{3,1,2,0:T(8,128)(2,1)} %copy-done.20) | copy-start | bytes 12582916
  569.9 8.9 collective-permute-start.1
  578.8 172.4 %reduce-scatter.20.cloned.1.call-start = ((), (), s32[]{:S(2)}) async-start(), calls=%async_computation.18 | async-start | bytes 2621440 | tf_op jit(solution)/shard_map/reduce_scatter | solution.py:636
  592.8 249.8 %reduce-scatter.16.cloned.1.call-start = ((), (), s32[]{:S(2)}) async-start(), calls=%async_computation.14 | async-start | bytes 4718592 | tf_op jit(solution)/shard_map/reduce_scatter | solution.py:636
  599.6 335.0 %reduce-scatter.26.cloned.1.call-start = ((), (), s32[]{:S(2)}) async-start(), calls=%async_computation.21 | async-start | bytes 4718592 | tf_op jit(solution)/shard_map/reduce_scatter | solution.py:636
  605.9 420.0 %reduce-scatter.24.cloned.1.call-start = ((), (), s32[]{:S(2)}) async-start(), calls=%async_computation.20 | async-start | bytes 4718592 | tf_op jit(solution)/shard_map/reduce_scatter | solution.py:636
  612.3 566.3 %reduce-scatter.22.cloned.1.call-start = ((), (), s32[]{:S(2)}) async-start(), calls=%async_computation.19 | async-start | bytes 9437184 | tf_op jit(solution)/shard_map/reduce_scatter | solution.py:636
  622.6 0.7 copy-start.34
  622.6 2.6 copy-start.33
  627.1 124.1 %copy-start.19 = (bf16[128,2048]{1,0:T(8,128)(2,1)S(1)}, bf16[128,2048]{1,0:T(8,128)(2,1)}, u32[]{:S(2)}) copy-start(bf16[128,2048]{1,0:T(8,128)(2,1)} %param.16) | copy-start | bytes 1572868
Sparse Core Ops, SparseCore 0:
  9.6 25.2 all-gather.8
  78.0 61.2 all-gather.16
  157.3 31.5 reduce-scatter.13
  192.7 73.4 all-gather.10
  268.3 71.6 all-gather.12
  357.5 86.1 reduce-scatter.17
  448.5 22.3 all-gather.14
  487.9 49.2 all-gather.18
  539.7 34.8 reduce-scatter.31
  577.1 36.3 reduce-scatter.29
  616.1 36.2 reduce-scatter.27
  656.5 60.8 reduce-scatter.33
  720.7 30.4 reduce-scatter.19
  754.7 87.8 reduce-scatter.15
  846.5 88.0 reduce-scatter.25
  938.1 87.8 reduce-scatter.23
  1029.8 148.7 reduce-scatter.21

commit v2 on v1

--- a/solution.py
+++ b/solution.py
@@ -623,6 +623,545 @@
     )(ends, grad_ends, mixed, tail, taps, columns, run_rows, solve, score, fresh, states, d_core, local)
 
 
+MESH = pl.DeviceIdType.MESH
+SIDE = 2
+
+
+def remote(source, target, send, arrive, device):
+    return pltpu.make_async_remote_copy(
+        src_ref=source,
+        dst_ref=target,
+        send_sem=send,
+        recv_sem=arrive,
+        device_id=device,
+        device_id_type=MESH,
+    )
+
+
+def greet(partners):
+    barrier = pltpu.get_barrier_semaphore()
+    expected = 0
+    for device, there in partners:
+        if there is None:
+            pl.semaphore_signal(barrier, inc=1, device_id=device, device_id_type=MESH)
+            expected = expected + 1
+        else:
+
+            @pl.when(there)
+            def _(device=device):
+                pl.semaphore_signal(barrier, inc=1, device_id=device, device_id_type=MESH)
+
+            expected = expected + there.astype(jnp.int32)
+    pl.semaphore_wait(barrier, expected)
+
+
+def head_places():
+    head, seq = lax.axis_index("head"), lax.axis_index("seq")
+    core = lax.rem(head, 2)
+    sibling = head + 1 - 2 * core
+    across = lax.rem(head + 2, 4)
+    return head, seq, sibling, across
+
+
+def head_partners():
+    head, seq, sibling, across = head_places()
+    return [((sibling, seq), None), ((across, seq), None)]
+
+
+def seq_places():
+    head, seq = lax.axis_index("head"), lax.axis_index("seq")
+    return head, seq // SIDE, lax.rem(seq, SIDE)
+
+
+def seq_partners(count):
+    head, line, side = seq_places()
+    return [
+        ((head, line * SIDE + 1 - side), None),
+        ((head, (line + 1) * SIDE + side), line < count - 1),
+        ((head, (line - 1) * SIDE + side), line > 0),
+    ]
+
+
+def run_together(steps):
+    steps = list(steps)
+    while steps:
+        alive = []
+        for step in steps:
+            try:
+                next(step)
+                alive.append(step)
+            except StopIteration:
+                pass
+        steps = alive
+
+
+def gather_head(own_ref, out_ref, local, send, arrive, pieces):
+    head, seq, sibling, across = head_places()
+    far = lax.rem(sibling + 2, 4)
+    rows = own_ref.shape[0] // pieces
+    keep = pltpu.make_async_copy(own_ref, out_ref.at[head], local.at[0])
+    keep.start()
+
+    def part(ref, piece):
+        return ref.at[pl.ds(piece * rows, rows)]
+
+    outgoing = []
+    for piece in range(pieces):
+        outgoing.append(
+            remote(
+                part(own_ref, piece),
+                part(out_ref.at[head], piece),
+                send.at[0, piece],
+                arrive.at[0, piece],
+                (across, seq),
+            )
+        )
+    for piece in range(pieces):
+        outgoing.append(
+            remote(
+                part(own_ref, piece),
+                part(out_ref.at[head], piece),
+                send.at[1, piece],
+                arrive.at[1, piece],
+                (sibling, seq),
+            )
+        )
+    for copy in outgoing:
+        copy.start()
+    yield
+    forwards = []
+    for piece in range(pieces):
+        outgoing[piece].wait_recv()
+        forward = remote(
+            part(out_ref.at[across], piece),
+            part(out_ref.at[across], piece),
+            send.at[2, piece],
+            arrive.at[2, piece],
+            (sibling, seq),
+        )
+        forward.start()
+        forwards.append(forward)
+        yield
+    for copy in outgoing[pieces:] + forwards:
+        copy.wait_recv()
+    for copy in outgoing + forwards:
+        copy.wait_send()
+    keep.wait()
+
+
+def scatter_head(source_at, out_ref, own, crossed, passed, local, send, arrive):
+    head, seq, sibling, across = head_places()
+    far = lax.rem(sibling + 2, 4)
+    loads = [
+        pltpu.make_async_copy(source_at(target), own.at[slot], local.at[slot])
+        for slot, target in enumerate((across, head))
+    ]
+    copies = [
+        remote(source_at(target), crossed.at[slot], send.at[slot], arrive.at[slot], (sibling, seq))
+        for slot, target in enumerate((far, sibling))
+    ]
+    for slot in range(2):
+        copies[slot].start()
+        loads[slot].start()
+    yield
+    loads[0].wait()
+    copies[0].wait_recv()
+    own[0] = (own[0].astype(f32) + crossed[0].astype(f32)).astype(own.dtype)
+    onward = remote(own.at[0], passed, send.at[2], arrive.at[2], (across, seq))
+    onward.start()
+    yield
+    loads[1].wait()
+    copies[1].wait_recv()
+    out_ref[...] = own[1].astype(f32) + crossed[1].astype(f32)
+    yield
+    onward.wait_recv()
+    out_ref[...] += passed[...].astype(f32)
+    onward.wait_send()
+    for copy in copies:
+        copy.wait_send()
+
+
+def gather_seq(own_ref, out_ref, local, side_send, side_arrive, line_send, line_arrive, count):
+    head, line, side = seq_places()
+    me = line * SIDE + side
+    beside = (head, line * SIDE + 1 - side)
+    ways = ((1, line < count - 1), (-1, line > 0))
+    keep = pltpu.make_async_copy(own_ref, out_ref.at[me], local.at[0])
+    keep.start()
+
+    def along(source, block, way, step):
+        slot = step if way > 0 else count + step
+        return remote(
+            source,
+            out_ref.at[block],
+            line_send.at[slot],
+            line_arrive.at[slot],
+            (head, (line + way) * SIDE + side),
+        )
+
+    def over(source, block, slot):
+        return remote(source, out_ref.at[block], side_send.at[slot], side_arrive.at[slot], beside)
+
+    for way, onward in ways:
+
+        @pl.when(onward)
+        def _(way=way):
+            along(own_ref, me, way, 0).start()
+
+    over(own_ref, me, 0).start()
+    yield
+    for step in range(1, count):
+        for way, onward in ways:
+            block = me - way * step * SIDE
+            arrives = line >= step if way > 0 else line + step < count
+
+            @pl.when(arrives)
+            def _(way=way, onward=onward, block=block, step=step):
+                landed = out_ref.at[block]
+                slot = step if way > 0 else count + step
+                remote(
+                    landed, landed, line_send.at[slot - 1], line_arrive.at[slot - 1], beside
+                ).wait_recv()
+
+                @pl.when(onward)
+                def _():
+                    along(landed, block, way, step).start()
+
+                over(landed, block, slot).start()
+
+        yield
+    over(own_ref, me, 0).wait()
+    for way, onward in ways:
+
+        @pl.when(onward)
+        def _(way=way):
+            along(own_ref, me, way, 0).wait_send()
+
+    for step in range(1, count):
+        for way, onward in ways:
+            block = me - way * step * SIDE
+            arrives = line >= step if way > 0 else line + step < count
+
+            @pl.when(arrives)
+            def _(way=way, onward=onward, block=block, step=step):
+                landed = out_ref.at[block]
+                slot = step if way > 0 else count + step
+                over(landed, block, slot).wait()
+
+                @pl.when(onward)
+                def _():
+                    along(landed, block, way, step).wait_send()
+
+    keep.wait()
+
+
+def scatter_seq(source_at, out_at, own, crossed, risen, fallen, local, sends, arrivals, count):
+    head, line, side = seq_places()
+    beside = (head, line * SIDE + 1 - side)
+    pieces = own.shape[0]
+
+    def targets(distance):
+        if distance == 0:
+            return [(line, None, 0)]
+        return [
+            (line - distance, line >= distance, -1),
+            (line + distance, line + distance < count, 1),
+        ]
+
+    def load(piece, target):
+        return pltpu.make_async_copy(
+            source_at(target * SIDE + side, piece), own.at[piece, target], local.at[piece, target]
+        )
+
+    def cross(piece, target):
+        return remote(
+            source_at(target * SIDE + 1 - side, piece),
+            crossed.at[piece, target],
+            sends.at[0, piece, target],
+            arrivals.at[0, piece, target],
+            beside,
+        )
+
+    def onward(piece, target, way, arriving=False):
+        landing = risen if way > 0 else fallen
+        return remote(
+            own.at[piece, target],
+            landing.at[piece, target],
+            sends.at[1, piece, target],
+            arrivals.at[1 if way > 0 else 2, piece, target],
+            beside if arriving else (head, (line + way) * SIDE + side),
+        )
+
+    def guarded(there, body):
+        if there is None:
+            body()
+        else:
+            pl.when(there)(body)
+
+    for piece in range(pieces):
+        for distance in range(count - 1, -1, -1):
+            for target, there, _ in targets(distance):
+
+                def begin(piece=piece, target=target):
+                    cross(piece, target).start()
+                    load(piece, target).start()
+
+                guarded(there, begin)
+    yield
+    for piece in range(pieces):
+        for distance in range(count - 1, 0, -1):
+            for way in (-1, 1):
+                target = line + way * distance
+                there = line >= distance if way < 0 else line + distance < count
+                first = line == count - 1 if way < 0 else line == 0
+                landing = risen if way > 0 else fallen
+
+                @pl.when(there)
+                def _(piece=piece, target=target, way=way, first=first, landing=landing):
+                    load(piece, target).wait()
+                    cross(piece, target).wait_recv()
+                    total = own[piece, target].astype(f32) + crossed[piece, target].astype(f32)
+
+                    @pl.when(first)
+                    def _():
+                        own[piece, target] = total.astype(own.dtype)
+
+                    @pl.when(jnp.logical_not(first))
+                    def _():
+                        onward(piece, target, way, True).wait_recv()
+                        own[piece, target] = (
+                            total + landing[piece, target].astype(f32)
+                        ).astype(own.dtype)
+
+                    onward(piece, target, way).start()
+
+            yield
+        load(piece, line).wait()
+        cross(piece, line).wait_recv()
+        out = out_at(piece)
+        out[...] = own[piece, line].astype(f32) + crossed[piece, line].astype(f32)
+        yield
+        for way, arrives in ((-1, line < count - 1), (1, line > 0)):
+            landing = risen if way > 0 else fallen
+
+            @pl.when(arrives)
+            def _(way=way, landing=landing, piece=piece, out=out):
+                onward(piece, line, way, True).wait_recv()
+                out[...] += landing[piece, line].astype(f32)
+
+        yield
+    for piece in range(pieces):
+        for distance in range(count - 1, -1, -1):
+            for target, there, way in targets(distance):
+
+                def finish(piece=piece, target=target, way=way):
+                    cross(piece, target).wait_send()
+                    if way:
+                        onward(piece, target, way).wait_send()
+
+                guarded(there, finish)
+
+
+ANY = pl.BlockSpec(memory_space=pl.ANY)
+IN_VMEM = pl.BlockSpec(memory_space=pltpu.VMEM)
+DMA = pltpu.SemaphoreType.DMA
+
+
+def link_call(body, number, ins, outs, shapes, scratch, moved):
+    return pl.pallas_call(
+        body,
+        in_specs=ins,
+        out_specs=outs,
+        out_shape=shapes,
+        scratch_shapes=scratch,
+        compiler_params=pltpu.CompilerParams(
+            collective_id=number, has_side_effects=True, vmem_limit_bytes=VMEM_BYTES
+        ),
+        cost_estimate=pl.CostEstimate(flops=0, bytes_accessed=moved, transcendentals=0),
+    )
+
+
+def gathered_head(value, number, pieces=4):
+    count = lax.axis_size("head")
+    if count != 4:
+        return lax.all_gather(value, "head", axis=0, tiled=True)
+    rows, width = value.shape
+
+    def body(own_ref, out_ref, local, send, arrive):
+        greet(head_partners())
+        run_together([gather_head(own_ref, out_ref, local, send, arrive, pieces)])
+
+    out = link_call(
+        body,
+        number,
+        [ANY],
+        ANY,
+        shaped((count, rows, width), value.dtype),
+        [DMA((1,)), DMA((3, pieces)), DMA((3, pieces))],
+        60_000_000,
+    )(value)
+    return out.reshape(count * rows, width)
+
+
+def gathered_seq(value, number):
+    total = lax.axis_size("seq")
+    count = total // SIDE
+    rows, width = value.shape
+    if total % SIDE or count < 2:
+        return lax.all_gather(value, "seq")
+
+    def body(own_ref, out_ref, *sems):
+        greet(seq_partners(count))
+        run_together([gather_seq(own_ref, out_ref, *sems, count)])
+
+    return link_call(
+        body,
+        number,
+        [ANY],
+        ANY,
+        shaped((total, rows, width), value.dtype),
+        [DMA((1,))] + [DMA((2 * count,)) for _ in range(4)],
+        120_000_000,
+    )(value)
+
+
+def head_scratch(rows, width):
+    return [
+        pltpu.VMEM((2, rows, width), bf16),
+        pltpu.VMEM((2, rows, width), bf16),
+        pltpu.VMEM((rows, width), bf16),
+        DMA((2,)),
+        DMA((3,)),
+        DMA((3,)),
+    ]
+
+
+def seq_scratch(pieces, count, rows, width):
+    return [pltpu.VMEM((pieces, count, rows, width), bf16) for _ in range(4)] + [
+        DMA((pieces, count)),
+        DMA((2, pieces, count)),
+        DMA((3, pieces, count)),
+    ]
+
+
+def scattered_head(value, number, pieces=2):
+    count = lax.axis_size("head")
+    if count != 4:
+        return scattered(value, "head")
+    rows, width = value.shape[0] // count, value.shape[1] // pieces
+
+    def body(source, out, *rest):
+        greet(head_partners())
+        steps = []
+        for piece in range(pieces):
+            span = pl.ds(piece * width, width)
+
+            def source_at(target, span=span):
+                return source.at[pl.ds(pl.multiple_of(target * rows, rows), rows), span]
+
+            steps.append(
+                scatter_head(source_at, out.at[:, span], *rest[6 * piece : 6 * piece + 6])
+            )
+        run_together(steps)
+
+    return link_call(
+        body,
+        number,
+        [ANY],
+        IN_VMEM,
+        shaped((rows, value.shape[1]), f32),
+        head_scratch(rows, width) * pieces,
+        60_000_000,
+    )(value)
+
+
+def scattered_seq(value, number, pieces=2):
+    total = lax.axis_size("seq")
+    count = total // SIDE
+    if total % SIDE or count < 2:
+        return scattered(value, "seq")
+    rows, width = value.shape[0] // total, value.shape[1] // pieces
+
+    def body(source, out, *rest):
+        greet(seq_partners(count))
+
+        def source_at(target, piece):
+            return source.at[
+                pl.ds(pl.multiple_of(target * rows, rows), rows), pl.ds(piece * width, width)
+            ]
+
+        def out_at(piece):
+            return out.at[:, pl.ds(piece * width, width)]
+
+        run_together([scatter_seq(source_at, out_at, *rest, count)])
+
+    return link_call(
+        body,
+        number,
+        [ANY],
+        IN_VMEM,
+        shaped((rows, value.shape[1]), f32),
+        seq_scratch(pieces, count, rows, width),
+        120_000_000,
+    )(value)
+
+
+def scattered_last(qkv, normed, mlp, number, pieces=4):
+    total, heads = lax.axis_size("seq"), lax.axis_size("head")
+    count = total // SIDE
+    if total % SIDE or count < 2 or heads != 4:
+        return (
+            scattered(qkv, "seq"),
+            scattered(normed, "head"),
+            [scattered(part, "head", 1) for part in mlp],
+        )
+    rows, width = qkv.shape[0] // total, qkv.shape[1] // pieces
+    own_rows = normed.shape[0] // heads
+    units, slices = mlp[0].shape[0], mlp[0].shape[1] // heads
+
+    def body(qkv_ref, normed_ref, *rest):
+        mlp_refs, rest = rest[: len(mlp)], rest[len(mlp) :]
+        qkv_out, normed_out, rest = rest[0], rest[1], rest[2:]
+        mlp_outs, rest = rest[: len(mlp)], rest[len(mlp) :]
+        greet(head_partners() + seq_partners(count))
+
+        def qkv_at(target, piece):
+            return qkv_ref.at[
+                pl.ds(pl.multiple_of(target * rows, rows), rows), pl.ds(piece * width, width)
+            ]
+
+        def qkv_out_at(piece):
+            return qkv_out.at[:, pl.ds(piece * width, width)]
+
+        def normed_at(target):
+            return normed_ref.at[pl.ds(pl.multiple_of(target * own_rows, own_rows), own_rows)]
+
+        steps = [scatter_seq(qkv_at, qkv_out_at, *rest[:7], count)]
+        steps.append(scatter_head(normed_at, normed_out, *rest[7:13]))
+        for index, (ref, out) in enumerate(zip(mlp_refs, mlp_outs)):
+
+            def mlp_at(target, ref=ref):
+                return ref.at[:, pl.ds(pl.multiple_of(target * slices, slices), slices)]
+
+            begin = 13 + 6 * index
+            steps.append(scatter_head(mlp_at, out, *rest[begin : begin + 6]))
+        run_together(steps)
+
+    outs = link_call(
+        body,
+        number,
+        [ANY] * (2 + len(mlp)),
+        [IN_VMEM] * (2 + len(mlp)),
+        [shaped((rows, qkv.shape[1]), f32), shaped((own_rows, normed.shape[1]), f32)]
+        + [shaped((units, slices), f32) for _ in mlp],
+        seq_scratch(pieces, count, rows, width)
+        + head_scratch(own_rows, normed.shape[1])
+        + head_scratch(units, slices) * len(mlp),
+        250_000_000,
+    )(qkv, normed, *mlp)
+    return outs[0], outs[1], list(outs[2:])
+
+
 def silu_slope(tensor):
     sigmoid_part = jax.nn.sigmoid(tensor)
     return sigmoid_part * (1.0 + tensor * (1.0 - sigmoid_part))
@@ -668,52 +1207,55 @@
     out_flat = out_weight.reshape(heads * DV, width)
     columns, run_rows = token_columns(decay_code, beta_code, total_len)
 
-    wide_in = gathered(block_in, "head").astype(f32)
+    wide_in = gathered_head(block_in, 1).astype(f32)
     hat_first = wide_in * rms_scale(wide_in)
     normed_first = (hat_first * gain_first).astype(bf16)
     mixed_in = mm(normed_first, qkv_flat).astype(bf16)
     tail_in = passed_along(mixed_in[span_rows - 8 :], "seq", 1)
     tail_in = jnp.where(jnp.arange(8)[:, None] >= 8 - lead_rows, tail_in.astype(f32), 0.0)
+    cot_all = gathered(out_cot, "seq")
     solve, score, fresh, reach, inner_part, turn, local_states, piece_end = run_local_forward(
         mixed_in, tail_in, taps, columns, run_rows, heads
     )
-    ends = lax.all_gather(piece_end, "seq")
+    ends = gathered_seq(piece_end.reshape(-1, DV + DK), 2).reshape(-1, heads, DK, DV + DK)
     gate_pre = mm(normed_first, gate_flat)
     states, core, branch = run_finish_forward(
         ends, local_states, reach, inner_part, gate_pre, gain_head
     )
-    middle = input_f + scattered(mm(branch, out_flat), "head")
+    middle = input_f + scattered_head(mm(branch, out_flat).astype(bf16), 3)
     scale_two = rms_scale(middle)
     hat_two = middle * scale_two
     normed_two = (hat_two * gain_second).astype(bf16)
-
-    rows_out = gathered(normed_two, "seq")
+    normed_two, cot_all = lax.optimization_barrier((normed_two, cot_all))
+
+    rows_out = gathered_seq(normed_two, 4).reshape(-1, width)
     gate_part = mm(rows_out, mlp_gate)
     up_part = mm(rows_out, mlp_up)
     hidden = (jax.nn.silu(gate_part) * up_part).astype(bf16)
-    mlp_out = scattered(mm(hidden, mlp_down), "seq")
-    output = (middle + mlp_out).astype(bf16)
     cot_f = out_cot.astype(f32)
-    cot_all = gathered(out_cot, "seq")
     d_hidden = mm_nt(cot_all, mlp_down)
     d_gate_mlp = (d_hidden * up_part * silu_slope(gate_part)).astype(bf16)
     d_up_mlp = (d_hidden * jax.nn.silu(gate_part)).astype(bf16)
-    d_normed_two = scattered(mm_nt(d_gate_mlp, mlp_gate) + mm_nt(d_up_mlp, mlp_up), "seq")
-    grad_down = mm_tn(hidden, cot_all)
-    grad_mgate = mm_tn(rows_out, d_gate_mlp)
-    grad_mup = mm_tn(rows_out, d_up_mlp)
+    d_rows = (mm_nt(d_gate_mlp, mlp_gate) + mm_nt(d_up_mlp, mlp_up)).astype(bf16)
+    d_normed_two = scattered_seq(d_rows, 5)
+    hidden, d_normed_two = lax.optimization_barrier((hidden, d_normed_two))
+    mlp_out = scattered(mm(hidden, mlp_down), "seq")
+    output = (middle + mlp_out).astype(bf16)
     gain_two_part = jnp.sum(d_normed_two * hat_two, 0)
     e_two = d_normed_two * gain_second
     d_middle = cot_f + scale_two * (
         e_two - hat_two * jnp.mean(e_two * hat_two, axis=-1, keepdims=True)
     )
-    d_mix_all = gathered(d_middle.astype(bf16), "head")
+    d_mix_all = gathered_head(d_middle.astype(bf16), 6)
     d_branch = mm_nt(d_mix_all, out_flat)
     d_core, d_gate_low, gain_out_part, local_grads, grad_end = run_local_backward(
         d_branch, core, gate_pre, gain_head, reach, turn
     )
-    grad_ends = lax.all_gather(grad_end, "seq")
+    grad_ends = gathered_seq(grad_end.reshape(-1, DV), 7).reshape(-1, heads, DK, DV)
     grad_out_w = mm_tn(branch, d_mix_all)
+    grad_out_s = scattered(grad_out_w, "seq", 1).reshape(heads, DV, -1)
+    grad_gate = mm_tn(normed_first, d_gate_low)
+    grad_gate_s = scattered(grad_gate, "seq").reshape(-1, heads, DV)
     d_mixed, d_tail, d_lead, grad_conv = run_finish_backward(
         ends,
         grad_ends,
@@ -733,40 +1275,56 @@
     d_tail = d_tail.at[8 - lead_rows :].add(from_next).astype(bf16)
     d_mixed = lax.dynamic_update_slice(d_mixed, d_tail, (span_rows - 8, 0))
     d_normed_part = mm_nt(d_mixed, qkv_flat) + mm_nt(d_gate_low, gate_flat)
-    d_normed_one = scattered(d_normed_part, "head")
-    grad_qkv = mm_tn(normed_first, d_mixed)
-    grad_gate = mm_tn(normed_first, d_gate_low)
     gain_one_part = jnp.sum(d_normed_part * hat_first, 0)
-
-    grad_mgate_h = scattered(grad_mgate, "head")
-    grad_mup_h = scattered(grad_mup, "head")
-    grad_down_h = scattered(grad_down, "head", 1)
-    gain_parts = [
-        scattered(scattered(part, "head"), "seq")
-        for part in (gain_one_part, gain_two_part, gain_out_part.reshape(-1))
-    ]
+    grad_qkv = mm_tn(normed_first, d_mixed).astype(bf16)
+    grad_mgate = mm_tn(d_gate_mlp, rows_out).astype(bf16)
+    grad_mup = mm_tn(d_up_mlp, rows_out).astype(bf16)
+    grad_down = mm_tn(hidden, cot_all).astype(bf16)
+
+    small = jnp.concatenate(
+        [gain_one_part, gain_two_part, gain_out_part.reshape(-1), grad_conv.reshape(-1)]
+    ).astype(bf16)
+    small_all = lax.all_gather(small, ("seq", "head"))
+    grad_qkv_s, d_normed_one, (grad_mgate_t, grad_mup_t, grad_down_h) = scattered_last(
+        grad_qkv, d_normed_part.astype(bf16), [grad_mgate, grad_mup, grad_down], 8
+    )
     scale_own = rms_scale(input_f)
     hat_own = input_f * scale_own
     e_one = d_normed_one * gain_first
     d_input = (
         d_middle + scale_own * (e_one - hat_own * jnp.mean(e_one * hat_own, axis=-1, keepdims=True))
     ).astype(bf16)
-    grad_qkv_s = scattered(grad_qkv, "seq").reshape(-1, heads, inner)
-    grad_gate_s = scattered(grad_gate, "seq").reshape(-1, heads, DV)
-    grad_out_s = scattered(grad_out_w, "seq", 1).reshape(heads, DV, -1)
-    grad_conv_s = scattered(grad_conv.reshape(-1, heads, inner), "seq", 2)
+
+    seq_count, head_count = lax.axis_size("seq"), lax.axis_size("head")
+    seq_at, head_at = lax.axis_index("seq"), lax.axis_index("head")
+    gains = jnp.sum(small_all[:, : 2 * width + DV].astype(f32), axis=0)
+
+    def own_slice(vector):
+        length = vector.shape[0] // (seq_count * head_count)
+        return lax.dynamic_slice(vector, ((head_at * seq_count + seq_at) * length,), (length,))
+
+    gain_one_g = own_slice(gains[:width])
+    gain_two_g = own_slice(gains[width : 2 * width])
+    gain_out_g = own_slice(gains[2 * width :])
+    conv_all = lax.dynamic_index_in_dim(
+        small_all[:, 2 * width + DV :].reshape(seq_count, head_count, -1), head_at, 1, False
+    )
+    conv_sum = jnp.sum(conv_all.astype(f32), axis=0).reshape(-1, heads, inner)
+    grad_conv_s = lax.dynamic_slice_in_dim(
+        conv_sum, seq_at * (inner // seq_count), inner // seq_count, 2
+    )
     return (
         output,
         d_input,
-        gain_parts[0],
-        grad_qkv_s,
+        gain_one_g,
+        grad_qkv_s.reshape(-1, heads, inner),
         grad_conv_s,
         grad_gate_s,
-        gain_parts[2],
+        gain_out_g,
         grad_out_s,
-        gain_parts[1],
-        grad_mgate_h,
-        grad_mup_h,
+        gain_two_g,
+        grad_mgate_t.T,
+        grad_mup_t.T,
         grad_down_h,
     )
 

time: 1200 us -> 698 us (0.58)
  waiting for transfers between devices: 867 us -> 0.76 us
  Pallas kernels: 68.9 us -> 446 us
  matrix products: 120 us -> 96 us
  blocking collectives: 27.9 us -> 46.6 us
    reduce_scatter x10 -> x3, waiting for transfers between devices: 588 us -> 0.02 us  [scattered(): lax.psum_scatter(value.astype(bf16), axis, scatter_dimension=dimension, t...]
    pallas_call x0 -> x8, Pallas kernels: none -> 378 us  [the longest x3 140 us: gathered_seq(): link_call(body, number, [ANY], ANY, shaped((total, rows, width), value.dt...]
    all_gather x4 -> x1, waiting for transfers between devices: 164 us -> 0.01 us  [gathered(): return lax.all_gather(value, axis, axis=0, tiled=True)]
    all_gather x2 -> x0, waiting for transfers between devices: 79.2 us -> none  [the longest x1 52.3 us: on_device(): ends = lax.all_gather(piece_end, 'seq')]
    all_gather x0 -> x1, blocking collectives: none -> 46.6 us  [on_device(): small_all = lax.all_gather(small, ('seq', 'head'))]
    unnamed x18 -> x4, waiting for transfers between devices: 34.7 us -> 0.73 us
    unnamed x2 -> x0, blocking collectives: 27.9 us -> none
    dot_general x6, matrix products: 45.1 us -> 31.8 us  [mm_tn(): lax.dot_general(left, right, (((0,), (0,)), ((), ())), preferred_element_...]
  transfers between devices with their start and end apart: 19 -> 6, of which waited for: 16 -> 0; matrix products, arithmetic and copies ran while one was open for 11% -> 17% of each run, Pallas kernels for 2% -> 48%
where the time goes in v2:
time: 698 us; the launch traced here: 691 us
  Pallas kernels  446 us (64%)
  matrix products  96 us (14%)
  local copies, waits for them, and re-layouts  57.8 us (8%)
  blocking collectives  46.6 us (7%)
  other arithmetic  23.6 us (3%)
  between operations  15.1 us (2%)
    pallas_call x3, Pallas kernels, gathered_seq(): link_call(body, number, [ANY], ANY, shaped((total, rows, width), value.dt...  140 us
    pallas_call x1, Pallas kernels, scattered_last(): link_call(body, number, [ANY] * (2 + len(mlp)), [IN_VMEM] * (2 + len(mlp)...  140 us
    pallas_call x1, Pallas kernels, scattered_seq(): link_call(body, number, [ANY], IN_VMEM, shaped((rows, value.shape[1]), f3...  51.7 us
    all_gather x1, blocking collectives, on_device(): small_all = lax.all_gather(small, ('seq', 'head'))  46.6 us
    unnamed x137, local copies, waits for them, and re-layouts  42.9 us
    dot_general x6, matrix products, mm_nt(): lax.dot_general(left, right, (((1,), (1,)), ((), ())), preferred_element_...  36.3 us
    dot_general x6, matrix products, mm_tn(): lax.dot_general(left, right, (((0,), (0,)), ((), ())), preferred_element_...  31.8 us
    pallas_call x2, Pallas kernels, gathered_head(): link_call(body, number, [ANY], ANY, shaped((count, rows, width), value.dt...  31.2 us
  transfers between devices with their start and end apart: 6, of which 0 were waited for; matrix products, arithmetic and copies ran while one was open for 17% of the time, Pallas kernels for 48%

profile of v2, /device:TPU:0, one launch (start us, length us, event | category | flops | bytes accessed | tf_op | source)
XLA Modules:
  0.0 691.4 jit_solution(9635968707997114455)
XLA Ops:
  8.0 1.1 copy-done.6
  9.1 16.8 %shard_map.229 = bf16[4,128,2048]{2,1,0:T(8,128)(2,1)S(1)} custom-call(bf16[128,2048]{1,0:T(8,128)(2,1)S(1)} %copy-done.6), custom_call_target="tpu_custom_call" | custom-call | bytes 60000000 | tf_op jit(solution)/shard_map/pallas_call | solution.py:994
  26.0 11.1 %copy.43 = bf16[256,8,4,512]{3,1,2,0:T(8,128)(2,1)} copy(bf16[256,8,4,512]{3,2,1,0:T(4,128)(2,1)} %bitcast.95) | data formatting | bytes 16777216
  38.2 8.9 %convolution_convert_fusion.8.mixed_ref = bf16[512,2048]{1,0:T(8,128)(2,1)S(1)} fusion(bf16[512,2048]{1,0:T(8,128)(2,1)S(1)} %bitcast.103, bf16[2048,2048]{1,0:T(8,128)(2,1)} %bitcast.96), kind=kOutput, calls=%fused_computation.15 | convolution fusion | flops 4296015872 | bytes 12582912 | tf_op jit(solution)/shard_map/dot_general | solution.py:57
  47.8 4.2 collective-permute-start
  52.2 6.3 fusion.13
  59.0 3.4 copy.45
  62.5 3.7 fusion.14.gate_ref
  67.4 22.1 %shard_map.230 = (bf16[4,2,256,256]{3,2,1,0:T(8,128)(2,1)S(1)}, bf16[4,2,256,256]{3,2,1,0:T(8,128)(2,1)S(1)}, bf16[4,512,384]{2,1,0:T(8,128)(2,1)S(1)}, bf16[4,5...) custom-call(bf16[512,2048]{1,0:T(8,128)(2,1)} %copy-done.49, ...), custom_call_target="tpu_custom_call" | custom-call | flops 12000000000 | bytes 20000000 | tf_op jit(solution)/shard_map/pallas_call | solution.py:479
  89.5 1.1 copy-done.33
  92.6 39.4 %shard_map.231 = bf16[8,512,384]{2,1,0:T(8,128)(2,1)S(1)} custom-call(bf16[512,384]{1,0:T(8,128)(2,1)S(1)} %bitcast.91), custom_call_target="tpu_custom_call" | custom-call | bytes 120000000 | tf_op jit(solution)/shard_map/pallas_call | solution.py:1017
  132.0 1.6 copy-done.12
  133.6 9.4 %shard_map.232 = (bf16[4,8,128,256]{3,2,1,0:T(8,128)(2,1)S(1)}, f32[512,1024]{1,0:T(8,128)S(1)}, bf16[512,1024]{1,0:T(8,128)(2,1)S(1)}) custom-call(bf16[8,4,128,384]{3,2,1,0:T(8,128)(2,1)} %bitcast.84, bf16[4,8,128,384]{3,2,1,0:T(8,128)(2,1)} %get-tuple-element.54.local_ref, bf16[4,512,128]{2,1,0:T(8,128)(2,1)S(1)} %get-tuple-element.55.reach_ref, ...), custom_call_target="tpu_custom_call" | custom-call | flops 3000000000 | bytes 20000000 | tf_op jit(solution)/shard_map/pallas_call | solution.py:522
  143.1 1.4 copy-done.23
  144.4 1.3 copy-done.24
  145.8 2.3 convolution_convert_fusion.7.source
  148.1 15.5 %shard_map.233 = f32[128,2048]{1,0:T(8,128)S(1)} custom-call(bf16[512,2048]{1,0:T(8,128)(2,1)S(1)} %convolution_convert_fusion.7.source), custom_call_target="tpu_custom_call" | custom-call | bytes 60000000 | tf_op jit(solution)/shard_map/pallas_call | solution.py:1067
  163.7 1.2 multiply_reduce_fusion.4
  164.8 2.2 multiply_convert_fusion.5.own_ref
  167.0 1.0 copy-done.15
  168.1 50.8 %shard_map.234 = bf16[8,128,2048]{2,1,0:T(8,128)(2,1)S(1)} custom-call(bf16[128,2048]{1,0:T(8,128)(2,1)S(1)} %copy-done.15), custom_call_target="tpu_custom_call" | custom-call | bytes 120000000 | tf_op jit(solution)/shard_map/pallas_call | solution.py:1017
  218.9 3.2 fusion.15
  222.2 3.3 fusion.16
  225.5 5.3 multiply_convert_fusion.2
  230.9 3.5 fusion.17
  234.4 4.4 add_convert_fusion.source
  238.8 51.7 %shard_map.235 = f32[128,2048]{1,0:T(8,128)S(1)} custom-call(bf16[1024,2048]{1,0:T(8,128)(2,1)S(1)} %add_convert_fusion.source), custom_call_target="tpu_custom_call" | custom-call | bytes 120000000 | tf_op jit(solution)/shard_map/pallas_call | solution.py:1098
  290.5 2.0 multiply_reduce_fusion.2
  292.5 1.7 fusion.10.own_ref
  294.2 14.4 %shard_map.236 = bf16[4,128,2048]{2,1,0:T(8,128)(2,1)S(1)} custom-call(bf16[128,2048]{1,0:T(8,128)(2,1)S(1)} %fusion.10.own_ref), custom_call_target="tpu_custom_call" | custom-call | bytes 60000000 | tf_op jit(solution)/shard_map/pallas_call | solution.py:994
  308.6 1.3 copy-done.13
  309.9 4.4 convolution_convert_fusion.1
  314.3 6.4 convolution_convert_fusion.3
  320.8 1.5 copy-done.14
  322.3 4.6 fusion.18.d_branch_ref
  327.0 9.5 %shard_map.237 = (bf16[512,1024]{1,0:T(8,128)(2,1)S(1)}, bf16[512,1024]{1,0:T(8,128)(2,1)S(1)}, f32[1,256]{1,0:T(1,128)S(1)}, bf16[4,8,128,384]{3,2,1,0:T(8,128)(2,1)}, bf16[4,128,256]{2,1,0:T(8,128)(2,1)S(1)}) custom-call(f32[512,1024]{1,0:T(8,128)S(1)} %fusion.18.d_branch_ref, f32[512,1024]{1,0:T(8,128)} %copy-done.24, f32[512,1024]{1,0:T(8,128)} %fusion.14.gate_ref, ...), custom_call_target="tpu_custom_call" | custom-call | flops 4000000000 | bytes 20000000 | tf_op jit(solution)/shard_map/pallas_call | solution.py:548
  336.6 49.9 %shard_map.238 = bf16[8,512,256]{2,1,0:T(8,128)(2,1)S(1)} custom-call(bf16[512,256]{1,0:T(8,128)(2,1)S(1)} %bitcast.92), custom_call_target="tpu_custom_call" | custom-call | bytes 120000000 | tf_op jit(solution)/shard_map/pallas_call | solution.py:1017
  386.5 1.3 copy-done.16
  387.8 26.4 %shard_map.239 = (bf16[512,2048]{1,0:T(8,128)(2,1)}, f32[8,2048]{1,0:T(8,128)S(1)}, f32[8,2048]{1,0:T(8,128)S(1)}, f32[4,2048]{1,0:T(4,128)S(1)}) custom-call(bf16[8,4,128,384]{3,2,1,0:T(8,128)(2,1)} %bitcast.85, bf16[8,4,128,256]{3,2,1,0:T(8,128)(2,1)} %bitcast.88, bf16[512,2048]{1,0:T(8,128)(2,1)} %copy-done.49, ...), custom_call_target="tpu_custom_call" | custom-call | flops 12000000000 | bytes 20000000 | tf_op jit(solution)/shard_map/pallas_call | solution.py:586
  414.2 1.3 collective-permute-start.1
  415.5 6.7 fusion.19
  423.4 11.8 %multiply_reduce_fusion = (bf16[2048]{0:T(1024)(128)(2,1)S(1)}, bf16[512,2048]{1,0:T(8,128)(2,1)}, bf16[512,2048]{1,0:T(8,128)(2,1)S(1)}) fusion(bf16[4,128,2048]{2,1,0:T(8,128)(2,1)S(1)} %copy-done.3, f32[512]{0:T(512)S(1)} %get-tuple-element.102, f32[2048]{0:T(1024)S(1)} %convert_element_type.124, f32[512,2048]{1,0:T(8,128)} %fusion.19, ...), kind=kOutput, calls=%fused_computation.3 | convolution fusion | flops 4303353856 | bytes 20985856 | tf_op jit(solution)/shard_map/dot_general | solution.py:61
  435.2 1.3 copy-done.57
  436.5 4.4 convolution_convert_fusion.2
  441.0 1.3 copy-done.60
  442.3 6.9 convolution_convert_fusion.6.rest_0_
  449.2 4.5 convolution_convert_fusion.5.rest_1_
  453.7 4.5 convolution_convert_fusion.4.rest_2_
  458.3 46.6 %all-gather = bf16[32,1,12544]{2,1,0:T(2,128)(2,1)S(1)} all-gather(bf16[1,1,12544]{2,1,0:T(2,128)(2,1)S(1)} %maximum_bitcast_fusion), channel_id=1, replica_groups=mesh['head'=4,'seq'=8] {'seq','head'}, dimensions={0}, use_global_device_ids=true | all-gather | bytes 827904 | tf_op jit(solution)/shard_map/all_gather | solution.py:1287
  506.0 7.1 %convolution_convert_fusion.qkv_ref = bf16[2048,2048]{1,0:T(8,128)(2,1)} fusion(bf16[512,2048]{1,0:T(8,128)(2,1)S(1)} %copy-done.58, bf16[512,2048]{1,0:T(8,128)(2,1)S(1)} %copy-done.55), kind=kOutput, calls=%fused_computation.1 | convolution fusion | flops 4299161600 | bytes 12582912 | tf_op jit(solution)/shard_map/dot_general | solution.py:65
  513.1 140.0 %shard_map.240 = (f32[256,2048]{1,0:T(8,128)}, f32[128,2048]{1,0:T(8,128)S(1)}, f32[704,512]{1,0:T(8,128)S(1)}, f32[704,512]{1,0:T(8,128)S(1)}, f32[704,512]{1,0:T(8,128)S(1)}) custom-call(bf16[2048,2048]{1,0:T(8,128)(2,1)} %convolution_convert_fusion.qkv_ref, bf16[512,2048]{1,0:T(8,128)(2,1)} %get-tuple-element.90.normed_ref, ...), custom_call_target="tpu_custom_call" | custom-call | bytes 250000000 | tf_op jit(solution)/shard_map/pallas_call | solution.py:1150
  654.0 1.1 copy-done.17
  655.1 1.1 copy-done.19
  656.3 1.1 copy-done.20
  657.4 3.9 reshape.259
  661.3 2.0 slice.56
  663.3 2.0 reshape.260
  665.3 1.4 convert_reduce_fusion.1
  670.6 2.1 convert.22
  672.7 2.8 fusion.7
  675.5 2.5 reshape.268
  678.0 2.7 copy.54
  680.7 2.6 copy.55
  683.3 1.1 copy.56
  (175 shorter events, 13.8 us)
Async XLA Ops:
  7.2 218.3 %copy-start = (bf16[704,2048]{1,0:T(8,128)(2,1)S(1)}, bf16[704,2048]{1,0:T(8,128)(2,1)}, u32[]{:S(2)}) copy-start(bf16[704,2048]{1,0:T(8,128)(2,1)} %param.27) | copy-start | bytes 8650756
  7.2 18.7 %copy-start.47 = (bf16[2048]{0:T(1024)(128)(2,1)S(1)}, bf16[2048]{0:T(1024)(128)(2,1)}, u32[]{:S(2)}) copy-start(bf16[2048]{0:T(1024)(128)(2,1)} %param.18) | copy-start | bytes 12292
  7.2 159.8 %all-gather.3.cloned.1.call-start = ((), (), s32[]{:S(2)}) async-start(), calls=%async_computation.3 | async-start | bytes 4718592 | tf_op jit(solution)/shard_map/all_gather | solution.py:1171
  7.9 662.6 %reduce-scatter.8.cloned.1.call-start = ((), (), s32[]{:S(2)}) async-start(), calls=%async_computation.6 | async-start | bytes 4718592 | tf_op jit(solution)/shard_map/reduce_scatter | solution.py:1175
  8.0 1.1 copy-start.6
  25.9 11.6 %copy-start.2 = (bf16[4,128,2048]{2,1,0:T(8,128)(2,1)}, bf16[4,128,2048]{2,1,0:T(8,128)(2,1)S(1)}, u32[]{:S(2)}) copy-start(bf16[4,128,2048]{2,1,0:T(8,128)(2,1)S(1)} %shard_map.229) | copy-start | bytes 6291460
  38.1 8.9 %copy-start.42 = (bf16[4,128,2048]{2,1,0:T(8,128)(2,1)}, bf16[4,128,2048]{2,1,0:T(8,128)(2,1)S(1)}, u32[]{:S(2)}) copy-start(bf16[4,128,2048]{2,1,0:T(8,128)(2,1)S(1)} %multiply_convert_fusion.1) | copy-start | bytes 6291460
  38.1 13.8 %copy-start.45 = (s32[512,4]{0,1:T(4,128)S(1)}, s32[512,4]{0,1:T(4,128)}, u32[]{:S(2)}) copy-start(s32[512,4]{0,1:T(4,128)} %param.28) | copy-start | bytes 24580
  47.1 4.8 copy-start.49
  47.8 18.8 %collective-permute-start = (bf16[8,2048]{1,0:T(8,128)(2,1)}, bf16[8,2048]{1,0:T(8,128)(2,1)}, u32[]{:S(2)}, u32[]{:S(2)}) collective-permute-start(bf16[8,2048]{1,0:T(8,128)(2,1)} %slice.52), channel_id=1, source_target_pairs={{0,1},{1,2},{2,3},{3,4},{4,5},{5,6},{6,7},{8,9},{9,10},{10,11},{11... | collective-permute-start | bytes 98312 | tf_op jit(solution)/shard_map/ppermute | solution.py:27
  59.0 3.4 copy-start.46
  59.0 3.4 copy-start.43
  62.4 3.8 copy-start.41
  62.5 3.7 copy-start.44
  62.5 4.0 copy-start.56
  62.5 4.0 copy-start.48
  66.5 23.1 %copy-start.21 = (f32[512,128]{1,0:T(8,128)}, f32[512,128]{1,0:T(8,128)S(1)}, u32[]{:S(2)}) copy-start(f32[512,128]{1,0:T(8,128)S(1)} %pad.10.clone.columns_ref) | copy-start | bytes 786436
  89.5 1.1 copy-start.33
  92.6 41.0 %copy-start.31 = (bf16[4,8,128,128]{3,2,1,0:T(8,128)(2,1)}, bf16[4,8,128,128]{3,2,1,0:T(8,128)(2,1)S(1)}, u32[]{:S(2)}) copy-start(bf16[4,8,128,128]{3,2,1,0:T(8,128)(2,1)S(1)} %get-tuple-element.63.turn_ref) | copy-start | bytes 3145732
  92.6 50.4 %copy-start.27 = (bf16[4,512,128]{2,1,0:T(8,128)(2,1)}, bf16[4,512,128]{2,1,0:T(8,128)(2,1)S(1)}, u32[]{:S(2)}) copy-start(bf16[4,512,128]{2,1,0:T(8,128)(2,1)S(1)} %get-tuple-element.55.reach_ref) | copy-start | bytes 1572868
  132.0 1.6 copy-start.12
  133.6 12.1 %copy-start.50 = (bf16[4,256,2048]{2,1,0:T(8,128)(2,1)S(1)}, bf16[4,256,2048]{2,1,0:T(8,128)(2,1)}, u32[]{:S(2)}) copy-start(bf16[4,256,2048]{2,1,0:T(8,128)(2,1)} %param.23) | copy-start | bytes 12582916
  143.0 1.4 copy-start.23
  144.4 1.3 copy-start.24
  145.7 2.3 copy-start.25
  148.1 15.6 %copy-start.7 = (bf16[128,2048]{1,0:T(8,128)(2,1)S(1)}, bf16[128,2048]{1,0:T(8,128)(2,1)}, u32[]{:S(2)}) copy-start(bf16[128,2048]{1,0:T(8,128)(2,1)} %own_ref.1) | copy-start | bytes 1572868
  168.1 50.8 %copy-start.53 = (bf16[2048,704]{0,1:T(8,128)(2,1)S(1)}, bf16[2048,704]{0,1:T(8,128)(2,1)}, u32[]{:S(2)}) copy-start(bf16[2048,704]{0,1:T(8,128)(2,1)} %param.25) | copy-start | bytes 8650756
  218.9 3.2 copy-start.8
  218.9 3.3 copy-start.54
  222.2 3.3 copy-start.51
  230.8 3.5 copy-start.59
  230.8 3.5 copy-start.61
  238.8 53.7 %copy-start.39 = (bf16[128,2048]{1,0:T(8,128)(2,1)S(1)}, bf16[128,2048]{1,0:T(8,128)(2,1)}, u32[]{:S(2)}) copy-start(bf16[128,2048]{1,0:T(8,128)(2,1)} %param.17) | copy-start | bytes 1572868
  290.5 18.1 %copy-start.4 = (f32[128,2048]{1,0:T(8,128)}, f32[128,2048]{1,0:T(8,128)S(1)}, u32[]{:S(2)}) copy-start(f32[128,2048]{1,0:T(8,128)S(1)} %shard_map.235) | copy-start | bytes 3145732
  292.5 17.4 %copy-start.26 = (bf16[512,1024]{1,0:T(8,128)(2,1)S(1)}, bf16[512,1024]{1,0:T(8,128)(2,1)}, u32[]{:S(2)}) copy-start(bf16[512,1024]{1,0:T(8,128)(2,1)} %copy-done.25) | copy-start | bytes 3145732
  308.6 1.3 copy-start.13
  314.3 358.4 %reduce-scatter.4.cloned.1.call-start = ((), (), s32[]{:S(2)}) async-start(), calls=%async_computation.4 | async-start | bytes 4718592 | tf_op jit(solution)/shard_map/reduce_scatter | solution.py:1175
  320.7 1.6 copy-start.14
  320.8 6.2 copy-start.28
  320.8 354.7 %reduce-scatter.6.cloned.1.call-start = ((), (), s32[]{:S(2)}) async-start(), calls=%async_computation.5 | async-start | bytes 4718592 | tf_op jit(solution)/shard_map/reduce_scatter | solution.py:1175
  322.3 4.7 copy-start.32
  327.0 60.8 %copy-start.22 = (f32[512,128]{1,0:T(8,128)S(1)}, f32[512,128]{1,0:T(8,128)}, u32[]{:S(2)}) copy-start(f32[512,128]{1,0:T(8,128)} %copy-done.21) | copy-start | bytes 786436
  327.0 60.8 %copy-start.34 = (bf16[4,512,384]{2,1,0:T(8,128)(2,1)S(1)}, bf16[4,512,384]{2,1,0:T(8,128)(2,1)}, u32[]{:S(2)}) copy-start(bf16[4,512,384]{2,1,0:T(8,128)(2,1)} %copy-done.33) | copy-start | bytes 4718596
  327.0 60.8 %copy-start.36 = (bf16[4,2,256,256]{3,2,1,0:T(8,128)(2,1)S(1)}, bf16[4,2,256,256]{3,2,1,0:T(8,128)(2,1)}, u32[]{:S(2)}) copy-start(bf16[4,2,256,256]{3,2,1,0:T(8,128)(2,1)} %copy-done.35) | copy-start | bytes 3145732
  327.0 60.7 %copy-start.38 = (bf16[4,2,256,256]{3,2,1,0:T(8,128)(2,1)S(1)}, bf16[4,2,256,256]{3,2,1,0:T(8,128)(2,1)}, u32[]{:S(2)}) copy-start(bf16[4,2,256,256]{3,2,1,0:T(8,128)(2,1)} %copy-done.37) | copy-start | bytes 3145732
  336.6 78.9 %copy-start.29 = (bf16[512,1024]{1,0:T(8,128)(2,1)}, bf16[512,1024]{1,0:T(8,128)(2,1)S(1)}, u32[]{:S(2)}) copy-start(bf16[512,1024]{1,0:T(8,128)(2,1)S(1)} %get-tuple-element.74) | copy-start | bytes 3145732
  386.4 1.3 copy-start.16
  414.2 8.0 %collective-permute-start.1 = (f32[3,2048]{1,0:T(4,128)S(1)}, f32[3,2048]{1,0:T(4,128)S(1)}, u32[]{:S(2)}, u32[]{:S(2)}) collective-permute-start(f32[3,2048]{1,0:T(4,128)S(1)} %slice.46), channel_id=1, source_target_pairs={{1,0},{2,1},{3,2},{4,3},{5,4},{6,5},{7,6},{9,8},{10,9},{11,10},{12... | collective-permute-start | bytes 73736 | tf_op jit(solution)/shard_map/ppermute | solution.py:27
  415.5 7.9 %copy-start.3 = (bf16[4,128,2048]{2,1,0:T(8,128)(2,1)S(1)}, bf16[4,128,2048]{2,1,0:T(8,128)(2,1)}, u32[]{:S(2)}) copy-start(bf16[4,128,2048]{2,1,0:T(8,128)(2,1)} %copy-done.2) | copy-start | bytes 6291460
  423.4 13.1 %copy-start.30 = (bf16[512,1024]{1,0:T(8,128)(2,1)S(1)}, bf16[512,1024]{1,0:T(8,128)(2,1)}, u32[]{:S(2)}) copy-start(bf16[512,1024]{1,0:T(8,128)(2,1)} %copy-done.29) | copy-start | bytes 3145732
  435.2 1.3 copy-start.57
  440.9 1.4 copy-start.60
  442.3 6.9 %copy-start.9 = (bf16[8,128,2048]{2,1,0:T(8,128)(2,1)S(1)}, bf16[8,128,2048]{2,1,0:T(8,128)(2,1)}, u32[]{:S(2)}) copy-start(bf16[8,128,2048]{2,1,0:T(8,128)(2,1)} %copy-done.8) | copy-start | bytes 12582916
  442.3 6.9 %copy-start.62 = (bf16[1024,704]{0,1:T(8,128)(2,1)S(1)}, bf16[1024,704]{0,1:T(8,128)(2,1)}, u32[]{:S(2)}) copy-start(bf16[1024,704]{0,1:T(8,128)(2,1)} %copy-done.61) | copy-start | bytes 4325380
  449.2 4.5 copy-start.52
  449.2 4.5 copy-start.63
  453.7 52.2 %copy-start.58 = (bf16[512,2048]{1,0:T(8,128)(2,1)S(1)}, bf16[512,2048]{1,0:T(8,128)(2,1)}, u32[]{:S(2)}) copy-start(bf16[512,2048]{1,0:T(8,128)(2,1)} %copy-done.57) | copy-start | bytes 6291460
  458.3 47.7 %copy-start.55 = (bf16[512,2048]{1,0:T(8,128)(2,1)S(1)}, bf16[512,2048]{1,0:T(8,128)(2,1)}, u32[]{:S(2)}) copy-start(bf16[512,2048]{1,0:T(8,128)(2,1)} %convert_dynamic-update-slice_fusion) | copy-start | bytes 6291460
  655.1 1.1 copy-start.19
  657.3 12.9 %copy-start.11 = (f32[128,2048]{1,0:T(8,128)S(1)}, f32[128,2048]{1,0:T(8,128)}, u32[]{:S(2)}) copy-start(f32[128,2048]{1,0:T(8,128)} %copy-done.10) | copy-start | bytes 3145732
  661.3 11.4 %copy-start.5 = (f32[128,2048]{1,0:T(8,128)S(1)}, f32[128,2048]{1,0:T(8,128)}, u32[]{:S(2)}) copy-start(f32[128,2048]{1,0:T(8,128)} %copy-done.4) | copy-start | bytes 3145732
  661.3 11.4 %copy-start.40 = (bf16[128,2048]{1,0:T(8,128)(2,1)S(1)}, bf16[128,2048]{1,0:T(8,128)(2,1)}, u32[]{:S(2)}) copy-start(bf16[128,2048]{1,0:T(8,128)(2,1)} %param.17) | copy-start | bytes 1572868
  678.0 5.3 copy-start.18
  678.0 6.4 copy-start.1
  (6 other events, 6.1 us)
Sparse Core Ops, SparseCore 0:
  10.2 76.7 all-gather.2
  314.4 102.0 reduce-scatter.7
  420.6 92.4 reduce-scatter.3
  516.6 125.3 reduce-scatter.5

commit v3 on v2

--- a/solution.py
+++ b/solution.py
@@ -18,7 +18,7 @@
 epsilon = 1e-06
 bf16 = jnp.bfloat16
 f32 = jnp.float32
-VMEM_BYTES = 48 * 2**20
+VMEM_BYTES = 56 * 2**20
 
 
 def passed_along(value, axis, steps):
@@ -40,7 +40,12 @@
 def token_columns(decay_code, beta_code, total_len):
     rows, heads = decay_code.shape
     rates = log_rates(decay_code, total_len)
-    run = jnp.cumsum(rates.reshape(rows // STRETCH, STRETCH, heads), axis=1)
+    run = jnp.einsum(
+        "ij,bjh->bih",
+        jnp.tril(jnp.ones((STRETCH, STRETCH), f32)),
+        rates.reshape(rows // STRETCH, STRETCH, heads),
+        precision=lax.Precision.HIGHEST,
+    )
     last = jnp.broadcast_to(run[:, -1:], run.shape).reshape(rows, heads)
     run = run.reshape(rows, heads)
     beta = 0.5 + beta_code.astype(f32) / 512.0
@@ -772,10 +777,9 @@
     yield
     loads[1].wait()
     copies[1].wait_recv()
-    out_ref[...] = own[1].astype(f32) + crossed[1].astype(f32)
-    yield
     onward.wait_recv()
-    out_ref[...] += passed[...].astype(f32)
+    total = own[1].astype(f32) + crossed[1].astype(f32) + passed[...].astype(f32)
+    out_ref[...] = total.astype(out_ref.dtype)
     onward.wait_send()
     for copy in copies:
         copy.wait_send()
@@ -870,12 +874,12 @@
 
     def load(piece, target):
         return pltpu.make_async_copy(
-            source_at(target * SIDE + side, piece), own.at[piece, target], local.at[piece, target]
+            source_at(target, side, piece), own.at[piece, target], local.at[piece, target]
         )
 
     def cross(piece, target):
         return remote(
-            source_at(target * SIDE + 1 - side, piece),
+            source_at(target, 1 - side, piece),
             crossed.at[piece, target],
             sends.at[0, piece, target],
             arrivals.at[0, piece, target],
@@ -898,56 +902,61 @@
         else:
             pl.when(there)(body)
 
+    def here(piece, target):
+        load(piece, target).wait()
+        total = own[piece, target].astype(f32)
+        if crossed is not None:
+            cross(piece, target).wait_recv()
+            total += crossed[piece, target].astype(f32)
+        return total
+
+    def arrived(piece, target, way):
+        landing = risen if way > 0 else fallen
+        onward(piece, target, way, True).wait_recv()
+        return landing[piece, target].astype(f32)
+
     for piece in range(pieces):
         for distance in range(count - 1, -1, -1):
             for target, there, _ in targets(distance):
 
                 def begin(piece=piece, target=target):
-                    cross(piece, target).start()
+                    if crossed is not None:
+                        cross(piece, target).start()
                     load(piece, target).start()
 
                 guarded(there, begin)
     yield
     for piece in range(pieces):
         for distance in range(count - 1, 0, -1):
-            for way in (-1, 1):
-                target = line + way * distance
-                there = line >= distance if way < 0 else line + distance < count
+            for target, there, way in targets(distance):
                 first = line == count - 1 if way < 0 else line == 0
-                landing = risen if way > 0 else fallen
-
-                @pl.when(there)
-                def _(piece=piece, target=target, way=way, first=first, landing=landing):
-                    load(piece, target).wait()
-                    cross(piece, target).wait_recv()
-                    total = own[piece, target].astype(f32) + crossed[piece, target].astype(f32)
-
-                    @pl.when(first)
-                    def _():
-                        own[piece, target] = total.astype(own.dtype)
-
-                    @pl.when(jnp.logical_not(first))
-                    def _():
-                        onward(piece, target, way, True).wait_recv()
-                        own[piece, target] = (
-                            total + landing[piece, target].astype(f32)
-                        ).astype(own.dtype)
-
+
+                @pl.when(jnp.logical_and(there, first))
+                def _(piece=piece, target=target, way=way):
+                    own[piece, target] = here(piece, target).astype(own.dtype)
                     onward(piece, target, way).start()
 
+                @pl.when(jnp.logical_and(there, jnp.logical_not(first)))
+                def _(piece=piece, target=target, way=way):
+                    total = here(piece, target) + arrived(piece, target, way)
+                    own[piece, target] = total.astype(own.dtype)
+                    onward(piece, target, way).start()
+
             yield
-        load(piece, line).wait()
-        cross(piece, line).wait_recv()
         out = out_at(piece)
-        out[...] = own[piece, line].astype(f32) + crossed[piece, line].astype(f32)
-        yield
-        for way, arrives in ((-1, line < count - 1), (1, line > 0)):
-            landing = risen if way > 0 else fallen
-
-            @pl.when(arrives)
-            def _(way=way, landing=landing, piece=piece, out=out):
-                onward(piece, line, way, True).wait_recv()
-                out[...] += landing[piece, line].astype(f32)
+
+        @pl.when(line == 0)
+        def _(piece=piece, out=out):
+            out[...] = (here(piece, line) + arrived(piece, line, -1)).astype(out.dtype)
+
+        @pl.when(line == count - 1)
+        def _(piece=piece, out=out):
+            out[...] = (here(piece, line) + arrived(piece, line, 1)).astype(out.dtype)
+
+        @pl.when(jnp.logical_and(line > 0, line < count - 1))
+        def _(piece=piece, out=out):
+            total = here(piece, line) + arrived(piece, line, -1) + arrived(piece, line, 1)
+            out[...] = total.astype(out.dtype)
 
         yield
     for piece in range(pieces):
@@ -955,7 +964,8 @@
             for target, there, way in targets(distance):
 
                 def finish(piece=piece, target=target, way=way):
-                    cross(piece, target).wait_send()
+                    if crossed is not None:
+                        cross(piece, target).wait_send()
                     if way:
                         onward(piece, target, way).wait_send()
 
@@ -1085,10 +1095,9 @@
     def body(source, out, *rest):
         greet(seq_partners(count))
 
-        def source_at(target, piece):
-            return source.at[
-                pl.ds(pl.multiple_of(target * rows, rows), rows), pl.ds(piece * width, width)
-            ]
+        def source_at(target, side, piece):
+            begin = pl.multiple_of((target * SIDE + side) * rows, rows)
+            return source.at[pl.ds(begin, rows), pl.ds(piece * width, width)]
 
         def out_at(piece):
             return out.at[:, pl.ds(piece * width, width)]
@@ -1106,60 +1115,105 @@
     )(value)
 
 
-def scattered_last(qkv, normed, mlp, number, pieces=4):
+def scattered_last(qkv, gate, normed, mlp, small, gain_rows, number, pieces=4, gate_pieces=2):
     total, heads = lax.axis_size("seq"), lax.axis_size("head")
     count = total // SIDE
-    if total % SIDE or count < 2 or heads != 4:
-        return (
-            scattered(qkv, "seq"),
-            scattered(normed, "head"),
-            [scattered(part, "head", 1) for part in mlp],
-        )
     rows, width = qkv.shape[0] // total, qkv.shape[1] // pieces
+    gate_width = gate.shape[1] // gate_pieces
     own_rows = normed.shape[0] // heads
     units, slices = mlp[0].shape[0], mlp[0].shape[1] // heads
-
-    def body(qkv_ref, normed_ref, *rest):
+    small_rows = small.shape[0]
+
+    def body(qkv_ref, gate_ref, normed_ref, small_ref, *rest):
         mlp_refs, rest = rest[: len(mlp)], rest[len(mlp) :]
-        qkv_out, normed_out, rest = rest[0], rest[1], rest[2:]
+        qkv_out, gate_out, normed_out, small_out, rest = rest[0], rest[1], rest[2], rest[3], rest[4:]
         mlp_outs, rest = rest[: len(mlp)], rest[len(mlp) :]
         greet(head_partners() + seq_partners(count))
 
-        def qkv_at(target, piece):
-            return qkv_ref.at[
-                pl.ds(pl.multiple_of(target * rows, rows), rows), pl.ds(piece * width, width)
-            ]
-
-        def qkv_out_at(piece):
-            return qkv_out.at[:, pl.ds(piece * width, width)]
+        def qkv_at(target, side, piece):
+            begin = pl.multiple_of((target * SIDE + side) * rows, rows)
+            return qkv_ref.at[pl.ds(begin, rows), pl.ds(piece * width, width)]
+
+        def gate_at(target, side, piece):
+            begin = pl.multiple_of(target * rows, rows)
+            return gate_ref.at[pl.ds(begin, rows), pl.ds(piece * gate_width, gate_width)]
 
         def normed_at(target):
             return normed_ref.at[pl.ds(pl.multiple_of(target * own_rows, own_rows), own_rows)]
 
-        steps = [scatter_seq(qkv_at, qkv_out_at, *rest[:7], count)]
-        steps.append(scatter_head(normed_at, normed_out, *rest[7:13]))
+        def small_steps(four, own, local, *sems):
+            yield from gather_head(small_ref, four, sems[0], sems[1], sems[2], 1)
+            own[...] = four[lax.axis_index("head")]
+            own[:gain_rows] = jnp.sum(four[:, :gain_rows], axis=0)
+            yield from gather_seq(own, small_out, local, *sems[3:7], count)
+
+        steps = [
+            scatter_seq(qkv_at, lambda piece: qkv_out.at[:, pl.ds(piece * width, width)], *rest[:7], count),
+            scatter_seq(
+                gate_at,
+                lambda piece: gate_out.at[:, pl.ds(piece * gate_width, gate_width)],
+                rest[7],
+                None,
+                *rest[8:13],
+                count,
+            ),
+            scatter_head(normed_at, normed_out, *rest[13:19]),
+            small_steps(*rest[19:29]),
+        ]
         for index, (ref, out) in enumerate(zip(mlp_refs, mlp_outs)):
 
             def mlp_at(target, ref=ref):
                 return ref.at[:, pl.ds(pl.multiple_of(target * slices, slices), slices)]
 
-            begin = 13 + 6 * index
+            begin = 29 + 6 * index
             steps.append(scatter_head(mlp_at, out, *rest[begin : begin + 6]))
         run_together(steps)
 
+    line_scratch = seq_scratch(gate_pieces, count, rows, gate_width)
     outs = link_call(
         body,
         number,
-        [ANY] * (2 + len(mlp)),
-        [IN_VMEM] * (2 + len(mlp)),
-        [shaped((rows, qkv.shape[1]), f32), shaped((own_rows, normed.shape[1]), f32)]
-        + [shaped((units, slices), f32) for _ in mlp],
+        [ANY] * (4 + len(mlp)),
+        [IN_VMEM] * (4 + len(mlp)),
+        [
+            shaped((rows, qkv.shape[1]), bf16),
+            shaped((rows, gate.shape[1]), bf16),
+            shaped((own_rows, normed.shape[1]), f32),
+            shaped((total, small_rows, small.shape[1]), f32),
+        ]
+        + [shaped((units, slices), bf16) for _ in mlp],
         seq_scratch(pieces, count, rows, width)
+        + line_scratch[1:]
         + head_scratch(own_rows, normed.shape[1])
+        + [
+            pltpu.VMEM((heads, small_rows, small.shape[1]), f32),
+            pltpu.VMEM((small_rows, small.shape[1]), f32),
+            DMA((1,)),
+            DMA((1,)),
+            DMA((3, 1)),
+            DMA((3, 1)),
+        ]
+        + [DMA((2 * count,)) for _ in range(4)]
         + head_scratch(units, slices) * len(mlp),
         250_000_000,
-    )(qkv, normed, *mlp)
-    return outs[0], outs[1], list(outs[2:])
+    )(qkv, gate, normed, small, *mlp)
+    return outs[0], outs[1], outs[2], outs[3], list(outs[4:])
+
+
+def side_columns(value, side, rows):
+    count = value.shape[1] // (rows * SIDE)
+    return jnp.concatenate(
+        [
+            lax.dynamic_slice_in_dim(value, (place * SIDE + side) * rows, rows, 1)
+            for place in range(count)
+        ],
+        axis=1,
+    )
+
+
+def swapped(value):
+    count = lax.axis_size("seq")
+    return lax.ppermute(value, "seq", [(place, place ^ 1) for place in range(count)])
 
 
 def silu_slope(tensor):
@@ -1207,9 +1261,15 @@
     out_flat = out_weight.reshape(heads * DV, width)
     columns, run_rows = token_columns(decay_code, beta_code, total_len)
 
-    wide_in = gathered_head(block_in, 1).astype(f32)
-    hat_first = wide_in * rms_scale(wide_in)
-    normed_first = (hat_first * gain_first).astype(bf16)
+    seq_count, head_count = lax.axis_size("seq"), lax.axis_size("head")
+    seq_at, head_at = lax.axis_index("seq"), lax.axis_index("head")
+    side = lax.rem(seq_at, SIDE)
+    slice_rows = width // seq_count
+    scale_own = rms_scale(input_f)
+    hat_own = input_f * scale_own
+    normed_own = (hat_own * gain_first).astype(bf16)
+    normed_first = gathered(normed_own, "head")
+    normed_side = gathered(swapped(side_columns(normed_own, 1 - side, slice_rows)), "head")
     mixed_in = mm(normed_first, qkv_flat).astype(bf16)
     tail_in = passed_along(mixed_in[span_rows - 8 :], "seq", 1)
     tail_in = jnp.where(jnp.arange(8)[:, None] >= 8 - lead_rows, tail_in.astype(f32), 0.0)
@@ -1254,8 +1314,7 @@
     grad_ends = gathered_seq(grad_end.reshape(-1, DV), 7).reshape(-1, heads, DK, DV)
     grad_out_w = mm_tn(branch, d_mix_all)
     grad_out_s = scattered(grad_out_w, "seq", 1).reshape(heads, DV, -1)
-    grad_gate = mm_tn(normed_first, d_gate_low)
-    grad_gate_s = scattered(grad_gate, "seq").reshape(-1, heads, DV)
+    d_gate_side = swapped(d_gate_low)
     d_mixed, d_tail, d_lead, grad_conv = run_finish_backward(
         ends,
         grad_ends,
@@ -1275,57 +1334,64 @@
     d_tail = d_tail.at[8 - lead_rows :].add(from_next).astype(bf16)
     d_mixed = lax.dynamic_update_slice(d_mixed, d_tail, (span_rows - 8, 0))
     d_normed_part = mm_nt(d_mixed, qkv_flat) + mm_nt(d_gate_low, gate_flat)
-    gain_one_part = jnp.sum(d_normed_part * hat_first, 0)
+    gain_one_part = jnp.sum(d_normed_part * normed_first.astype(f32), 0) / gain_first
     grad_qkv = mm_tn(normed_first, d_mixed).astype(bf16)
+    grad_gate = (
+        mm_tn(side_columns(normed_first, side, slice_rows), d_gate_low)
+        + mm_tn(normed_side, d_gate_side)
+    ).astype(bf16)
     grad_mgate = mm_tn(d_gate_mlp, rows_out).astype(bf16)
     grad_mup = mm_tn(d_up_mlp, rows_out).astype(bf16)
     grad_down = mm_tn(hidden, cot_all).astype(bf16)
 
-    small = jnp.concatenate(
-        [gain_one_part, gain_two_part, gain_out_part.reshape(-1), grad_conv.reshape(-1)]
-    ).astype(bf16)
-    small_all = lax.all_gather(small, ("seq", "head"))
-    grad_qkv_s, d_normed_one, (grad_mgate_t, grad_mup_t, grad_down_h) = scattered_last(
-        grad_qkv, d_normed_part.astype(bf16), [grad_mgate, grad_mup, grad_down], 8
-    )
-    scale_own = rms_scale(input_f)
-    hat_own = input_f * scale_own
+    gains = jnp.concatenate([gain_one_part, gain_two_part, gain_out_part.reshape(-1)])
+    gain_rows = -(-gains.shape[0] // 1024) * 8
+    gains = jnp.pad(gains, (0, gain_rows * 128 - gains.shape[0])).reshape(gain_rows, 128)
+    small = jnp.concatenate([gains, grad_conv.reshape(-1, 128)])
+    grad_qkv_s, grad_gate_s, d_normed_one, small_all, (grad_mgate_t, grad_mup_t, grad_down_h) = (
+        scattered_last(
+            grad_qkv,
+            grad_gate,
+            d_normed_part.astype(bf16),
+            [grad_mgate, grad_mup, grad_down],
+            small,
+            gain_rows,
+            8,
+        )
+    )
     e_one = d_normed_one * gain_first
     d_input = (
         d_middle + scale_own * (e_one - hat_own * jnp.mean(e_one * hat_own, axis=-1, keepdims=True))
     ).astype(bf16)
 
-    seq_count, head_count = lax.axis_size("seq"), lax.axis_size("head")
-    seq_at, head_at = lax.axis_index("seq"), lax.axis_index("head")
-    gains = jnp.sum(small_all[:, : 2 * width + DV].astype(f32), axis=0)
-
-    def own_slice(vector):
-        length = vector.shape[0] // (seq_count * head_count)
-        return lax.dynamic_slice(vector, ((head_at * seq_count + seq_at) * length,), (length,))
-
-    gain_one_g = own_slice(gains[:width])
-    gain_two_g = own_slice(gains[width : 2 * width])
-    gain_out_g = own_slice(gains[2 * width :])
-    conv_all = lax.dynamic_index_in_dim(
-        small_all[:, 2 * width + DV :].reshape(seq_count, head_count, -1), head_at, 1, False
-    )
-    conv_sum = jnp.sum(conv_all.astype(f32), axis=0).reshape(-1, heads, inner)
+    small_sum = jnp.sum(small_all, axis=0)
+    gains = small_sum[:gain_rows].reshape(-1)
+
+    def own_slice(begin, length):
+        length = length // (seq_count * head_count)
+        return lax.dynamic_slice(
+            gains, (begin + (head_at * seq_count + seq_at) * length,), (length,)
+        )
+
     grad_conv_s = lax.dynamic_slice_in_dim(
-        conv_sum, seq_at * (inner // seq_count), inner // seq_count, 2
+        small_sum[gain_rows:].reshape(-1, heads, inner),
+        seq_at * (inner // seq_count),
+        inner // seq_count,
+        2,
     )
     return (
         output,
         d_input,
-        gain_one_g,
-        grad_qkv_s.reshape(-1, heads, inner),
+        own_slice(0, width),
+        grad_qkv_s.astype(f32).reshape(-1, heads, inner),
         grad_conv_s,
-        grad_gate_s,
-        gain_out_g,
+        grad_gate_s.astype(f32).reshape(-1, heads, DV),
+        own_slice(2 * width, DV),
         grad_out_s,
-        gain_two_g,
-        grad_mgate_t.T,
-        grad_mup_t.T,
-        grad_down_h,
+        own_slice(width, width),
+        grad_mgate_t.astype(f32).T,
+        grad_mup_t.astype(f32).T,
+        grad_down_h.astype(f32),
     )
 
 

time: 698 us -> 703 us (level)
  Pallas kernels: 446 us -> 498 us
  blocking collectives: 46.6 us -> 0 us
  local copies, waits for them, and re-layouts: 57.8 us -> 36 us
  matrix products: 96 us -> 110 us
    all_gather x1 -> x0, blocking collectives: 46.6 us -> none  [on_device(): small_all = lax.all_gather(small, ('seq', 'head'))]
    pallas_call x3, Pallas kernels: 140 us -> 173 us  [gathered_seq(): link_call(body, number, [ANY], ANY, shaped((total, rows, width), value.dt...]
    unnamed x137 -> x94, local copies, waits for them, and re-layouts: 42.9 us -> 18.8 us
    pallas_call x1, Pallas kernels: 140 us -> 163 us  [scattered_last(): link_call(body, number, [ANY] * (4 + len(mlp)), [IN_VMEM] * (4 + len(mlp)...]
    pallas_call x2 -> x1, Pallas kernels: 31.2 us -> 18.9 us  [gathered_head(): link_call(body, number, [ANY], ANY, shaped((count, rows, width), value.dt...]
    dot_general x6 -> x7, matrix products: 31.8 us -> 39.4 us  [mm_tn(): lax.dot_general(left, right, (((0,), (0,)), ((), ())), preferred_element_...]
  transfers between devices with their start and end apart: 6 -> 9, of which waited for: 0 -> 1; matrix products, arithmetic and copies ran while one was open for 17% -> 23% of each run, Pallas kernels for 48% -> 72%
where the time goes in v3:
time: 703 us; the launch traced here: 696 us
  Pallas kernels  498 us (71%)
  matrix products  110 us (16%)
  local copies, waits for them, and re-layouts  36 us (5%)
  other arithmetic  25.6 us (4%)
  between operations  14.6 us (2%)
  starting transfers between devices  11 us (2%)
    pallas_call x3, Pallas kernels, gathered_seq(): link_call(body, number, [ANY], ANY, shaped((total, rows, width), value.dt...  173 us
    pallas_call x1, Pallas kernels, scattered_last(): link_call(body, number, [ANY] * (4 + len(mlp)), [IN_VMEM] * (4 + len(mlp)...  163 us
    pallas_call x1, Pallas kernels, scattered_seq(): link_call(body, number, [ANY], IN_VMEM, shaped((rows, value.shape[1]), f3...  54.5 us
    dot_general x6, matrix products, mm_nt(): lax.dot_general(left, right, (((1,), (1,)), ((), ())), preferred_element_...  39.6 us
    dot_general x7, matrix products, mm_tn(): lax.dot_general(left, right, (((0,), (0,)), ((), ())), preferred_element_...  39.4 us
    dot_general x6, matrix products, mm(): return jnp.dot(left, right, preferred_element_type=f32)  30.7 us
    pallas_call x1, Pallas kernels, run_finish_backward(): kernel_call(finish_backward, heads, [whole(ends.shape), whole(grad_ends.s...  27.2 us
    pallas_call x1, Pallas kernels, run_local_forward(): kernel_call(local_forward, heads, [by_columns(rows, INNER), by_columns(8,...  22.9 us
  transfers between devices with their start and end apart: 9, of which 1 were waited for; matrix products, arithmetic and copies ran while one was open for 23% of the time, Pallas kernels for 72%

profile of v3, /device:TPU:0, one launch (start us, length us, event | category | flops | bytes accessed | tf_op | source)
XLA Modules:
  0.0 695.8 jit_solution(15889978282548648043)
XLA Ops:
  7.2 0.8 convert_element_type.102
  8.1 1.2 fusion.10
  9.3 2.0 fusion.4
  11.4 0.7 all-gather.6.cloned.1.call-update
  12.2 1.0 constant_dynamic-slice_fusion.4
  13.2 0.7 pad_maximum_fusion
  13.9 2.9 collective-permute-start.2
  16.9 10.4 %copy.31 = bf16[256,8,4,512]{3,1,2,0:T(8,128)(2,1)} copy(bf16[256,8,4,512]{3,2,1,0:T(4,128)(2,1)} %bitcast.74) | data formatting | bytes 16777216
  28.7 0.7 pad.14.clone.columns_ref
  30.1 5.2 copy.33
  35.9 0.7 copy-done.17
  36.8 8.7 %convolution_convert_fusion.7.mixed_ref = bf16[512,2048]{1,0:T(8,128)(2,1)S(1)} fusion(bf16[512,2048]{1,0:T(8,128)(2,1)} %all-gather.4.cloned.1.call-done, bf16[2048,2048]{1,0:T(8,128)(2,1)} %bitcast.75), kind=kOutput, calls=%fused_computation.11 | convolution fusion | flops 4296015872 | bytes 12582912 | tf_op jit(solution)/shard_map/dot_general | solution.py:62
  45.5 3.8 collective-permute-start
  49.4 3.7 fusion.30.gate_ref
  53.1 0.7 convert_select_fusion.tail_ref
  53.8 22.9 %shard_map.229 = (bf16[4,2,256,256]{3,2,1,0:T(8,128)(2,1)}, bf16[4,2,256,256]{3,2,1,0:T(8,128)(2,1)}, bf16[4,512,384]{2,1,0:T(8,128)(2,1)}, bf16[4,512,128]{2,1,...) custom-call(bf16[512,2048]{1,0:T(8,128)(2,1)} %copy-done.31, ...), custom_call_target="tpu_custom_call" | custom-call | flops 12000000000 | bytes 20000000 | tf_op jit(solution)/shard_map/pallas_call | solution.py:484
  76.7 66.5 %shard_map.230 = bf16[8,512,384]{2,1,0:T(8,128)(2,1)} custom-call(bf16[512,384]{1,0:T(8,128)(2,1)} %bitcast.90), custom_call_target="tpu_custom_call" | custom-call | bytes 120000000 | tf_op jit(solution)/shard_map/pallas_call | solution.py:1027
  143.3 10.5 %shard_map.231 = (bf16[4,8,128,256]{3,2,1,0:T(8,128)(2,1)}, f32[512,1024]{1,0:T(8,128)}, bf16[512,1024]{1,0:T(8,128)(2,1)}) custom-call(bf16[8,4,128,384]{3,2,1,0:T(8,128)(2,1)} %bitcast.84, bf16[4,8,128,384]{3,2,1,0:T(8,128)(2,1)} %get-tuple-element.56.local_ref, bf16[4,512,128]{2,1,0:T(8,128)(2,1)} %get-tuple-element.57.reach_ref, ...), custom_call_target="tpu_custom_call" | custom-call | flops 3000000000 | bytes 20000000 | tf_op jit(solution)/shard_map/pallas_call | solution.py:527
  153.7 4.9 convolution_convert_fusion.6.source
  158.6 17.3 %shard_map.232 = f32[128,2048]{1,0:T(8,128)} custom-call(bf16[512,2048]{1,0:T(8,128)(2,1)} %convolution_convert_fusion.6.source), custom_call_target="tpu_custom_call" | custom-call | bytes 60000000 | tf_op jit(solution)/shard_map/pallas_call | solution.py:1077
  176.0 1.4 multiply_reduce_fusion.3
  177.4 1.0 copy-done.1
  178.4 0.9 multiply_convert_fusion.3.own_ref
  179.3 53.5 %shard_map.233 = bf16[8,128,2048]{2,1,0:T(8,128)(2,1)} custom-call(bf16[128,2048]{1,0:T(8,128)(2,1)} %multiply_convert_fusion.3.own_ref), custom_call_target="tpu_custom_call" | custom-call | bytes 120000000 | tf_op jit(solution)/shard_map/pallas_call | solution.py:1027
  232.9 5.2 fusion.31
  238.2 3.2 fusion.32
  241.4 5.3 multiply_convert_fusion
  246.7 3.5 fusion.33
  250.3 5.2 add_convert_fusion.source
  255.5 54.5 %shard_map.234 = f32[128,2048]{1,0:T(8,128)} custom-call(bf16[1024,2048]{1,0:T(8,128)(2,1)} %add_convert_fusion.source), custom_call_target="tpu_custom_call" | custom-call | bytes 120000000 | tf_op jit(solution)/shard_map/pallas_call | solution.py:1107
  310.0 1.6 multiply_reduce_fusion.1
  311.6 2.4 fusion.27.own_ref
  314.1 18.9 %shard_map.235 = bf16[4,128,2048]{2,1,0:T(8,128)(2,1)} custom-call(bf16[128,2048]{1,0:T(8,128)(2,1)} %fusion.27.own_ref), custom_call_target="tpu_custom_call" | custom-call | bytes 60000000 | tf_op jit(solution)/shard_map/pallas_call | solution.py:1004
  333.0 6.0 convolution_convert_fusion.1
  339.1 2.2 constant_dynamic-slice_fusion.8
  341.3 6.5 fusion.34.d_branch_ref
  347.8 10.4 %shard_map.236 = (bf16[512,1024]{1,0:T(8,128)(2,1)}, bf16[512,1024]{1,0:T(8,128)(2,1)}, f32[1,256]{1,0:T(1,128)}, bf16[4,8,128,384]{3,2,1,0:T(8,128)(2,1)}, bf16[4,128,256]{2,1,0:T(8,128)(2,1)}) custom-call(f32[512,1024]{1,0:T(8,128)} %fusion.34.d_branch_ref, f32[512,1024]{1,0:T(8,128)} %get-tuple-element.64.core_ref, f32[512,1024]{1,0:T(8,128)} %fusion.30.gate_ref, ...), custom_call_target="tpu_custom_call" | custom-call | flops 4000000000 | bytes 20000000 | tf_op jit(solution)/shard_map/pallas_call | solution.py:553
  358.2 53.4 %shard_map.237 = bf16[8,512,256]{2,1,0:T(8,128)(2,1)} custom-call(bf16[512,256]{1,0:T(8,128)(2,1)} %bitcast.91), custom_call_target="tpu_custom_call" | custom-call | bytes 120000000 | tf_op jit(solution)/shard_map/pallas_call | solution.py:1027
  411.6 27.2 %shard_map.238 = (bf16[512,2048]{1,0:T(8,128)(2,1)}, f32[8,2048]{1,0:T(8,128)}, f32[8,2048]{1,0:T(8,128)}, f32[4,2048]{1,0:T(4,128)}) custom-call(bf16[8,4,128,384]{3,2,1,0:T(8,128)(2,1)} %bitcast.85, bf16[8,4,128,256]{3,2,1,0:T(8,128)(2,1)} %bitcast.88, bf16[512,2048]{1,0:T(8,128)(2,1)} %copy-done.31, f32[8,2048]{1,0:T(8,128)} %convert_select_fusion.tail_ref, ...), custom_call_target="tpu_custom_call" | custom-call | flops 12000000000 | bytes 20000000 | tf_op jit(solution)/shard_map/pallas_call | solution.py:591
  438.8 1.5 slice.37
  440.3 1.3 collective-permute-start.1
  441.6 2.7 collective-permute-start.3
  444.3 5.1 convolution_convert_fusion.2
  449.4 7.4 %convolution_convert_fusion.5.rest_0_ = bf16[704,2048]{1,0:T(8,128)(2,1)} fusion(bf16[1024,704]{0,1:T(8,128)(2,1)} %copy-done.40, bf16[1024,2048]{1,0:T(8,128)(2,1)} %bitcast.78), kind=kOutput, calls=%fused_computation.8 | convolution fusion | flops 2954231808 | bytes 8519680 | tf_op jit(solution)/shard_map/dot_general | solution.py:70
  456.8 7.0 %fusion.35 = f32[512,2048]{1,0:T(8,128)} fusion(bf16[512,1024]{1,0:T(8,128)(2,1)} %get-tuple-element.76, bf16[2048,1024]{1,0:T(8,128)(2,1)} %bitcast.82), kind=kOutput, calls=%fused_computation.93 | convolution fusion | flops 2147483648 | bytes 9437184 | tf_op jit(solution)/shard_map/dot_general | solution.py:66
  463.8 4.5 convolution_convert_fusion.4.rest_1_
  468.3 4.5 convolution_convert_fusion.3.rest_2_
  472.9 4.6 fusion.11
  477.5 1.4 reshape.172
  479.5 0.8 slice_add_fusion
  480.3 0.7 scatter-add.4
  481.6 12.1 %multiply_reduce_fusion = (f32[2048]{0:T(1024)S(1)}, bf16[512,2048]{1,0:T(8,128)(2,1)}) fusion(bf16[512,2048]{1,0:T(8,128)(2,1)} %all-gather.4.cloned.1.call-done, f32[512,2048]{1,0:T(8,128)} %fusion.35, bf16[512,2048]{1,0:T(8,128)(2,1)} %convert_dynamic-update-slice_fusion, bf16[2048,2048]{1,0:T(8,128)(2,1)} %bitcast.76), kind=kOutput, calls=%fused_computation.2 | convolution fusion | flops 4300208128 | bytes 18882560 | tf_op jit(solution)/shard_map/dot_general | solution.py:66
  493.7 0.6 pad_maximum_fusion.1.small_ref
  494.4 6.9 convolution_convert_fusion.qkv_ref
  501.3 5.4 add_convert_fusion.1.gate_ref
  506.7 162.6 %shard_map.239 = (bf16[256,2048]{1,0:T(8,128)(2,1)}, bf16[256,1024]{1,0:T(8,128)(2,1)}, f32[128,2048]{1,0:T(8,128)}, f32[8,104,128]{2,1,0:T(8,128)}, bf16[704,51...) custom-call(bf16[2048,2048]{1,0:T(8,128)(2,1)} %convolution_convert_fusion.qkv_ref, ...), custom_call_target="tpu_custom_call" | custom-call | bytes 250000000 | tf_op jit(solution)/shard_map/pallas_call | solution.py:1173
  669.4 1.0 reduce_sum.69
  670.5 3.7 reshape.182
  674.2 2.5 reshape.184
  676.7 2.6 convert_element_type.130
  680.4 0.7 constant_dynamic-slice_fusion
  681.4 2.0 convert_bitcast_fusion
  683.4 2.1 convert.5
  685.5 3.6 fusion.9
  (135 shorter events, 6.0 us)
Async XLA Ops:
  7.2 234.2 %copy-start = (bf16[704,2048]{1,0:T(8,128)(2,1)S(1)}, bf16[704,2048]{1,0:T(8,128)(2,1)}, u32[]{:S(2)}) copy-start(bf16[704,2048]{1,0:T(8,128)(2,1)} %param.27) | copy-start | bytes 8650756
  7.2 29.6 %all-gather.4.cloned.1.call-start = ((), (), s32[]{:S(2)}) async-start(), calls=%async_computation.2 | async-start | bytes 2621440 | tf_op jit(solution)/shard_map/all_gather | solution.py:1225
  8.1 4.1 copy-start.19
  9.3 2.9 copy-start.27
  11.4 168.0 %all-gather.6.cloned.1.call-start = ((), (), s32[]{:S(2)}) async-start(), calls=%async_computation.3 | async-start | bytes 4718592 | tf_op jit(solution)/shard_map/all_gather | solution.py:1225
  12.1 489.2 %all-gather.8.cloned.1.call-start = ((), (), s32[]{:S(2)}) async-start(), calls=%async_computation.5 | async-start | bytes 1310720 | tf_op jit(solution)/shard_map/all_gather | solution.py:1225
  13.9 22.0 %collective-permute-start.2 = (bf16[128,1024]{1,0:T(8,128)(2,1)}, bf16[128,1024]{1,0:T(8,128)(2,1)S(1)}, u32[]{:S(2)}, u32[]{:S(2)}) collective-permute-start(bf16[128,1024]{1,0:T(8,128)(2,1)} %pad_maximum_fusion), channel_id=1, source_target_pairs={{0,1},{1,0},{2,3},{3,2},{4,5},{5,4},{6,7},{7,6},{8,9},{9,8},{10,11... | collective-permute-start | bytes 786440 | tf_op jit(solution)/shard_map/ppermute | solution.py:1216
  16.9 10.4 %copy-start.24 = (bf16[4,4,512]{2,1,0:T(4,128)(2,1)S(1)}, bf16[4,4,512]{2,1,0:T(4,128)(2,1)}, u32[]{:S(2)}) copy-start(bf16[4,4,512]{2,1,0:T(4,128)(2,1)} %param.20) | copy-start | bytes 49156
  16.9 11.0 %copy-start.25 = (s32[512,4]{0,1:T(4,128)S(1)}, s32[512,4]{0,1:T(4,128)}, u32[]{:S(2)}) copy-start(s32[512,4]{0,1:T(4,128)} %param.28) | copy-start | bytes 24580
  16.9 11.7 %copy-start.26 = (s32[512,4]{0,1:T(4,128)S(1)}, s32[512,4]{0,1:T(4,128)}, u32[]{:S(2)}) copy-start(s32[512,4]{0,1:T(4,128)} %param.29) | copy-start | bytes 24580
  30.1 5.2 copy-start.38
  30.1 5.8 copy-start.29
  35.9 0.7 copy-start.17
  36.6 646.7 %reduce-scatter.5.cloned.1.call-start = ((), (), s32[]{:S(2)}) async-start(), calls=%async_computation.6 | async-start | bytes 4718592 | tf_op jit(solution)/shard_map/reduce_scatter | solution.py:1229
  36.8 12.5 %copy-start.7 = (bf16[256,8,4,256]{3,1,2,0:T(8,128)(2,1)S(1)}, bf16[256,8,4,256]{3,1,2,0:T(8,128)(2,1)}, u32[]{:S(2)}) copy-start(bf16[256,8,4,256]{3,1,2,0:T(8,128)(2,1)} %copy.33) | copy-start | bytes 12582916
  36.8 12.5 %copy-start.11 = (bf16[512,2048]{1,0:T(8,128)(2,1)S(1)}, bf16[512,2048]{1,0:T(8,128)(2,1)}, u32[]{:S(2)}) copy-start(bf16[512,2048]{1,0:T(8,128)(2,1)} %all-gather.4.cloned.1.call-done) | copy-start | bytes 6291460
  45.5 7.6 %copy-start.31 = (bf16[512,2048]{1,0:T(8,128)(2,1)}, bf16[512,2048]{1,0:T(8,128)(2,1)S(1)}, u32[]{:S(2)}) copy-start(bf16[512,2048]{1,0:T(8,128)(2,1)S(1)} %convolution_convert_fusion.7.mixed_ref) | copy-start | bytes 6291460
  45.5 7.5 %collective-permute-start = (bf16[8,2048]{1,0:T(8,128)(2,1)S(1)}, bf16[8,2048]{1,0:T(8,128)(2,1)S(1)}, u32[]{:S(2)}, u32[]{:S(2)}) collective-permute-start(bf16[8,2048]{1,0:T(8,128)(2,1)S(1)} %slice.40), channel_id=1, source_target_pairs={{0,1},{1,2},{2,3},{3,4},{4,5},{5,6},{6,7},{8,9},{9,10},{10,11},{11... | collective-permute-start | bytes 98312 | tf_op jit(solution)/shard_map/ppermute | solution.py:27
  143.2 10.5 %copy-start.32 = (bf16[4,256,2048]{2,1,0:T(8,128)(2,1)S(1)}, bf16[4,256,2048]{2,1,0:T(8,128)(2,1)}, u32[]{:S(2)}) copy-start(bf16[4,256,2048]{2,1,0:T(8,128)(2,1)} %param.23) | copy-start | bytes 12582916
  158.6 17.3 %copy-start.3 = (bf16[128,2048]{1,0:T(8,128)(2,1)S(1)}, bf16[128,2048]{1,0:T(8,128)(2,1)}, u32[]{:S(2)}) copy-start(bf16[128,2048]{1,0:T(8,128)(2,1)} %param.16) | copy-start | bytes 1572868
  177.4 1.0 copy-start.1
  179.3 53.6 %copy-start.35 = (bf16[2048,704]{0,1:T(8,128)(2,1)S(1)}, bf16[2048,704]{0,1:T(8,128)(2,1)}, u32[]{:S(2)}) copy-start(bf16[2048,704]{0,1:T(8,128)(2,1)} %param.25) | copy-start | bytes 8650756
  232.9 5.3 copy-start.5
  232.9 5.3 copy-start.36
  238.2 3.2 copy-start.33
  246.7 3.5 copy-start.40
  246.7 3.6 copy-start.41
  255.5 54.5 %copy-start.2 = (f32[128,2048]{1,0:T(8,128)S(1)}, f32[128,2048]{1,0:T(8,128)}, u32[]{:S(2)}) copy-start(f32[128,2048]{1,0:T(8,128)} %copy-done.1) | copy-start | bytes 3145732
  255.5 56.1 %copy-start.4 = (bf16[128,2048]{1,0:T(8,128)(2,1)S(1)}, bf16[128,2048]{1,0:T(8,128)(2,1)}, u32[]{:S(2)}) copy-start(bf16[128,2048]{1,0:T(8,128)(2,1)} %param.17) | copy-start | bytes 1572868
  311.6 21.4 %copy-start.39 = (bf16[512,1024]{1,0:T(8,128)(2,1)S(1)}, bf16[512,1024]{1,0:T(8,128)(2,1)}, u32[]{:S(2)}) copy-start(bf16[512,1024]{1,0:T(8,128)(2,1)} %get-tuple-element.59) | copy-start | bytes 3145732
  339.0 346.4 %reduce-scatter.3.cloned.1.call-start = ((), (), s32[]{:S(2)}) async-start(), calls=%async_computation.4 | async-start | bytes 4718592 | tf_op jit(solution)/shard_map/reduce_scatter | solution.py:1229
  411.6 32.7 %copy-start.43 = (bf16[1024,704]{0,1:T(8,128)(2,1)S(1)}, bf16[1024,704]{0,1:T(8,128)(2,1)}, u32[]{:S(2)}) copy-start(bf16[1024,704]{0,1:T(8,128)(2,1)} %get-tuple-element.62) | copy-start | bytes 4325380
  440.3 38.6 %collective-permute-start.1 = (f32[3,2048]{1,0:T(4,128)}, f32[3,2048]{1,0:T(4,128)S(1)}, u32[]{:S(2)}, u32[]{:S(2)}) collective-permute-start(f32[3,2048]{1,0:T(4,128)} %slice.37), channel_id=1, source_target_pairs={{1,0},{2,1},{3,2},{4,3},{5,4},{6,5},{7,6},{9,8},{10,9},{11,10},{12... | collective-permute-start | bytes 73736 | tf_op jit(solution)/shard_map/ppermute | solution.py:27
  441.6 59.7 %collective-permute-start.3 = (bf16[512,1024]{1,0:T(8,128)(2,1)}, bf16[512,1024]{1,0:T(8,128)(2,1)}, u32[]{:S(2)}, u32[]{:S(2)}) collective-permute-start(bf16[512,1024]{1,0:T(8,128)(2,1)} %get-tuple-element.76), channel_id=1, source_target_pairs={{0,1},{1,0},{2,3},{3,2},{4,5},{5,4},{6,7},{7,6},{8,9},{9,8},{10,11... | collective-permute-start | bytes 3145736 | tf_op jit(solution)/shard_map/ppermute | solution.py:1216
  456.7 7.0 %copy-start.6 = (bf16[8,128,2048]{2,1,0:T(8,128)(2,1)S(1)}, bf16[8,128,2048]{2,1,0:T(8,128)(2,1)}, u32[]{:S(2)}) copy-start(bf16[8,128,2048]{2,1,0:T(8,128)(2,1)} %shard_map.233) | copy-start | bytes 12582916
  456.8 7.0 %copy-start.42 = (bf16[1024,704]{0,1:T(8,128)(2,1)S(1)}, bf16[1024,704]{0,1:T(8,128)(2,1)}, u32[]{:S(2)}) copy-start(bf16[1024,704]{0,1:T(8,128)(2,1)} %copy-done.41) | copy-start | bytes 4325380
  463.8 4.5 copy-start.34
  463.8 4.5 copy-start.44
  468.3 4.6 copy-start.13
  468.3 4.6 copy-start.14
  468.3 4.6 copy-start.15
  468.3 4.5 copy-start.16
  472.9 6.6 copy-start.18
  478.9 0.6 copy-start.22
  481.6 12.1 %copy-start.23 = (bf16[2048]{0:T(1024)(128)(2,1)S(1)}, bf16[2048]{0:T(1024)(128)(2,1)}, u32[]{:S(2)}) copy-start(bf16[2048]{0:T(1024)(128)(2,1)} %param.18) | copy-start | bytes 12292
  481.6 12.1 %copy-start.30 = (f32[1,256]{1,0:T(1,128)S(1)}, f32[1,256]{1,0:T(1,128)}, u32[]{:S(2)}) copy-start(f32[1,256]{1,0:T(1,128)} %get-tuple-element.77) | copy-start | bytes 3076
  481.6 12.1 %copy-start.21 = (f32[64,128]{1,0:T(8,128)S(1)}, f32[64,128]{1,0:T(8,128)}, u32[]{:S(2)}) copy-start(f32[64,128]{1,0:T(8,128)} %reshape.172) | copy-start | bytes 98308
  481.6 12.8 %copy-start.12 = (bf16[512,2048]{1,0:T(8,128)(2,1)S(1)}, bf16[512,2048]{1,0:T(8,128)(2,1)}, u32[]{:S(2)}) copy-start(bf16[512,2048]{1,0:T(8,128)(2,1)} %all-gather.4.cloned.1.call-done) | copy-start | bytes 6291460
  481.6 12.8 %copy-start.37 = (bf16[512,2048]{1,0:T(8,128)(2,1)S(1)}, bf16[512,2048]{1,0:T(8,128)(2,1)}, u32[]{:S(2)}) copy-start(bf16[512,2048]{1,0:T(8,128)(2,1)} %convert_dynamic-update-slice_fusion) | copy-start | bytes 6291460
  670.4 10.6 %copy-start.20 = (f32[2048]{0:T(1024)S(1)}, f32[2048]{0:T(1024)}, u32[]{:S(2)}) copy-start(f32[2048]{0:T(1024)} %copy-done.19) | copy-start | bytes 24580
  670.4 10.6 %copy-start.28 = (f32[128]{0:T(128)S(1)}, f32[128]{0:T(128)}, u32[]{:S(2)}) copy-start(f32[128]{0:T(128)} %copy-done.27) | copy-start | bytes 1540
  676.6 4.4 copy-start.8
  676.7 4.7 copy-start.9
  676.7 4.7 copy-start.10
Sparse Core Ops, SparseCore 0:
  11.5 25.2 all-gather.3
  38.9 88.4 all-gather.5
  129.0 15.7 all-gather.7
  339.2 103.6 reduce-scatter.4
  456.9 102.1 reduce-scatter.2

commit v4 on v3

--- a/solution.py
+++ b/solution.py
@@ -754,7 +754,7 @@
     keep.wait()
 
 
-def scatter_head(source_at, out_ref, own, crossed, passed, local, send, arrive):
+def scatter_head(source_at, out_ref, own, crossed, passed, local, send, arrive, pause=0):
     head, seq, sibling, across = head_places()
     far = lax.rem(sibling + 2, 4)
     loads = [
@@ -774,7 +774,8 @@
     own[0] = (own[0].astype(f32) + crossed[0].astype(f32)).astype(own.dtype)
     onward = remote(own.at[0], passed, send.at[2], arrive.at[2], (across, seq))
     onward.start()
-    yield
+    for _ in range(1 + pause):
+        yield
     loads[1].wait()
     copies[1].wait_recv()
     onward.wait_recv()
@@ -987,7 +988,7 @@
         compiler_params=pltpu.CompilerParams(
             collective_id=number, has_side_effects=True, vmem_limit_bytes=VMEM_BYTES
         ),
-        cost_estimate=pl.CostEstimate(flops=0, bytes_accessed=moved, transcendentals=0),
+        cost_estimate=pl.CostEstimate(flops=0, bytes_accessed=moved // 8, transcendentals=0),
     )
 
 
@@ -1013,6 +1014,43 @@
     return out.reshape(count * rows, width)
 
 
+def gathered_sided(value, half, number, pieces=4, half_pieces=2):
+    count = lax.axis_size("head")
+    rows, width = value.shape
+
+    def body(own_ref, half_ref, out_ref, beside_ref, landing, *sems):
+        head, line, side = seq_places()
+        beside = (head, line * SIDE + 1 - side)
+        greet(head_partners() + [(beside, None)])
+
+        def half_steps():
+            copy = remote(half_ref, landing, sems[6].at[0], sems[6].at[1], beside)
+            copy.start()
+            yield
+            yield
+            copy.wait()
+            yield from gather_head(landing, beside_ref, *sems[3:6], half_pieces)
+
+        run_together([half_steps(), gather_head(own_ref, out_ref, *sems[:3], pieces)])
+
+    out, beside = link_call(
+        body,
+        number,
+        [ANY, ANY],
+        [ANY, ANY],
+        [
+            shaped((count, rows, width), value.dtype),
+            shaped((count, rows, half.shape[1]), value.dtype),
+        ],
+        [pltpu.VMEM(half.shape, half.dtype)]
+        + [DMA((1,)), DMA((3, pieces)), DMA((3, pieces))]
+        + [DMA((1,)), DMA((3, half_pieces)), DMA((3, half_pieces))]
+        + [DMA((2,))],
+        60_000_000,
+    )(value, half)
+    return out.reshape(count * rows, width), beside.reshape(count * rows, half.shape[1])
+
+
 def gathered_seq(value, number):
     total = lax.axis_size("seq")
     count = total // SIDE
@@ -1145,10 +1183,12 @@
             yield from gather_head(small_ref, four, sems[0], sems[1], sems[2], 1)
             own[...] = four[lax.axis_index("head")]
             own[:gain_rows] = jnp.sum(four[:, :gain_rows], axis=0)
-            yield from gather_seq(own, small_out, local, *sems[3:7], count)
+            for step in gather_seq(own, small_out, local, *sems[3:7], count):
+                for _ in range(3):
+                    yield
 
         steps = [
-            scatter_seq(qkv_at, lambda piece: qkv_out.at[:, pl.ds(piece * width, width)], *rest[:7], count),
+            small_steps(*rest[19:29]),
             scatter_seq(
                 gate_at,
                 lambda piece: gate_out.at[:, pl.ds(piece * gate_width, gate_width)],
@@ -1157,8 +1197,13 @@
                 *rest[8:13],
                 count,
             ),
-            scatter_head(normed_at, normed_out, *rest[13:19]),
-            small_steps(*rest[19:29]),
+            scatter_seq(
+                qkv_at,
+                lambda piece: qkv_out.at[:, pl.ds(piece * width, width)],
+                *rest[:7],
+                count,
+            ),
+            scatter_head(normed_at, normed_out, *rest[13:19], 2),
         ]
         for index, (ref, out) in enumerate(zip(mlp_refs, mlp_outs)):
 
@@ -1166,7 +1211,9 @@
                 return ref.at[:, pl.ds(pl.multiple_of(target * slices, slices), slices)]
 
             begin = 29 + 6 * index
-            steps.append(scatter_head(mlp_at, out, *rest[begin : begin + 6]))
+            steps.append(
+                scatter_head(mlp_at, out, *rest[begin : begin + 6], 5 + 3 * index)
+            )
         run_together(steps)
 
     line_scratch = seq_scratch(gate_pieces, count, rows, gate_width)
@@ -1261,6 +1308,7 @@
     out_flat = out_weight.reshape(heads * DV, width)
     columns, run_rows = token_columns(decay_code, beta_code, total_len)
 
+    cot_all = gathered(out_cot, "seq")
     seq_count, head_count = lax.axis_size("seq"), lax.axis_size("head")
     seq_at, head_at = lax.axis_index("seq"), lax.axis_index("head")
     side = lax.rem(seq_at, SIDE)
@@ -1268,12 +1316,12 @@
     scale_own = rms_scale(input_f)
     hat_own = input_f * scale_own
     normed_own = (hat_own * gain_first).astype(bf16)
-    normed_first = gathered(normed_own, "head")
-    normed_side = gathered(swapped(side_columns(normed_own, 1 - side, slice_rows)), "head")
+    normed_first, normed_side = gathered_sided(
+        normed_own, side_columns(normed_own, 1 - side, slice_rows), 1
+    )
     mixed_in = mm(normed_first, qkv_flat).astype(bf16)
     tail_in = passed_along(mixed_in[span_rows - 8 :], "seq", 1)
     tail_in = jnp.where(jnp.arange(8)[:, None] >= 8 - lead_rows, tail_in.astype(f32), 0.0)
-    cot_all = gathered(out_cot, "seq")
     solve, score, fresh, reach, inner_part, turn, local_states, piece_end = run_local_forward(
         mixed_in, tail_in, taps, columns, run_rows, heads
     )
@@ -1282,11 +1330,11 @@
     states, core, branch = run_finish_forward(
         ends, local_states, reach, inner_part, gate_pre, gain_head
     )
+    branch, cot_all = lax.optimization_barrier((branch, cot_all))
     middle = input_f + scattered_head(mm(branch, out_flat).astype(bf16), 3)
     scale_two = rms_scale(middle)
     hat_two = middle * scale_two
     normed_two = (hat_two * gain_second).astype(bf16)
-    normed_two, cot_all = lax.optimization_barrier((normed_two, cot_all))
 
     rows_out = gathered_seq(normed_two, 4).reshape(-1, width)
     gate_part = mm(rows_out, mlp_gate)

time: 703 us -> 659 us (0.937)
  Pallas kernels: 498 us -> 462 us
    pallas_call x1, Pallas kernels: 163 us -> 134 us  [scattered_last(): link_call(body, number, [ANY] * (4 + len(mlp)), [IN_VMEM] * (4 + len(mlp)...]
    pallas_call x3, Pallas kernels: 173 us -> 148 us  [gathered_seq(): link_call(body, number, [ANY], ANY, shaped((total, rows, width), value.dt...]
    pallas_call x0 -> x1, Pallas kernels: none -> 23.9 us  [gathered_sided(): link_call(body, number, [ANY, ANY], [ANY, ANY], [shaped((count, rows, wid...]
    unnamed x94 -> x96, local copies, waits for them, and re-layouts: 18.8 us -> 16 us
  transfers between devices with their start and end apart: 9 -> 6, of which waited for: 1 -> 0; matrix products, arithmetic and copies ran while one was open for 23% -> 18% of each run, Pallas kernels for 72% -> 50%
where the time goes in v4:
time: 659 us; the launch traced here: 651 us
  Pallas kernels  462 us (70%)
  matrix products  109 us (17%)
  local copies, waits for them, and re-layouts  32.3 us (5%)
  other arithmetic  24.8 us (4%)
  between operations  14.6 us (2%)
  starting transfers between devices  7.73 us (1%)
    pallas_call x3, Pallas kernels, gathered_seq(): link_call(body, number, [ANY], ANY, shaped((total, rows, width), value.dt...  148 us
    pallas_call x1, Pallas kernels, scattered_last(): link_call(body, number, [ANY] * (4 + len(mlp)), [IN_VMEM] * (4 + len(mlp)...  134 us
    pallas_call x1, Pallas kernels, scattered_seq(): link_call(body, number, [ANY], IN_VMEM, shaped((rows, value.shape[1]), f3...  50.1 us
    dot_general x6, matrix products, mm_nt(): lax.dot_general(left, right, (((1,), (1,)), ((), ())), preferred_element_...  39.7 us
    dot_general x7, matrix products, mm_tn(): lax.dot_general(left, right, (((0,), (0,)), ((), ())), preferred_element_...  37.7 us
    dot_general x6, matrix products, mm(): return jnp.dot(left, right, preferred_element_type=f32)  31.6 us
    pallas_call x1, Pallas kernels, run_finish_backward(): kernel_call(finish_backward, heads, [whole(ends.shape), whole(grad_ends.s...  27.2 us
    pallas_call x1, Pallas kernels, gathered_sided(): link_call(body, number, [ANY, ANY], [ANY, ANY], [shaped((count, rows, wid...  23.9 us
  transfers between devices with their start and end apart: 6, of which 0 were waited for; matrix products, arithmetic and copies ran while one was open for 18% of the time, Pallas kernels for 50%

profile of v4, /device:TPU:0, one launch (start us, length us, event | category | flops | bytes accessed | tf_op | source)
XLA Modules:
  0.0 651.2 jit_solution(17216959834633845638)
XLA Ops:
  7.2 0.7 all-gather.2.cloned.1.call-update
  8.0 0.8 convert_element_type.102
  8.7 1.2 fusion.10
  10.6 1.2 fusion.4.own_ref
  11.9 0.8 pad_maximum_fusion.half_ref
  12.7 23.9 %shard_map.229 = (bf16[4,128,2048]{2,1,0:T(8,128)(2,1)}, bf16[4,128,1024]{2,1,0:T(8,128)(2,1)}) custom-call(bf16[128,2048]{1,0:T(8,128)(2,1)} %copy-done.9, bf16[128,1024]{1,0:T(8,128)(2,1)} %pad_maximum_fusion.half_ref), custom_call_target="tpu_custom_call" | custom-call | bytes 7500000 | tf_op jit(solution)/shard_map/pallas_call | solution.py:1036
  36.6 10.4 %copy.31 = bf16[256,8,4,512]{3,1,2,0:T(8,128)(2,1)} copy(bf16[256,8,4,512]{3,2,1,0:T(4,128)(2,1)} %bitcast.77) | data formatting | bytes 16777216
  47.0 8.2 %convolution_convert_fusion.7.mixed_ref = bf16[512,2048]{1,0:T(8,128)(2,1)S(1)} fusion(bf16[512,2048]{1,0:T(8,128)(2,1)S(1)} %bitcast.95, bf16[2048,2048]{1,0:T(8,128)(2,1)} %bitcast.78), kind=kOutput, calls=%fused_computation.11 | convolution fusion | flops 4296015872 | bytes 12582912 | tf_op jit(solution)/shard_map/dot_general | solution.py:62
  55.2 3.6 collective-permute-start
  59.6 3.4 copy.33
  63.1 3.6 fusion.30.gate_ref
  67.5 0.7 pad.14.clone.columns_ref
  68.3 0.6 pad.15.run_rows_ref
  69.5 0.7 convert_select_fusion.tail_ref
  70.2 22.9 %shard_map.230 = (bf16[4,2,256,256]{3,2,1,0:T(8,128)(2,1)}, bf16[4,2,256,256]{3,2,1,0:T(8,128)(2,1)}, bf16[4,512,384]{2,1,0:T(8,128)(2,1)}, bf16[4,512,128]{2,1,...) custom-call(bf16[512,2048]{1,0:T(8,128)(2,1)} %copy-done.33, ...), custom_call_target="tpu_custom_call" | custom-call | flops 12000000000 | bytes 20000000 | tf_op jit(solution)/shard_map/pallas_call | solution.py:484
  93.1 41.3 %shard_map.231 = bf16[8,512,384]{2,1,0:T(8,128)(2,1)} custom-call(bf16[512,384]{1,0:T(8,128)(2,1)} %bitcast.98), custom_call_target="tpu_custom_call" | custom-call | bytes 15000000 | tf_op jit(solution)/shard_map/pallas_call | solution.py:1065
  134.4 10.4 %shard_map.232 = (bf16[4,8,128,256]{3,2,1,0:T(8,128)(2,1)}, f32[512,1024]{1,0:T(8,128)}, bf16[512,1024]{1,0:T(8,128)(2,1)}) custom-call(bf16[8,4,128,384]{3,2,1,0:T(8,128)(2,1)} %bitcast.87, bf16[4,8,128,384]{3,2,1,0:T(8,128)(2,1)} %get-tuple-element.59.local_ref, bf16[4,512,128]{2,1,0:T(8,128)(2,1)} %get-tuple-element.60.reach_ref, ...), custom_call_target="tpu_custom_call" | custom-call | flops 3000000000 | bytes 20000000 | tf_op jit(solution)/shard_map/pallas_call | solution.py:527
  144.8 6.2 convolution_convert_fusion.6.source
  151.0 16.9 %shard_map.233 = f32[128,2048]{1,0:T(8,128)} custom-call(bf16[512,2048]{1,0:T(8,128)(2,1)} %convolution_convert_fusion.6.source), custom_call_target="tpu_custom_call" | custom-call | bytes 7500000 | tf_op jit(solution)/shard_map/pallas_call | solution.py:1115
  167.9 1.4 multiply_reduce_fusion.3
  169.4 1.0 multiply_convert_fusion.3.own_ref
  170.3 51.9 %shard_map.234 = bf16[8,128,2048]{2,1,0:T(8,128)(2,1)} custom-call(bf16[128,2048]{1,0:T(8,128)(2,1)} %multiply_convert_fusion.3.own_ref), custom_call_target="tpu_custom_call" | custom-call | bytes 15000000 | tf_op jit(solution)/shard_map/pallas_call | solution.py:1065
  222.3 5.3 fusion.31
  227.6 3.2 fusion.32
  230.8 5.3 multiply_convert_fusion
  236.1 3.5 fusion.33
  239.7 5.2 add_convert_fusion.source
  244.9 50.1 %shard_map.235 = f32[128,2048]{1,0:T(8,128)} custom-call(bf16[1024,2048]{1,0:T(8,128)(2,1)} %add_convert_fusion.source), custom_call_target="tpu_custom_call" | custom-call | bytes 15000000 | tf_op jit(solution)/shard_map/pallas_call | solution.py:1145
  295.1 1.6 multiply_reduce_fusion.1
  296.7 2.4 fusion.27.own_ref
  299.1 18.1 %shard_map.236 = bf16[4,128,2048]{2,1,0:T(8,128)(2,1)} custom-call(bf16[128,2048]{1,0:T(8,128)(2,1)} %fusion.27.own_ref), custom_call_target="tpu_custom_call" | custom-call | bytes 7500000 | tf_op jit(solution)/shard_map/pallas_call | solution.py:1005
  317.2 6.0 convolution_convert_fusion.1
  323.3 2.2 constant_dynamic-slice_fusion.4
  325.5 6.5 fusion.34.d_branch_ref
  332.0 10.4 %shard_map.237 = (bf16[512,1024]{1,0:T(8,128)(2,1)}, bf16[512,1024]{1,0:T(8,128)(2,1)}, f32[1,256]{1,0:T(1,128)}, bf16[4,8,128,384]{3,2,1,0:T(8,128)(2,1)}, bf16[4,128,256]{2,1,0:T(8,128)(2,1)}) custom-call(f32[512,1024]{1,0:T(8,128)} %fusion.34.d_branch_ref, f32[512,1024]{1,0:T(8,128)} %get-tuple-element.67.core_ref, f32[512,1024]{1,0:T(8,128)} %fusion.30.gate_ref, ...), custom_call_target="tpu_custom_call" | custom-call | flops 4000000000 | bytes 20000000 | tf_op jit(solution)/shard_map/pallas_call | solution.py:553
  342.4 54.9 %shard_map.238 = bf16[8,512,256]{2,1,0:T(8,128)(2,1)} custom-call(bf16[512,256]{1,0:T(8,128)(2,1)} %bitcast.99), custom_call_target="tpu_custom_call" | custom-call | bytes 15000000 | tf_op jit(solution)/shard_map/pallas_call | solution.py:1065
  397.3 27.2 %shard_map.239 = (bf16[512,2048]{1,0:T(8,128)(2,1)}, f32[8,2048]{1,0:T(8,128)}, f32[8,2048]{1,0:T(8,128)}, f32[4,2048]{1,0:T(4,128)}) custom-call(bf16[8,4,128,384]{3,2,1,0:T(8,128)(2,1)} %bitcast.88, bf16[8,4,128,256]{3,2,1,0:T(8,128)(2,1)} %bitcast.91, bf16[512,2048]{1,0:T(8,128)(2,1)} %copy-done.33, f32[8,2048]{1,0:T(8,128)} %convert_select_fusion.tail_ref, ...), custom_call_target="tpu_custom_call" | custom-call | flops 12000000000 | bytes 20000000 | tf_op jit(solution)/shard_map/pallas_call | solution.py:591
  424.5 1.5 slice.37
  425.9 1.3 collective-permute-start.1
  427.2 2.7 collective-permute-start.2
  429.9 5.1 convolution_convert_fusion.2
  435.0 7.3 %convolution_convert_fusion.5.rest_0_ = bf16[704,2048]{1,0:T(8,128)(2,1)} fusion(bf16[1024,704]{0,1:T(8,128)(2,1)} %copy-done.41, bf16[1024,2048]{1,0:T(8,128)(2,1)} %bitcast.81), kind=kOutput, calls=%fused_computation.8 | convolution fusion | flops 2954231808 | bytes 8519680 | tf_op jit(solution)/shard_map/dot_general | solution.py:70
  442.4 7.0 %fusion.35 = f32[512,2048]{1,0:T(8,128)} fusion(bf16[512,1024]{1,0:T(8,128)(2,1)} %get-tuple-element.79, bf16[2048,1024]{1,0:T(8,128)(2,1)} %bitcast.86), kind=kOutput, calls=%fused_computation.93 | convolution fusion | flops 2147483648 | bytes 9437184 | tf_op jit(solution)/shard_map/dot_general | solution.py:66
  449.4 4.5 convolution_convert_fusion.4.rest_1_
  453.9 4.5 convolution_convert_fusion.3.rest_2_
  458.5 4.6 fusion.11
  463.1 1.4 reshape.180
  464.5 0.6 copy-done.24
  465.1 0.8 slice_add_fusion
  465.9 0.7 scatter-add.4
  466.6 0.6 convert_dynamic-update-slice_fusion
  467.2 12.2 %multiply_reduce_fusion = (f32[2048]{0:T(1024)S(1)}, bf16[512,2048]{1,0:T(8,128)(2,1)}) fusion(bf16[4,128,2048]{2,1,0:T(8,128)(2,1)} %get-tuple-element.57, f32[512,2048]{1,0:T(8,128)} %fusion.35, bf16[512,2048]{1,0:T(8,128)(2,1)} %convert_dynamic-update-slice_fusion, bf16[2048,2048]{1,0:T(8,128)(2,1)} %bitcast.79), kind=kOutput, calls=%fused_computation.2 | convolution fusion | flops 4300208128 | bytes 18882560 | tf_op jit(solution)/shard_map/dot_general | solution.py:66
  479.5 0.6 pad_maximum_fusion.1.small_ref
  480.1 6.9 %convolution_convert_fusion.qkv_ref = bf16[2048,2048]{1,0:T(8,128)(2,1)} fusion(bf16[512,2048]{1,0:T(8,128)(2,1)S(1)} %bitcast.97, bf16[512,2048]{1,0:T(8,128)(2,1)S(1)} %copy-done.38), kind=kOutput, calls=%fused_computation.1 | convolution fusion | flops 4299161600 | bytes 12582912 | tf_op jit(solution)/shard_map/dot_general | solution.py:70
  487.0 3.8 add_convert_fusion.1.gate_ref
  490.9 133.9 %shard_map.240 = (bf16[256,2048]{1,0:T(8,128)(2,1)}, bf16[256,1024]{1,0:T(8,128)(2,1)}, f32[128,2048]{1,0:T(8,128)}, f32[8,104,128]{2,1,0:T(8,128)}, bf16[704,51...) custom-call(bf16[2048,2048]{1,0:T(8,128)(2,1)} %convolution_convert_fusion.qkv_ref, ...), custom_call_target="tpu_custom_call" | custom-call | bytes 31250000 | tf_op jit(solution)/shard_map/pallas_call | solution.py:1220
  624.8 1.0 reduce_sum.69
  625.9 3.7 reshape.190
  629.6 2.5 reshape.192
  632.1 2.6 convert_element_type.130
  635.8 0.7 constant_dynamic-slice_fusion
  636.8 2.0 convert_bitcast_fusion
  638.8 2.1 convert.5
  640.9 3.6 fusion.9
  (130 shorter events, 4.6 us)
Async XLA Ops:
  7.2 223.6 %copy-start = (bf16[704,2048]{1,0:T(8,128)(2,1)S(1)}, bf16[704,2048]{1,0:T(8,128)(2,1)}, u32[]{:S(2)}) copy-start(bf16[704,2048]{1,0:T(8,128)(2,1)} %param.27) | copy-start | bytes 8650756
  7.2 137.6 %all-gather.2.cloned.1.call-start = ((), (), s32[]{:S(2)}) async-start(), calls=%async_computation.2 | async-start | bytes 4718592 | tf_op jit(solution)/shard_map/all_gather | solution.py:1272
  7.9 630.9 %reduce-scatter.5.cloned.1.call-start = ((), (), s32[]{:S(2)}) async-start(), calls=%async_computation.4 | async-start | bytes 4718592 | tf_op jit(solution)/shard_map/reduce_scatter | solution.py:1276
  8.7 38.3 %copy-start.21 = (f32[2048]{0:T(1024)}, f32[2048]{0:T(1024)S(1)}, u32[]{:S(2)}) copy-start(f32[2048]{0:T(1024)S(1)} %convert_element_type.102) | copy-start | bytes 24580
  10.0 0.6 copy-start.29
  11.8 0.9 copy-start.9
  36.6 10.5 %copy-start.13 = (bf16[4,128,2048]{2,1,0:T(8,128)(2,1)S(1)}, bf16[4,128,2048]{2,1,0:T(8,128)(2,1)}, u32[]{:S(2)}) copy-start(bf16[4,128,2048]{2,1,0:T(8,128)(2,1)} %get-tuple-element.57) | copy-start | bytes 6291460
  47.0 11.9 %copy-start.27 = (s32[512,4]{0,1:T(4,128)S(1)}, s32[512,4]{0,1:T(4,128)}, u32[]{:S(2)}) copy-start(s32[512,4]{0,1:T(4,128)} %param.28) | copy-start | bytes 24580
  55.2 3.7 copy-start.33
  55.2 14.2 %collective-permute-start = (bf16[8,2048]{1,0:T(8,128)(2,1)S(1)}, bf16[8,2048]{1,0:T(8,128)(2,1)S(1)}, u32[]{:S(2)}, u32[]{:S(2)}) collective-permute-start(bf16[8,2048]{1,0:T(8,128)(2,1)S(1)} %slice.40), channel_id=1, source_target_pairs={{0,1},{1,2},{2,3},{3,4},{4,5},{5,6},{6,7},{8,9},{9,10},{10,11},{11... | collective-permute-start | bytes 98312 | tf_op jit(solution)/shard_map/ppermute | solution.py:27
  59.6 3.4 copy-start.28
  59.6 3.5 copy-start.14
  63.0 3.7 copy-start.6
  63.0 3.7 copy-start.26
  63.1 5.8 copy-start.39
  63.1 6.4 copy-start.31
  151.0 16.9 %copy-start.2 = (bf16[128,2048]{1,0:T(8,128)(2,1)S(1)}, bf16[128,2048]{1,0:T(8,128)(2,1)}, u32[]{:S(2)}) copy-start(bf16[128,2048]{1,0:T(8,128)(2,1)} %param.16) | copy-start | bytes 1572868
  169.3 127.3 %copy-start.1 = (f32[128,2048]{1,0:T(8,128)}, f32[128,2048]{1,0:T(8,128)S(1)}, u32[]{:S(2)}) copy-start(f32[128,2048]{1,0:T(8,128)S(1)} %get-tuple-element.93) | copy-start | bytes 3145732
  169.4 52.9 %copy-start.36 = (bf16[2048,704]{0,1:T(8,128)(2,1)S(1)}, bf16[2048,704]{0,1:T(8,128)(2,1)}, u32[]{:S(2)}) copy-start(bf16[2048,704]{0,1:T(8,128)(2,1)} %param.25) | copy-start | bytes 8650756
  222.3 5.3 copy-start.4
  222.3 5.3 copy-start.37
  227.6 3.2 copy-start.34
  236.1 3.6 copy-start.41
  236.1 3.6 copy-start.42
  244.9 51.7 %copy-start.3 = (bf16[128,2048]{1,0:T(8,128)(2,1)S(1)}, bf16[128,2048]{1,0:T(8,128)(2,1)}, u32[]{:S(2)}) copy-start(bf16[128,2048]{1,0:T(8,128)(2,1)} %param.17) | copy-start | bytes 1572868
  296.7 20.5 %copy-start.40 = (bf16[512,1024]{1,0:T(8,128)(2,1)S(1)}, bf16[512,1024]{1,0:T(8,128)(2,1)}, u32[]{:S(2)}) copy-start(bf16[512,1024]{1,0:T(8,128)(2,1)} %get-tuple-element.63) | copy-start | bytes 3145732
  323.2 317.7 %reduce-scatter.3.cloned.1.call-start = ((), (), s32[]{:S(2)}) async-start(), calls=%async_computation.3 | async-start | bytes 4718592 | tf_op jit(solution)/shard_map/reduce_scatter | solution.py:1276
  397.3 32.7 %copy-start.44 = (bf16[1024,704]{0,1:T(8,128)(2,1)S(1)}, bf16[1024,704]{0,1:T(8,128)(2,1)}, u32[]{:S(2)}) copy-start(bf16[1024,704]{0,1:T(8,128)(2,1)} %get-tuple-element.65) | copy-start | bytes 4325380
  425.9 38.6 %collective-permute-start.1 = (f32[3,2048]{1,0:T(4,128)}, f32[3,2048]{1,0:T(4,128)S(1)}, u32[]{:S(2)}, u32[]{:S(2)}) collective-permute-start(f32[3,2048]{1,0:T(4,128)} %slice.37), channel_id=1, source_target_pairs={{1,0},{2,1},{3,2},{4,3},{5,4},{6,5},{7,6},{9,8},{10,9},{11,10},{12... | collective-permute-start | bytes 73736 | tf_op jit(solution)/shard_map/ppermute | solution.py:27
  427.2 59.8 %collective-permute-start.2 = (bf16[512,1024]{1,0:T(8,128)(2,1)}, bf16[512,1024]{1,0:T(8,128)(2,1)}, u32[]{:S(2)}, u32[]{:S(2)}) collective-permute-start(bf16[512,1024]{1,0:T(8,128)(2,1)} %get-tuple-element.79), channel_id=1, source_target_pairs={{0,1},{1,0},{2,3},{3,2},{4,5},{5,4},{6,7},{7,6},{8,9},{9,8},{10,11... | collective-permute-start | bytes 3145736 | tf_op jit(solution)/shard_map/ppermute | solution.py:1263
  442.4 7.0 %copy-start.5 = (bf16[8,128,2048]{2,1,0:T(8,128)(2,1)S(1)}, bf16[8,128,2048]{2,1,0:T(8,128)(2,1)}, u32[]{:S(2)}) copy-start(bf16[8,128,2048]{2,1,0:T(8,128)(2,1)} %shard_map.234) | copy-start | bytes 12582916
  442.4 7.0 %copy-start.43 = (bf16[1024,704]{0,1:T(8,128)(2,1)S(1)}, bf16[1024,704]{0,1:T(8,128)(2,1)}, u32[]{:S(2)}) copy-start(bf16[1024,704]{0,1:T(8,128)(2,1)} %copy-done.42) | copy-start | bytes 4325380
  449.4 4.5 copy-start.35
  449.4 4.5 copy-start.45
  453.9 4.6 copy-start.16
  453.9 4.6 copy-start.17
  453.9 4.6 copy-start.18
  453.9 4.6 copy-start.19
  458.5 6.6 %copy-start.20 = (f32[8,2048]{1,0:T(8,128)S(1)}, f32[8,2048]{1,0:T(8,128)}, u32[]{:S(2)}) copy-start(f32[8,2048]{1,0:T(8,128)} %get-tuple-element.77) | copy-start | bytes 196612
  464.5 0.6 copy-start.24
  467.2 12.2 %copy-start.25 = (bf16[2048]{0:T(1024)(128)(2,1)S(1)}, bf16[2048]{0:T(1024)(128)(2,1)}, u32[]{:S(2)}) copy-start(bf16[2048]{0:T(1024)(128)(2,1)} %param.18) | copy-start | bytes 12292
  467.2 12.2 %copy-start.32 = (f32[1,256]{1,0:T(1,128)S(1)}, f32[1,256]{1,0:T(1,128)}, u32[]{:S(2)}) copy-start(f32[1,256]{1,0:T(1,128)} %get-tuple-element.81) | copy-start | bytes 3076
  467.2 12.2 %copy-start.23 = (f32[64,128]{1,0:T(8,128)S(1)}, f32[64,128]{1,0:T(8,128)}, u32[]{:S(2)}) copy-start(f32[64,128]{1,0:T(8,128)} %reshape.180) | copy-start | bytes 98308
  467.2 12.9 %copy-start.15 = (bf16[4,128,2048]{2,1,0:T(8,128)(2,1)S(1)}, bf16[4,128,2048]{2,1,0:T(8,128)(2,1)}, u32[]{:S(2)}) copy-start(bf16[4,128,2048]{2,1,0:T(8,128)(2,1)} %get-tuple-element.57) | copy-start | bytes 6291460
  467.2 12.9 %copy-start.38 = (bf16[512,2048]{1,0:T(8,128)(2,1)S(1)}, bf16[512,2048]{1,0:T(8,128)(2,1)}, u32[]{:S(2)}) copy-start(bf16[512,2048]{1,0:T(8,128)(2,1)} %convert_dynamic-update-slice_fusion) | copy-start | bytes 6291460
  480.1 6.9 %copy-start.7 = (f32[1024,1024]{1,0:T(8,128)S(1)}, f32[1024,1024]{1,0:T(8,128)}, u32[]{:S(2)}) copy-start(f32[1024,1024]{1,0:T(8,128)} %fusion.11) | copy-start | bytes 12582916
  480.1 6.9 %copy-start.10 = (bf16[4,128,1024]{2,1,0:T(8,128)(2,1)S(1)}, bf16[4,128,1024]{2,1,0:T(8,128)(2,1)}, u32[]{:S(2)}) copy-start(bf16[4,128,1024]{2,1,0:T(8,128)(2,1)} %get-tuple-element.80) | copy-start | bytes 3145732
  625.9 10.6 %copy-start.22 = (f32[2048]{0:T(1024)S(1)}, f32[2048]{0:T(1024)}, u32[]{:S(2)}) copy-start(f32[2048]{0:T(1024)} %copy-done.21) | copy-start | bytes 24580
  625.9 10.6 %copy-start.30 = (f32[128]{0:T(128)S(1)}, f32[128]{0:T(128)}, u32[]{:S(2)}) copy-start(f32[128]{0:T(128)} %copy-done.29) | copy-start | bytes 1540
  632.1 4.4 copy-start.8
  632.1 4.7 copy-start.11
  632.1 4.7 copy-start.12
Sparse Core Ops, SparseCore 0:
  10.2 76.7 all-gather.1
  323.4 105.3 reduce-scatter.4
  442.5 107.1 reduce-scatter.2

commit v5 on v4

--- a/solution.py
+++ b/solution.py
@@ -478,15 +478,15 @@
 
 
 def run_local_forward(mixed, tail, taps, columns, run_rows, heads):
-    rows = mixed.shape[0]
+    rows = mixed.shape[1]
     count = taps.shape[0]
     groups, stretches = rows // GROUP, rows // STRETCH
     return kernel_call(
         local_forward,
         heads,
         [
-            by_columns(rows, INNER),
-            by_columns(8, INNER),
+            by_head((rows, INNER)),
+            by_head((8, INNER)),
             by_columns(count, INNER),
             whole(columns.shape),
             whole(run_rows.shape),
@@ -532,7 +532,7 @@
             by_head((stretches, DK, DV + DK)),
             by_head((rows, DK)),
             by_columns(rows, DV),
-            by_columns(rows, DV),
+            by_head((rows, DV)),
             whole(gain.shape),
         ],
         [by_head((stretches, DK, DV)), by_columns(rows, DV), by_columns(rows, DV)],
@@ -556,7 +556,7 @@
         [
             by_columns(rows, DV),
             by_columns(rows, DV),
-            by_columns(rows, DV),
+            by_head((rows, DV)),
             whole(gain.shape),
             by_head((rows, DK)),
             whole(turn.shape),
@@ -585,7 +585,7 @@
     ends, grad_ends, mixed, tail, taps, columns, run_rows, solve, score, fresh, states, d_core, local
 ):
     heads, stretches = local.shape[:2]
-    rows = mixed.shape[0]
+    rows = mixed.shape[1]
     groups = rows // GROUP
     count = taps.shape[0]
     return kernel_call(
@@ -594,8 +594,8 @@
         [
             whole(ends.shape),
             whole(grad_ends.shape),
-            by_columns(rows, INNER),
-            by_columns(8, INNER),
+            by_head((rows, INNER)),
+            by_head((8, INNER)),
             by_columns(count, INNER),
             whole(columns.shape),
             whole(run_rows.shape),
@@ -1153,7 +1153,135 @@
     )(value)
 
 
-def scattered_last(qkv, gate, normed, mlp, small, gain_rows, number, pieces=4, gate_pieces=2):
+def product_steps(left_hbm, right_hbm, out_refs, picks, lefts, rights, tiles, load, store, per_round):
+    loads = [
+        pltpu.make_async_copy(ref, held, load.at[index])
+        for index, (ref, held) in enumerate(zip(left_hbm + right_hbm, lefts + rights))
+    ]
+    for copy in loads:
+        copy.start()
+    yield
+    for copy in loads:
+        copy.wait()
+    units, width = tiles.shape[1:]
+    block = units // 4 if units % 64 == 0 else units
+    span = 512
+    stores = []
+    done = 0
+    for index, pick in enumerate(picks):
+        for begin in range(0, width, span):
+            columns = pl.ds(begin, span)
+
+            def one(part, carry, index=index, pick=pick, columns=columns):
+                rows = pl.ds(pl.multiple_of(part * block, block), block)
+                tiles[index, rows, columns] = mm(
+                    lefts[index][rows, :], rights[pick][:, columns]
+                ).astype(tiles.dtype)
+                return carry
+
+            lax.fori_loop(0, units // block, one, 0)
+            done += 1
+            if done % per_round == 0:
+                yield
+        copy = pltpu.make_async_copy(tiles.at[index], out_refs[index], store.at[index])
+        copy.start()
+        stores.append(copy)
+    for copy in stores:
+        copy.wait()
+
+
+def scattered_seq_products(value, lefts, rights, picks, number, pieces=2):
+    total = lax.axis_size("seq")
+    count = total // SIDE
+    rows, width = value.shape[0] // total, value.shape[1] // pieces
+    units, depth = lefts[0].shape
+    breadth = rights[0].shape[1]
+    n_left, n_right = len(lefts), len(rights)
+    held = 4 * value.size // SIDE + n_left * units * (depth + breadth) + n_right * rights[0].size
+    if 2 * held > VMEM_BYTES:
+        products = [mm(left, rights[pick]).astype(bf16) for left, pick in zip(lefts, picks)]
+        return scattered_seq(value, number, pieces), products
+
+    def body(source, *rest):
+        left_hbm, rest = rest[:n_left], rest[n_left:]
+        right_hbm, rest = rest[:n_right], rest[n_right:]
+        out, out_refs, rest = rest[0], rest[1 : 1 + n_left], rest[1 + n_left :]
+        link, rest = rest[:7], rest[7:]
+        left_held, rest = rest[:n_left], rest[n_left:]
+        right_held, rest = rest[:n_right], rest[n_right:]
+        greet(seq_partners(count))
+
+        def source_at(target, side, piece):
+            begin = pl.multiple_of((target * SIDE + side) * rows, rows)
+            return source.at[pl.ds(begin, rows), pl.ds(piece * width, width)]
+
+        def out_at(piece):
+            return out.at[:, pl.ds(piece * width, width)]
+
+        run_together(
+            [
+                scatter_seq(source_at, out_at, *link, count),
+                product_steps(
+                    left_hbm, right_hbm, out_refs, picks, left_held, right_held, *rest, 2
+                ),
+            ]
+        )
+
+    outs = link_call(
+        body,
+        number,
+        [ANY] * (1 + n_left + n_right),
+        [IN_VMEM] + [ANY] * n_left,
+        [shaped((rows, value.shape[1]), f32)]
+        + [shaped((units, breadth), bf16) for _ in lefts],
+        seq_scratch(pieces, count, rows, width)
+        + [pltpu.VMEM((units, depth), bf16) for _ in lefts]
+        + [pltpu.VMEM((depth, breadth), bf16) for _ in rights]
+        + [
+            pltpu.VMEM((n_left, units, breadth), bf16),
+            DMA((n_left + n_right,)),
+            DMA((n_left,)),
+        ],
+        120_000_000,
+    )(value, *lefts, *rights)
+    return outs[0], list(outs[1:])
+
+
+def gathered_swapped(ends, d_gate, number):
+    total = lax.axis_size("seq")
+    count = total // SIDE
+
+    def body(ends_ref, gate_ref, ends_out, gate_out, *rest):
+        head, line, side = seq_places()
+        beside = (head, line * SIDE + 1 - side)
+        greet(seq_partners(count))
+
+        def swap_steps():
+            yield
+            yield
+            copy = remote(gate_ref, gate_out, rest[5].at[0], rest[5].at[1], beside)
+            copy.start()
+            for _ in range(count):
+                yield
+            copy.wait()
+
+        run_together([gather_seq(ends_ref, ends_out, *rest[:5], count), swap_steps()])
+
+    return link_call(
+        body,
+        number,
+        [ANY] * 2,
+        [ANY] * 2,
+        [
+            shaped((total,) + ends.shape, ends.dtype),
+            shaped(d_gate.shape, d_gate.dtype),
+        ],
+        [DMA((1,))] + [DMA((2 * count,)) for _ in range(4)] + [DMA((2,))],
+        150_000_000,
+    )(ends, d_gate)
+
+
+def scattered_last(qkv, gate, normed, hat, mlp, small, gain_rows, number, pieces=4, gate_pieces=2):
     total, heads = lax.axis_size("seq"), lax.axis_size("head")
     count = total // SIDE
     rows, width = qkv.shape[0] // total, qkv.shape[1] // pieces
@@ -1162,7 +1290,7 @@
     units, slices = mlp[0].shape[0], mlp[0].shape[1] // heads
     small_rows = small.shape[0]
 
-    def body(qkv_ref, gate_ref, normed_ref, small_ref, *rest):
+    def body(qkv_ref, gate_ref, normed_ref, hat_ref, small_ref, *rest):
         mlp_refs, rest = rest[: len(mlp)], rest[len(mlp) :]
         qkv_out, gate_out, normed_out, small_out, rest = rest[0], rest[1], rest[2], rest[3], rest[4:]
         mlp_outs, rest = rest[: len(mlp)], rest[len(mlp) :]
@@ -1179,16 +1307,21 @@
         def normed_at(target):
             return normed_ref.at[pl.ds(pl.multiple_of(target * own_rows, own_rows), own_rows)]
 
-        def small_steps(four, own, local, *sems):
-            yield from gather_head(small_ref, four, sems[0], sems[1], sems[2], 1)
-            own[...] = four[lax.axis_index("head")]
+        def normed_steps(four, own, local, *sems):
+            yield from scatter_head(normed_at, normed_out, *rest[13:19], 1)
+            own[...] = small_ref[...]
+            product = jnp.sum(normed_out[...] * hat_ref[...], axis=0, keepdims=True)
+            for row in range(product.shape[1] // 128):
+                own[row : row + 1] = product[:, row * 128 : (row + 1) * 128]
+            yield
+            yield from gather_head(own, four, sems[0], sems[1], sems[2], 1)
             own[:gain_rows] = jnp.sum(four[:, :gain_rows], axis=0)
             for step in gather_seq(own, small_out, local, *sems[3:7], count):
                 for _ in range(3):
                     yield
 
         steps = [
-            small_steps(*rest[19:29]),
+            normed_steps(*rest[19:29]),
             scatter_seq(
                 gate_at,
                 lambda piece: gate_out.at[:, pl.ds(piece * gate_width, gate_width)],
@@ -1203,7 +1336,6 @@
                 *rest[:7],
                 count,
             ),
-            scatter_head(normed_at, normed_out, *rest[13:19], 2),
         ]
         for index, (ref, out) in enumerate(zip(mlp_refs, mlp_outs)):
 
@@ -1220,7 +1352,7 @@
     outs = link_call(
         body,
         number,
-        [ANY] * (4 + len(mlp)),
+        [ANY] * 3 + [IN_VMEM] * 2 + [ANY] * len(mlp),
         [IN_VMEM] * (4 + len(mlp)),
         [
             shaped((rows, qkv.shape[1]), bf16),
@@ -1243,7 +1375,7 @@
         + [DMA((2 * count,)) for _ in range(4)]
         + head_scratch(units, slices) * len(mlp),
         250_000_000,
-    )(qkv, gate, normed, small, *mlp)
+    )(qkv, gate, normed, hat, small, *mlp)
     return outs[0], outs[1], outs[2], outs[3], list(outs[4:])
 
 
@@ -1303,8 +1435,6 @@
     gain_second = gain_two.astype(f32)
     gain_head = gain_out.reshape(1, -1)
     taps = conv_weight.reshape(conv_weight.shape[0], heads * inner)
-    qkv_flat = qkv_weight.reshape(width, heads * inner)
-    gate_flat = gate_weight.reshape(width, heads * DV)
     out_flat = out_weight.reshape(heads * DV, width)
     columns, run_rows = token_columns(decay_code, beta_code, total_len)
 
@@ -1319,50 +1449,72 @@
     normed_first, normed_side = gathered_sided(
         normed_own, side_columns(normed_own, 1 - side, slice_rows), 1
     )
-    mixed_in = mm(normed_first, qkv_flat).astype(bf16)
-    tail_in = passed_along(mixed_in[span_rows - 8 :], "seq", 1)
+    mixed_in = jnp.einsum(
+        "td,dhc->htc", normed_first, qkv_weight, preferred_element_type=f32
+    ).astype(bf16)
+    tail_in = passed_along(mixed_in[:, span_rows - 8 :], "seq", 1)
     tail_in = jnp.where(jnp.arange(8)[:, None] >= 8 - lead_rows, tail_in.astype(f32), 0.0)
     solve, score, fresh, reach, inner_part, turn, local_states, piece_end = run_local_forward(
         mixed_in, tail_in, taps, columns, run_rows, heads
     )
     ends = gathered_seq(piece_end.reshape(-1, DV + DK), 2).reshape(-1, heads, DK, DV + DK)
-    gate_pre = mm(normed_first, gate_flat)
+    gate_pre = jnp.einsum("td,dhv->htv", normed_first, gate_weight, preferred_element_type=f32)
     states, core, branch = run_finish_forward(
         ends, local_states, reach, inner_part, gate_pre, gain_head
     )
     branch, cot_all = lax.optimization_barrier((branch, cot_all))
+    branch_side = swapped(branch)
     middle = input_f + scattered_head(mm(branch, out_flat).astype(bf16), 3)
     scale_two = rms_scale(middle)
     hat_two = middle * scale_two
     normed_two = (hat_two * gain_second).astype(bf16)
 
     rows_out = gathered_seq(normed_two, 4).reshape(-1, width)
-    gate_part = mm(rows_out, mlp_gate)
-    up_part = mm(rows_out, mlp_up)
+    cot_f = out_cot.astype(f32)
+    gate_units, up_units = mlp_gate.T, mlp_up.T
+    gate_part = mm_nt(gate_units, rows_out)
+    up_part = mm_nt(up_units, rows_out)
+    d_hidden = mm_nt(mlp_down, cot_all)
     hidden = (jax.nn.silu(gate_part) * up_part).astype(bf16)
-    cot_f = out_cot.astype(f32)
-    d_hidden = mm_nt(cot_all, mlp_down)
     d_gate_mlp = (d_hidden * up_part * silu_slope(gate_part)).astype(bf16)
     d_up_mlp = (d_hidden * jax.nn.silu(gate_part)).astype(bf16)
-    d_rows = (mm_nt(d_gate_mlp, mlp_gate) + mm_nt(d_up_mlp, mlp_up)).astype(bf16)
-    d_normed_two = scattered_seq(d_rows, 5)
-    hidden, d_normed_two = lax.optimization_barrier((hidden, d_normed_two))
-    mlp_out = scattered(mm(hidden, mlp_down), "seq")
-    output = (middle + mlp_out).astype(bf16)
+    d_rows = (mm_tn(d_gate_mlp, gate_units) + mm_tn(d_up_mlp, up_units)).astype(bf16)
+    d_normed_two, (grad_mgate, grad_mup, grad_down) = scattered_seq_products(
+        d_rows, [d_gate_mlp, d_up_mlp, hidden], [rows_out, cot_all], [0, 0, 1], 5
+    )
     gain_two_part = jnp.sum(d_normed_two * hat_two, 0)
     e_two = d_normed_two * gain_second
     d_middle = cot_f + scale_two * (
         e_two - hat_two * jnp.mean(e_two * hat_two, axis=-1, keepdims=True)
     )
-    d_mix_all = gathered_head(d_middle.astype(bf16), 6)
+    hidden, d_middle = lax.optimization_barrier((hidden, d_middle))
+    mlp_part, d_middle = lax.optimization_barrier(
+        (mm_tn(hidden, mlp_down).astype(bf16), d_middle)
+    )
+    mlp_out = scattered(mlp_part, "seq")
+    d_mix = d_middle.astype(bf16)
+    d_mix_all, d_mix_side = gathered_sided(d_mix, side_columns(d_mix, 1 - side, slice_rows), 6)
     d_branch = mm_nt(d_mix_all, out_flat)
+    out_half = (
+        mm_tn(side_columns(d_mix_all, side, slice_rows), branch) + mm_tn(d_mix_side, branch_side)
+    ).astype(bf16)
     d_core, d_gate_low, gain_out_part, local_grads, grad_end = run_local_backward(
         d_branch, core, gate_pre, gain_head, reach, turn
     )
-    grad_ends = gathered_seq(grad_end.reshape(-1, DV), 7).reshape(-1, heads, DK, DV)
-    grad_out_w = mm_tn(branch, d_mix_all)
-    grad_out_s = scattered(grad_out_w, "seq", 1).reshape(heads, DV, -1)
-    d_gate_side = swapped(d_gate_low)
+    out_half, grad_end = lax.optimization_barrier((out_half, grad_end))
+    grad_out_s = lax.psum_scatter(
+        out_half,
+        "seq",
+        scatter_dimension=0,
+        axis_index_groups=[
+            [place * SIDE + across for place in range(seq_count // SIDE)] for across in range(SIDE)
+        ],
+        tiled=True,
+    )
+    grad_ends, d_gate_side = gathered_swapped(grad_end.reshape(-1, DV), d_gate_low, 7)
+    grad_ends = grad_ends.reshape(-1, heads, DK, DV)
+    mlp_out, grad_ends = lax.optimization_barrier((mlp_out, grad_ends))
+    output = (middle + mlp_out).astype(bf16)
     d_mixed, d_tail, d_lead, grad_conv = run_finish_backward(
         ends,
         grad_ends,
@@ -1381,18 +1533,24 @@
     from_next = passed_along(d_lead[:lead_rows], "seq", -1)
     d_tail = d_tail.at[8 - lead_rows :].add(from_next).astype(bf16)
     d_mixed = lax.dynamic_update_slice(d_mixed, d_tail, (span_rows - 8, 0))
-    d_normed_part = mm_nt(d_mixed, qkv_flat) + mm_nt(d_gate_low, gate_flat)
-    gain_one_part = jnp.sum(d_normed_part * normed_first.astype(f32), 0) / gain_first
+    d_normed_part = jnp.einsum(
+        "thc,dhc->td",
+        d_mixed.reshape(span_rows, heads, inner),
+        qkv_weight,
+        preferred_element_type=f32,
+    ) + jnp.einsum(
+        "thv,dhv->td",
+        d_gate_low.reshape(span_rows, heads, DV),
+        gate_weight,
+        preferred_element_type=f32,
+    )
     grad_qkv = mm_tn(normed_first, d_mixed).astype(bf16)
     grad_gate = (
         mm_tn(side_columns(normed_first, side, slice_rows), d_gate_low)
         + mm_tn(normed_side, d_gate_side)
     ).astype(bf16)
-    grad_mgate = mm_tn(d_gate_mlp, rows_out).astype(bf16)
-    grad_mup = mm_tn(d_up_mlp, rows_out).astype(bf16)
-    grad_down = mm_tn(hidden, cot_all).astype(bf16)
-
-    gains = jnp.concatenate([gain_one_part, gain_two_part, gain_out_part.reshape(-1)])
+
+    gains = jnp.concatenate([jnp.zeros_like(gain_two_part), gain_two_part, gain_out_part.reshape(-1)])
     gain_rows = -(-gains.shape[0] // 1024) * 8
     gains = jnp.pad(gains, (0, gain_rows * 128 - gains.shape[0])).reshape(gain_rows, 128)
     small = jnp.concatenate([gains, grad_conv.reshape(-1, 128)])
@@ -1401,6 +1559,7 @@
             grad_qkv,
             grad_gate,
             d_normed_part.astype(bf16),
+            hat_own,
             [grad_mgate, grad_mup, grad_down],
             small,
             gain_rows,
@@ -1435,7 +1594,7 @@
         grad_conv_s,
         grad_gate_s.astype(f32).reshape(-1, heads, DV),
         own_slice(2 * width, DV),
-        grad_out_s,
+        grad_out_s.astype(f32).T.reshape(heads, DV, -1),
         own_slice(width, width),
         grad_mgate_t.astype(f32).T,
         grad_mup_t.astype(f32).T,

time: 659 us -> 736 us (1.12)
  Pallas kernels: 462 us -> 522 us
  waiting for transfers between devices: 0.73 us -> 49.7 us
  matrix products: 109 us -> 88 us
  local copies, waits for them, and re-layouts: 32.3 us -> 18.9 us
    pallas_call x4, Pallas kernels: 225 us -> 319 us  [the longest x1 149 us: scattered_last(): link_call(body, number, [ANY] * 3 + [IN_VMEM] * 2 + [ANY] * len(mlp), [IN...]
    pallas_call x3 -> x2, Pallas kernels: 148 us -> 93.5 us  [gathered_seq(): link_call(body, number, [ANY], ANY, shaped((total, rows, width), value.dt...]
    reduce_scatter x2 -> x1, waiting for transfers between devices: 0.01 us -> 45.1 us  [scattered(): lax.psum_scatter(value.astype(bf16), axis, scatter_dimension=dimension, t...]
    dot_general x0 -> x4, matrix products: none -> 29.9 us  [the longest x1 10.4 us: on_device(): jnp.einsum('thc,dhc->td', d_mixed.reshape(span_rows, heads, inner), qkv_w...]
    dot_general x6 -> x1, matrix products: 31.6 us -> 6.22 us  [mm(): return jnp.dot(left, right, preferred_element_type=f32)]
    dot_general x6 -> x4, matrix products: 39.7 us -> 17.5 us  [mm_nt(): lax.dot_general(left, right, (((1,), (1,)), ((), ())), preferred_element_...]
    pallas_call x1 -> x2, Pallas kernels: 23.9 us -> 44.2 us  [gathered_sided(): link_call(body, number, [ANY, ANY], [ANY, ANY], [shaped((count, rows, wid...]
    unnamed x96 -> x81, local copies, waits for them, and re-layouts: 16 us -> 3.59 us
  transfers between devices with their start and end apart: 6 -> 6, of which waited for: 0 -> 2; matrix products, arithmetic and copies ran while one was open for 18% -> 12% of each run, Pallas kernels for 50% -> 47%
where the time goes in v5:
time: 736 us; the launch traced here: 729 us
  Pallas kernels  522 us (71%)
  matrix products  88 us (12%)
  waiting for transfers between devices  49.7 us (7%)
  other arithmetic  30.5 us (4%)
  local copies, waits for them, and re-layouts  18.9 us (3%)
  between operations  14.7 us (2%)
    pallas_call x1, Pallas kernels, scattered_last(): link_call(body, number, [ANY] * 3 + [IN_VMEM] * 2 + [ANY] * len(mlp), [IN...  149 us
    pallas_call x2, Pallas kernels, gathered_seq(): link_call(body, number, [ANY], ANY, shaped((total, rows, width), value.dt...  93.5 us
    pallas_call x1, Pallas kernels, gathered_swapped(): link_call(body, number, [ANY] * 2, [ANY] * 2, [shaped((total,) + ends.sha...  89.7 us
    pallas_call x1, Pallas kernels, scattered_seq_products(): link_call(body, number, [ANY] * (1 + n_left + n_right), [IN_VMEM] + [ANY]...  57.3 us
    reduce_scatter x1, waiting for transfers between devices, scattered(): lax.psum_scatter(value.astype(bf16), axis, scatter_dimension=dimension, t...  45.1 us
    pallas_call x2, Pallas kernels, gathered_sided(): link_call(body, number, [ANY, ANY], [ANY, ANY], [shaped((count, rows, wid...  44.2 us
    dot_general x8, matrix products, mm_tn(): lax.dot_general(left, right, (((0,), (0,)), ((), ())), preferred_element_...  34.2 us
    pallas_call x1, Pallas kernels, run_finish_backward(): kernel_call(finish_backward, heads, [whole(ends.shape), whole(grad_ends.s...  27.1 us
  transfers between devices with their start and end apart: 6, of which 2 were waited for; matrix products, arithmetic and copies ran while one was open for 12% of the time, Pallas kernels for 47%

profile of v5, /device:TPU:0, one launch (start us, length us, event | category | flops | bytes accessed | tf_op | source)
XLA Modules:
  0.0 729.5 jit_solution(4355802740212143958)
XLA Ops:
  7.2 0.7 all-gather.2.cloned.1.call-update
  8.0 0.8 convert_element_type.92
  8.7 1.2 fusion.27
  10.0 2.2 convert_multiply_fusion
  12.2 0.8 pad_maximum_fusion.half_ref
  13.1 23.9 %shard_map.229 = (bf16[4,128,2048]{2,1,0:T(8,128)(2,1)}, bf16[4,128,1024]{2,1,0:T(8,128)(2,1)}) custom-call(bf16[128,2048]{1,0:T(8,128)(2,1)} %copy-done.9, bf16[128,1024]{1,0:T(8,128)(2,1)} %pad_maximum_fusion.half_ref), custom_call_target="tpu_custom_call" | custom-call | bytes 7500000 | tf_op jit(solution)/shard_map/pallas_call | solution.py:1036
  37.0 8.6 %convert_bitcast_fusion.mixed_ref = bf16[4,512,512]{2,1,0:T(8,128)(2,1)S(1)} fusion(bf16[512,2048,1]{1,0,2:T(8,128)(2,1)} %bitcast.130, bf16[2048,4,512]{2,1,0:T(4,128)(2,1)} %param.19), kind=kOutput, calls=%fused_computation.33 | convolution fusion | flops 4296015872 | bytes 12582912 | tf_op jit(solution)/shard_map/td,dhc->htc/dot_general | solution.py:1452
  45.7 2.9 collective-permute-start
  49.3 6.5 fusion.24.gate_ref
  56.0 0.7 pad.14.clone.columns_ref
  58.6 0.7 convert_select_fusion.tail_ref
  59.3 22.9 %shard_map.230 = (bf16[4,2,256,256]{3,2,1,0:T(8,128)(2,1)}, bf16[4,2,256,256]{3,2,1,0:T(8,128)(2,1)}, bf16[4,512,384]{2,1,0:T(8,128)(2,1)}, bf16[4,512,128]{2,1,...) custom-call(bf16[4,512,512]{2,1,0:T(8,128)(2,1)} %copy-done.30, ...), custom_call_target="tpu_custom_call" | custom-call | flops 12000000000 | bytes 20000000 | tf_op jit(solution)/shard_map/pallas_call | solution.py:484
  82.2 41.7 %shard_map.231 = bf16[8,512,384]{2,1,0:T(8,128)(2,1)} custom-call(bf16[512,384]{1,0:T(8,128)(2,1)} %bitcast.136), custom_call_target="tpu_custom_call" | custom-call | bytes 15000000 | tf_op jit(solution)/shard_map/pallas_call | solution.py:1065
  124.0 10.3 %shard_map.232 = (bf16[4,8,128,256]{3,2,1,0:T(8,128)(2,1)}, f32[512,1024]{1,0:T(8,128)}, bf16[512,1024]{1,0:T(8,128)(2,1)}) custom-call(bf16[8,4,128,384]{3,2,1,0:T(8,128)(2,1)} %bitcast.124, bf16[4,8,128,384]{3,2,1,0:T(8,128)(2,1)} %get-tuple-element.73.local_ref, bf16[4,512,128]{2,1,0:T(8,128)(2,1)} %get-tuple-element.74.reach_ref, ...), custom_call_target="tpu_custom_call" | custom-call | flops 3000000000 | bytes 20000000 | tf_op jit(solution)/shard_map/pallas_call | solution.py:527
  134.3 1.1 collective-permute-start.1
  135.4 6.2 convolution_convert_fusion.2.source
  141.7 17.5 %shard_map.233 = f32[128,2048]{1,0:T(8,128)} custom-call(bf16[512,2048]{1,0:T(8,128)(2,1)} %convolution_convert_fusion.2.source), custom_call_target="tpu_custom_call" | custom-call | bytes 7500000 | tf_op jit(solution)/shard_map/pallas_call | solution.py:1115
  159.2 1.4 multiply_reduce_fusion.3
  160.7 0.9 multiply_convert_fusion.own_ref
  161.6 51.8 %shard_map.234 = bf16[8,128,2048]{2,1,0:T(8,128)(2,1)} custom-call(bf16[128,2048]{1,0:T(8,128)(2,1)} %multiply_convert_fusion.own_ref), custom_call_target="tpu_custom_call" | custom-call | bytes 15000000 | tf_op jit(solution)/shard_map/pallas_call | solution.py:1065
  213.5 5.2 fusion.57
  218.7 3.2 fusion.58
  221.9 5.3 fusion.13
  227.3 3.5 fusion.59
  230.8 5.4 add_convert_fusion.source
  236.2 57.3 %shard_map.235 = (f32[128,2048]{1,0:T(8,128)}, bf16[704,2048]{1,0:T(8,128)(2,1)}, bf16[704,2048]{1,0:T(8,128)(2,1)}, bf16[704,2048]{1,0:T(8,128)(2,1)}) custom-call(bf16[1024,2048]{1,0:T(8,128)(2,1)} %add_convert_fusion.source, bf16[704,1024]{1,0:T(8,128)(2,1)} %copy-done.13, bf16[704,1024]{1,0:T(8,128)(2,1)} %copy-done.12, ...), custom_call_target="tpu_custom_call" | custom-call | bytes 15000000 | tf_op jit(solution)/shard_map/pallas_call | solution.py:1230
  293.5 1.7 multiply_reduce_fusion.1
  295.2 2.5 multiply_add_fusion
  297.7 5.1 convolution_convert_fusion.1
  302.8 1.3 convert_element_type.109.own_ref
  304.2 0.8 pad_maximum_fusion.1.half_ref
  305.0 20.3 %shard_map.236 = (bf16[4,128,2048]{2,1,0:T(8,128)(2,1)}, bf16[4,128,1024]{2,1,0:T(8,128)(2,1)}) custom-call(bf16[128,2048]{1,0:T(8,128)(2,1)} %copy-done.8, bf16[128,1024]{1,0:T(8,128)(2,1)} %pad_maximum_fusion.1.half_ref), custom_call_target="tpu_custom_call" | custom-call | bytes 7500000 | tf_op jit(solution)/shard_map/pallas_call | solution.py:1036
  325.3 1.3 constant_dynamic-slice_fusion.8
  326.6 2.7 fusion.30
  329.8 3.7 fusion.60.d_branch_ref
  333.5 10.4 %shard_map.237 = (bf16[512,1024]{1,0:T(8,128)(2,1)}, bf16[512,1024]{1,0:T(8,128)(2,1)}, f32[1,256]{1,0:T(1,128)}, bf16[4,8,128,384]{3,2,1,0:T(8,128)(2,1)}, bf16[4,128,256]{2,1,0:T(8,128)(2,1)}) custom-call(f32[512,1024]{1,0:T(8,128)} %fusion.60.d_branch_ref, f32[512,1024]{1,0:T(8,128)} %get-tuple-element.86.core_ref, f32[4,512,256]{2,1,0:T(8,128)} %fusion.24.gate_ref, ...), custom_call_target="tpu_custom_call" | custom-call | flops 4000000000 | bytes 20000000 | tf_op jit(solution)/shard_map/pallas_call | solution.py:553
  343.9 3.8 add_convert_fusion.2
  348.6 1.3 constant_dynamic-slice_fusion.4
  349.9 1.3 fusion.38
  351.2 0.9 copy-done.32
  352.1 4.4 fusion.5
  356.5 89.7 %shard_map.238 = (bf16[8,512,256]{2,1,0:T(8,128)(2,1)}, bf16[512,1024]{1,0:T(8,128)(2,1)}) custom-call(bf16[512,256]{1,0:T(8,128)(2,1)} %bitcast.137, bf16[512,1024]{1,0:T(8,128)(2,1)} %get-tuple-element.90.gate_ref), custom_call_target="tpu_custom_call" | custom-call | bytes 18750000 | tf_op jit(solution)/shard_map/pallas_call | solution.py:1270
  446.2 3.9 add_convert_fusion.1.gate_ref
  450.1 1.1 convert_bitcast_fusion.3
  451.3 1.3 copy.44
  452.6 45.1 %reduce-scatter.3.cloned.1.call-done = bf16[128,2048]{1,0:T(8,128)(2,1)} async-done(((bf16[1024,2048]{1,0:T(8,128)(2,1)}), bf16[128,2048]{1,0:T(8,128)(2,1)}) %reduce-scatter.3.cloned.1.call-update) | async-done | bytes 524304 | tf_op jit(solution)/shard_map/reduce_scatter | solution.py:1408
  497.6 2.2 convert_element_type.108
  499.8 27.1 %shard_map.239 = (bf16[512,2048]{1,0:T(8,128)(2,1)}, f32[8,2048]{1,0:T(8,128)}, f32[8,2048]{1,0:T(8,128)}, f32[4,2048]{1,0:T(4,128)}) custom-call(bf16[8,4,128,384]{3,2,1,0:T(8,128)(2,1)} %bitcast.125, bf16[8,4,128,256]{3,2,1,0:T(8,128)(2,1)} %bitcast.145, bf16[4,512,512]{2,1,0:T(8,128)(2,1)} %copy-done.30, f32[4,8,512]{2,1,0:T(8,128)} %convert_select_fusion.tail_ref, ...), custom_call_target="tpu_custom_call" | custom-call | flops 12000000000 | bytes 20000000 | tf_op jit(solution)/shard_map/pallas_call | solution.py:591
  526.9 0.8 reshape.183
  527.7 0.8 slice.37
  528.6 1.5 collective-permute-start.2
  530.7 3.7 collective-permute-done.2
  534.4 0.9 slice_add_fusion
  535.2 1.5 scatter-add.4
  536.7 1.4 convert_dynamic-update-slice_fusion
  538.2 8.6 %convolution_convert_fusion.qkv_ref = bf16[2048,2048]{1,0:T(8,128)(2,1)} fusion(bf16[512,2048]{1,0:T(8,128)(2,1)S(1)} %bitcast.133, bf16[512,2048]{1,0:T(8,128)(2,1)} %convert_dynamic-update-slice_fusion), kind=kOutput, calls=%fused_computation.1 | convolution fusion | flops 4299161600 | bytes 12582912 | tf_op jit(solution)/shard_map/dot_general | solution.py:70
  546.8 10.4 %fusion.4.normed_ref = bf16[512,2048]{1,0:T(8,128)(2,1)} fusion(f32[512,2048,1]{1,0,2:T(8,128)S(1)} %copy-done.38, bf16[2048,4,512]{2,1,0:T(4,128)(2,1)} %param.19, bf16[64,4,8,512]{3,2,1,0:T(8,128)(2,1)S(1)} %bitcast.146), kind=kOutput, calls=%fused_computation.7 | convolution fusion | flops 4297064448 | bytes 16777216 | tf_op jit(solution)/shard_map/thc,dhc->td/dot_general | solution.py:1536
  557.1 148.6 %shard_map.240 = (bf16[256,2048]{1,0:T(8,128)(2,1)}, bf16[256,1024]{1,0:T(8,128)(2,1)}, f32[128,2048]{1,0:T(8,128)}, f32[8,104,128]{2,1,0:T(8,128)}, bf16[704,51...) custom-call(bf16[2048,2048]{1,0:T(8,128)(2,1)} %convolution_convert_fusion.qkv_ref, ...), custom_call_target="tpu_custom_call" | custom-call | bytes 31250000 | tf_op jit(solution)/shard_map/pallas_call | solution.py:1352
  705.8 1.2 reduce_sum.59
  707.0 3.8 reshape.193
  710.8 1.3 convert_element_type.117
  712.4 1.4 reshape.195
  713.9 3.5 convert_bitcast_fusion.1
  717.4 3.5 add_convert_fusion.3
  (118 shorter events, 7.1 us)
Async XLA Ops:
  7.2 214.7 %copy-start = (bf16[704,2048]{1,0:T(8,128)(2,1)S(1)}, bf16[704,2048]{1,0:T(8,128)(2,1)}, u32[]{:S(2)}) copy-start(bf16[704,2048]{1,0:T(8,128)(2,1)} %param.27) | copy-start | bytes 8650756
  7.2 127.1 %all-gather.2.cloned.1.call-start = ((), (), s32[]{:S(2)}) async-start(), calls=%async_computation.2 | async-start | bytes 4718592 | tf_op jit(solution)/shard_map/all_gather | solution.py:1404
  7.9 442.2 %reduce-scatter.5.cloned.1.call-start = ((), (), s32[]{:S(2)}) async-start(), calls=%async_computation.4 | async-start | bytes 2621440 | tf_op jit(solution)/shard_map/reduce_scatter | solution.py:1505
  8.7 36.9 %copy-start.21 = (f32[2048]{0:T(1024)}, f32[2048]{0:T(1024)S(1)}, u32[]{:S(2)}) copy-start(f32[2048]{0:T(1024)S(1)} %convert_element_type.92) | copy-start | bytes 24580
  10.0 35.7 %copy-start.26 = (f32[128]{0:T(128)}, f32[128]{0:T(128)S(1)}, u32[]{:S(2)}) copy-start(f32[128]{0:T(128)S(1)} %add_rsqrt_fusion.1) | copy-start | bytes 1540
  12.2 0.9 copy-start.9
  37.0 11.6 %copy-start.24 = (s32[512,4]{0,1:T(4,128)S(1)}, s32[512,4]{0,1:T(4,128)}, u32[]{:S(2)}) copy-start(s32[512,4]{0,1:T(4,128)} %param.28) | copy-start | bytes 24580
  37.0 12.3 %copy-start.25 = (s32[512,4]{0,1:T(4,128)S(1)}, s32[512,4]{0,1:T(4,128)}, u32[]{:S(2)}) copy-start(s32[512,4]{0,1:T(4,128)} %param.29) | copy-start | bytes 24580
  45.7 2.9 copy-start.30
  45.7 12.9 %collective-permute-start = (bf16[4,8,512]{2,1,0:T(8,128)(2,1)S(1)}, bf16[4,8,512]{2,1,0:T(8,128)(2,1)S(1)}, u32[]{:S(2)}, u32[]{:S(2)}) collective-permute-start(bf16[4,8,512]{2,1,0:T(8,128)(2,1)S(1)} %slice.40), channel_id=1, source_target_pairs={{0,1},{1,2},{2,3},{3,4},{4,5},{5,6},{6,7},{8,9},{9,10},{10,11},{11... | collective-permute-start | bytes 98312 | tf_op jit(solution)/shard_map/ppermute | solution.py:27
  49.3 8.1 %copy-start.23 = (bf16[4,4,512]{2,1,0:T(4,128)(2,1)S(1)}, bf16[4,4,512]{2,1,0:T(4,128)(2,1)}, u32[]{:S(2)}) copy-start(bf16[4,4,512]{2,1,0:T(4,128)(2,1)} %param.20) | copy-start | bytes 49156
  49.3 8.7 %copy-start.37 = (bf16[256]{0:T(256)(128)(2,1)S(1)}, bf16[256]{0:T(256)(128)(2,1)}, u32[]{:S(2)}) copy-start(bf16[256]{0:T(256)(128)(2,1)} %param.22) | copy-start | bytes 1540
  49.3 9.3 %copy-start.28 = (bf16[2048]{0:T(1024)(128)(2,1)S(1)}, bf16[2048]{0:T(1024)(128)(2,1)}, u32[]{:S(2)}) copy-start(bf16[2048]{0:T(1024)(128)(2,1)} %param.24) | copy-start | bytes 12292
  134.3 209.6 %collective-permute-start.1 = (bf16[512,1024]{1,0:T(8,128)(2,1)}, bf16[512,1024]{1,0:T(8,128)(2,1)}, u32[]{:S(2)}, u32[]{:S(2)}) collective-permute-start(bf16[512,1024]{1,0:T(8,128)(2,1)} %get-tuple-element.77), channel_id=1, source_target_pairs={{0,1},{1,0},{2,3},{3,2},{4,5},{5,4},{6,7},{7,6},{8,9},{9,8},{10,11... | collective-permute-start | bytes 3145736 | tf_op jit(solution)/shard_map/ppermute | solution.py:1395
  141.6 17.5 %copy-start.4 = (bf16[128,2048]{1,0:T(8,128)(2,1)S(1)}, bf16[128,2048]{1,0:T(8,128)(2,1)}, u32[]{:S(2)}) copy-start(bf16[128,2048]{1,0:T(8,128)(2,1)} %param.16) | copy-start | bytes 1572868
  160.6 134.6 %copy-start.2 = (f32[128,2048]{1,0:T(8,128)}, f32[128,2048]{1,0:T(8,128)S(1)}, u32[]{:S(2)}) copy-start(f32[128,2048]{1,0:T(8,128)S(1)} %get-tuple-element.145) | copy-start | bytes 3145732
  160.6 52.8 %copy-start.33 = (bf16[2048,704]{0,1:T(8,128)(2,1)S(1)}, bf16[2048,704]{0,1:T(8,128)(2,1)}, u32[]{:S(2)}) copy-start(bf16[2048,704]{0,1:T(8,128)(2,1)} %param.25) | copy-start | bytes 8650756
  213.4 5.3 copy-start.3
  213.5 5.3 copy-start.35
  218.7 3.2 copy-start.7
  221.9 5.3 copy-start.34
  227.3 3.6 copy-start.13
  227.3 3.6 copy-start.12
  236.2 59.0 %copy-start.10 = (bf16[128,2048]{1,0:T(8,128)(2,1)S(1)}, bf16[128,2048]{1,0:T(8,128)(2,1)}, u32[]{:S(2)}) copy-start(bf16[128,2048]{1,0:T(8,128)(2,1)} %param.17) | copy-start | bytes 1572868
  293.5 4.2 copy-start.11
  304.1 0.9 copy-start.8
  326.6 2.7 copy-start.20
  326.6 3.1 copy-start.31
  333.5 10.4 %copy-start.16 = (bf16[4,128,1024]{2,1,0:T(8,128)(2,1)S(1)}, bf16[4,128,1024]{2,1,0:T(8,128)(2,1)}, u32[]{:S(2)}) copy-start(bf16[4,128,1024]{2,1,0:T(8,128)(2,1)} %get-tuple-element.85) | copy-start | bytes 3145732
  347.8 2.1 copy-start.29
  347.8 2.1 copy-start.14
  347.8 149.8 %reduce-scatter.3.cloned.1.call-start = ((), (), s32[]{:S(2)}) async-start(), calls=%async_computation.3 | async-start | bytes 4718592 | tf_op jit(solution)/shard_map/reduce_scatter | solution.py:1408
  349.9 2.2 copy-start.32
  352.1 94.1 %copy-start.15 = (bf16[4,128,1024]{2,1,0:T(8,128)(2,1)S(1)}, bf16[4,128,1024]{2,1,0:T(8,128)(2,1)}, u32[]{:S(2)}) copy-start(bf16[4,128,1024]{2,1,0:T(8,128)(2,1)} %get-tuple-element.103) | copy-start | bytes 3145732
  499.8 38.4 %copy-start.19 = (bf16[4,128,2048]{2,1,0:T(8,128)(2,1)S(1)}, bf16[4,128,2048]{2,1,0:T(8,128)(2,1)}, u32[]{:S(2)}) copy-start(bf16[4,128,2048]{2,1,0:T(8,128)(2,1)} %get-tuple-element.71) | copy-start | bytes 6291460
  528.6 5.8 collective-permute-start.2
  538.2 8.6 %copy-start.36 = (bf16[512,2048]{1,0:T(8,128)(2,1)S(1)}, bf16[512,2048]{1,0:T(8,128)(2,1)}, u32[]{:S(2)}) copy-start(bf16[512,2048]{1,0:T(8,128)(2,1)} %convert_dynamic-update-slice_fusion) | copy-start | bytes 6291460
  538.2 8.6 %copy-start.38 = (f32[512,2048,1]{1,0,2:T(8,128)S(1)}, f32[512,2048,1]{1,0,2:T(8,128)}, u32[]{:S(2)}) copy-start(f32[512,2048,1]{1,0,2:T(8,128)} %fusion.5) | copy-start | bytes 12582916
  705.8 5.0 copy-start.17
  705.8 6.3 copy-start.5
  705.8 6.3 copy-start.6
  705.8 6.3 copy-start.22
  705.8 6.3 copy-start.27
  707.0 5.4 copy-start.18
  713.9 8.8 %copy-start.1 = (bf16[704,2048]{1,0:T(8,128)(2,1)S(1)}, bf16[704,2048]{1,0:T(8,128)(2,1)}, u32[]{:S(2)}) copy-start(bf16[704,2048]{1,0:T(8,128)(2,1)} %param.27) | copy-start | bytes 8650756
Sparse Core Ops, SparseCore 0:
  10.2 76.7 all-gather.1
  347.9 52.9 reduce-scatter.4
  405.0 92.5 reduce-scatter.2

commit v6 on v5

--- a/solution.py
+++ b/solution.py
@@ -19,6 +19,7 @@
 bf16 = jnp.bfloat16
 f32 = jnp.float32
 VMEM_BYTES = 56 * 2**20
+HOLD = 4
 
 
 def passed_along(value, axis, steps):
@@ -754,7 +755,7 @@
     keep.wait()
 
 
-def scatter_head(source_at, out_ref, own, crossed, passed, local, send, arrive, pause=0):
+def scatter_head(source_at, out_ref, own, crossed, passed, local, send, arrive, hold=0, pause=0):
     head, seq, sibling, across = head_places()
     far = lax.rem(sibling + 2, 4)
     loads = [
@@ -768,7 +769,8 @@
     for slot in range(2):
         copies[slot].start()
         loads[slot].start()
-    yield
+    for _ in range(1 + hold):
+        yield
     loads[0].wait()
     copies[0].wait_recv()
     own[0] = (own[0].astype(f32) + crossed[0].astype(f32)).astype(own.dtype)
@@ -1308,7 +1310,7 @@
             return normed_ref.at[pl.ds(pl.multiple_of(target * own_rows, own_rows), own_rows)]
 
         def normed_steps(four, own, local, *sems):
-            yield from scatter_head(normed_at, normed_out, *rest[13:19], 1)
+            yield from scatter_head(normed_at, normed_out, *rest[13:19], 0, 1)
             own[...] = small_ref[...]
             product = jnp.sum(normed_out[...] * hat_ref[...], axis=0, keepdims=True)
             for row in range(product.shape[1] // 128):
@@ -1344,7 +1346,7 @@
 
             begin = 29 + 6 * index
             steps.append(
-                scatter_head(mlp_at, out, *rest[begin : begin + 6], 5 + 3 * index)
+                scatter_head(mlp_at, out, *rest[begin : begin + 6], HOLD, 2 + 3 * index)
             )
         run_together(steps)
 
@@ -1501,7 +1503,9 @@
     d_core, d_gate_low, gain_out_part, local_grads, grad_end = run_local_backward(
         d_branch, core, gate_pre, gain_head, reach, turn
     )
-    out_half, grad_end = lax.optimization_barrier((out_half, grad_end))
+    grad_ends, d_gate_side = gathered_swapped(grad_end.reshape(-1, DV), d_gate_low, 7)
+    out_half, grad_ends, mlp_out = lax.optimization_barrier((out_half, grad_ends, mlp_out))
+    output = (middle + mlp_out).astype(bf16)
     grad_out_s = lax.psum_scatter(
         out_half,
         "seq",
@@ -1511,10 +1515,7 @@
         ],
         tiled=True,
     )
-    grad_ends, d_gate_side = gathered_swapped(grad_end.reshape(-1, DV), d_gate_low, 7)
     grad_ends = grad_ends.reshape(-1, heads, DK, DV)
-    mlp_out, grad_ends = lax.optimization_barrier((mlp_out, grad_ends))
-    output = (middle + mlp_out).astype(bf16)
     d_mixed, d_tail, d_lead, grad_conv = run_finish_backward(
         ends,
         grad_ends,
@@ -1530,6 +1531,7 @@
         d_core,
         local_grads,
     )
+    d_lead, grad_out_s = lax.optimization_barrier((d_lead, grad_out_s))
     from_next = passed_along(d_lead[:lead_rows], "seq", -1)
     d_tail = d_tail.at[8 - lead_rows :].add(from_next).astype(bf16)
     d_mixed = lax.dynamic_update_slice(d_mixed, d_tail, (span_rows - 8, 0))

time: 736 us -> 641 us (0.87)
  Pallas kernels: 522 us -> 475 us
  waiting for transfers between devices: 49.7 us -> 4.26 us
    reduce_scatter x1, waiting for transfers between devices: 45.1 us -> 0.01 us  [scattered(): lax.psum_scatter(value.astype(bf16), axis, scatter_dimension=dimension, t...]
    pallas_call x1, Pallas kernels: 89.7 us -> 59.6 us  [gathered_swapped(): link_call(body, number, [ANY] * 2, [ANY] * 2, [shaped((total,) + ends.sha...]
    pallas_call x1, Pallas kernels: 149 us -> 119 us  [scattered_last(): link_call(body, number, [ANY] * 3 + [IN_VMEM] * 2 + [ANY] * len(mlp), [IN...]
    pallas_call x2, Pallas kernels: 44.2 us -> 58.4 us  [gathered_sided(): link_call(body, number, [ANY, ANY], [ANY, ANY], [shaped((count, rows, wid...]
  transfers between devices with their start and end apart: 6 -> 6, of which waited for: 2 -> 2; matrix products, arithmetic and copies ran while one was open for 12% -> 8% of each run, Pallas kernels for 47% -> 37%
where the time goes in v6:
time: 641 us; the launch traced here: 630 us
  Pallas kernels  475 us (74%)
  matrix products  89 us (14%)
  other arithmetic  26.7 us (4%)
  local copies, waits for them, and re-layouts  16.7 us (3%)
  between operations  14.7 us (2%)
    pallas_call x1, Pallas kernels, scattered_last(): link_call(body, number, [ANY] * 3 + [IN_VMEM] * 2 + [ANY] * len(mlp), [IN...  119 us
    pallas_call x2, Pallas kernels, gathered_seq(): link_call(body, number, [ANY], ANY, shaped((total, rows, width), value.dt...  93.8 us
    pallas_call x1, Pallas kernels, gathered_swapped(): link_call(body, number, [ANY] * 2, [ANY] * 2, [shaped((total,) + ends.sha...  59.6 us
    pallas_call x2, Pallas kernels, gathered_sided(): link_call(body, number, [ANY, ANY], [ANY, ANY], [shaped((count, rows, wid...  58.4 us
    pallas_call x1, Pallas kernels, scattered_seq_products(): link_call(body, number, [ANY] * (1 + n_left + n_right), [IN_VMEM] + [ANY]...  55.4 us
    dot_general x8, matrix products, mm_tn(): lax.dot_general(left, right, (((0,), (0,)), ((), ())), preferred_element_...  32.3 us
    pallas_call x1, Pallas kernels, run_finish_backward(): kernel_call(finish_backward, heads, [whole(ends.shape), whole(grad_ends.s...  27.5 us
    pallas_call x1, Pallas kernels, run_local_forward(): kernel_call(local_forward, heads, [by_head((rows, INNER)), by_head((8, IN...  22.9 us
  transfers between devices with their start and end apart: 6, of which 2 were waited for; matrix products, arithmetic and copies ran while one was open for 8% of the time, Pallas kernels for 37%

profile of v6, /device:TPU:0, one launch (start us, length us, event | category | flops | bytes accessed | tf_op | source)
XLA Modules:
  0.0 630.4 jit_solution(15252903690990575478)
XLA Ops:
  7.2 0.7 all-gather.2.cloned.1.call-update
  8.0 0.8 convert_element_type.92
  8.7 1.2 fusion.27
  10.0 2.2 convert_multiply_fusion
  12.2 0.8 pad_maximum_fusion.half_ref
  13.1 23.9 %shard_map.229 = (bf16[4,128,2048]{2,1,0:T(8,128)(2,1)}, bf16[4,128,1024]{2,1,0:T(8,128)(2,1)}) custom-call(bf16[128,2048]{1,0:T(8,128)(2,1)} %copy-done.11, bf16[128,1024]{1,0:T(8,128)(2,1)} %pad_maximum_fusion.half_ref), custom_call_target="tpu_custom_call" | custom-call | bytes 7500000 | tf_op jit(solution)/shard_map/pallas_call | solution.py:1038
  37.0 8.6 %convert_bitcast_fusion.mixed_ref = bf16[4,512,512]{2,1,0:T(8,128)(2,1)S(1)} fusion(bf16[512,2048,1]{1,0,2:T(8,128)(2,1)} %bitcast.130, bf16[2048,4,512]{2,1,0:T(4,128)(2,1)} %param.19), kind=kOutput, calls=%fused_computation.33 | convolution fusion | flops 4296015872 | bytes 12582912 | tf_op jit(solution)/shard_map/td,dhc->htc/dot_general | solution.py:1454
  45.7 2.9 collective-permute-start
  49.3 6.5 %fusion.24.gate_ref = f32[4,512,256]{2,1,0:T(8,128)} fusion(bf16[512,2048,1]{1,0,2:T(8,128)(2,1)} %bitcast.131, bf16[2048,4,256]{2,1,0:T(4,128)(2,1)} %param.21), kind=kOutput, calls=%fused_computation.34 | convolution fusion | flops 2147483648 | bytes 8388608 | tf_op jit(solution)/shard_map/td,dhv->htv/dot_general | solution.py:1463
  56.0 0.7 pad.14.clone.columns_ref
  56.8 0.6 pad.15.run_rows_ref
  57.4 0.6 copy.48
  58.5 0.7 convert_select_fusion.tail_ref
  59.2 22.9 %shard_map.230 = (bf16[4,2,256,256]{3,2,1,0:T(8,128)(2,1)}, bf16[4,2,256,256]{3,2,1,0:T(8,128)(2,1)}, bf16[4,512,384]{2,1,0:T(8,128)(2,1)}, bf16[4,512,128]{2,1,...) custom-call(bf16[4,512,512]{2,1,0:T(8,128)(2,1)} %copy-done.34, ...), custom_call_target="tpu_custom_call" | custom-call | flops 12000000000 | bytes 20000000 | tf_op jit(solution)/shard_map/pallas_call | solution.py:485
  82.2 42.0 %shard_map.231 = bf16[8,512,384]{2,1,0:T(8,128)(2,1)} custom-call(bf16[512,384]{1,0:T(8,128)(2,1)} %bitcast.136), custom_call_target="tpu_custom_call" | custom-call | bytes 15000000 | tf_op jit(solution)/shard_map/pallas_call | solution.py:1067
  124.2 10.4 %shard_map.232 = (bf16[4,8,128,256]{3,2,1,0:T(8,128)(2,1)}, f32[512,1024]{1,0:T(8,128)}, bf16[512,1024]{1,0:T(8,128)(2,1)}) custom-call(bf16[8,4,128,384]{3,2,1,0:T(8,128)(2,1)} %bitcast.124, bf16[4,8,128,384]{3,2,1,0:T(8,128)(2,1)} %get-tuple-element.74.local_ref, bf16[4,512,128]{2,1,0:T(8,128)(2,1)} %get-tuple-element.75.reach_ref, ...), custom_call_target="tpu_custom_call" | custom-call | flops 3000000000 | bytes 20000000 | tf_op jit(solution)/shard_map/pallas_call | solution.py:528
  134.6 6.2 convolution_convert_fusion.2.source
  140.8 16.9 %shard_map.233 = f32[128,2048]{1,0:T(8,128)} custom-call(bf16[512,2048]{1,0:T(8,128)(2,1)} %convolution_convert_fusion.2.source), custom_call_target="tpu_custom_call" | custom-call | bytes 7500000 | tf_op jit(solution)/shard_map/pallas_call | solution.py:1117
  157.7 1.4 multiply_reduce_fusion.3
  159.2 0.9 multiply_convert_fusion.own_ref
  160.1 51.8 %shard_map.234 = bf16[8,128,2048]{2,1,0:T(8,128)(2,1)} custom-call(bf16[128,2048]{1,0:T(8,128)(2,1)} %multiply_convert_fusion.own_ref), custom_call_target="tpu_custom_call" | custom-call | bytes 15000000 | tf_op jit(solution)/shard_map/pallas_call | solution.py:1067
  212.0 5.3 fusion.57
  217.3 3.2 fusion.58
  220.5 5.3 fusion.13
  225.8 3.5 fusion.59
  229.3 5.4 add_convert_fusion.source
  234.8 55.4 %shard_map.235 = (f32[128,2048]{1,0:T(8,128)}, bf16[704,2048]{1,0:T(8,128)(2,1)}, bf16[704,2048]{1,0:T(8,128)(2,1)}, bf16[704,2048]{1,0:T(8,128)(2,1)}) custom-call(bf16[1024,2048]{1,0:T(8,128)(2,1)} %add_convert_fusion.source, bf16[704,1024]{1,0:T(8,128)(2,1)} %copy-done.15, bf16[704,1024]{1,0:T(8,128)(2,1)} %copy-done.14, ...), custom_call_target="tpu_custom_call" | custom-call | bytes 15000000 | tf_op jit(solution)/shard_map/pallas_call | solution.py:1232
  290.2 1.7 multiply_reduce_fusion.1
  291.9 2.5 multiply_add_fusion
  294.4 5.1 convolution_convert_fusion.1
  299.8 0.9 copy-done.7
  300.9 0.8 pad_maximum_fusion.1.half_ref
  301.7 34.5 %shard_map.236 = (bf16[4,128,2048]{2,1,0:T(8,128)(2,1)}, bf16[4,128,1024]{2,1,0:T(8,128)(2,1)}) custom-call(bf16[128,2048]{1,0:T(8,128)(2,1)} %copy-done.10, bf16[128,1024]{1,0:T(8,128)(2,1)} %pad_maximum_fusion.1.half_ref), custom_call_target="tpu_custom_call" | custom-call | bytes 7500000 | tf_op jit(solution)/shard_map/pallas_call | solution.py:1038
  336.2 6.6 %fusion.60.d_branch_ref = f32[512,1024]{1,0:T(8,128)} fusion(bf16[512,2048]{1,0:T(8,128)(2,1)} %bitcast.134, bf16[1024,2048]{1,0:T(8,128)(2,1)} %bitcast.144), kind=kOutput, calls=%fused_computation.122 | convolution fusion | flops 2147483648 | bytes 8388608 | tf_op jit(solution)/shard_map/dot_general | solution.py:67
  342.8 10.5 %shard_map.237 = (bf16[512,1024]{1,0:T(8,128)(2,1)}, bf16[512,1024]{1,0:T(8,128)(2,1)}, f32[1,256]{1,0:T(1,128)}, bf16[4,8,128,384]{3,2,1,0:T(8,128)(2,1)}, bf16[4,128,256]{2,1,0:T(8,128)(2,1)}) custom-call(f32[512,1024]{1,0:T(8,128)} %fusion.60.d_branch_ref, f32[512,1024]{1,0:T(8,128)} %get-tuple-element.86.core_ref, f32[4,512,256]{2,1,0:T(8,128)} %fusion.24.gate_ref, ...), custom_call_target="tpu_custom_call" | custom-call | flops 4000000000 | bytes 20000000 | tf_op jit(solution)/shard_map/pallas_call | solution.py:554
  353.3 59.6 %shard_map.238 = (bf16[8,512,256]{2,1,0:T(8,128)(2,1)}, bf16[512,1024]{1,0:T(8,128)(2,1)}) custom-call(bf16[512,256]{1,0:T(8,128)(2,1)} %bitcast.137, bf16[512,1024]{1,0:T(8,128)(2,1)} %get-tuple-element.89.gate_ref), custom_call_target="tpu_custom_call" | custom-call | bytes 18750000 | tf_op jit(solution)/shard_map/pallas_call | solution.py:1272
  413.1 1.3 fusion.30
  414.4 2.7 add_convert_fusion.2
  417.1 1.2 convert_element_type.110
  418.4 1.3 constant_dynamic-slice_fusion.4
  419.7 1.3 fusion.38
  421.3 2.7 add_convert_fusion.1.gate_ref
  424.2 4.4 fusion.5
  428.6 27.5 %shard_map.239 = (bf16[512,2048]{1,0:T(8,128)(2,1)}, f32[8,2048]{1,0:T(8,128)}, f32[8,2048]{1,0:T(8,128)}, f32[4,2048]{1,0:T(4,128)}) custom-call(bf16[8,4,128,384]{3,2,1,0:T(8,128)(2,1)} %bitcast.125, bf16[8,4,128,256]{3,2,1,0:T(8,128)(2,1)} %bitcast.145, bf16[4,512,512]{2,1,0:T(8,128)(2,1)} %copy-done.34, f32[4,8,512]{2,1,0:T(8,128)} %convert_select_fusion.tail_ref, ...), custom_call_target="tpu_custom_call" | custom-call | flops 12000000000 | bytes 20000000 | tf_op jit(solution)/shard_map/pallas_call | solution.py:592
  456.1 0.8 reshape.183
  456.9 0.6 pad_maximum_fusion.2.small_ref
  457.5 0.9 add_convert_fusion.4
  458.4 1.5 reduce-scatter.5.cloned.1.call-done
  459.9 0.8 slice.37
  460.8 1.3 collective-permute-start.2
  462.0 1.1 convert_bitcast_fusion.3
  463.2 1.3 copy.44
  464.5 2.0 collective-permute-done.2
  467.1 0.6 convert_dynamic-update-slice_fusion
  467.7 10.2 %convolution_convert_fusion.qkv_ref = bf16[2048,2048]{1,0:T(8,128)(2,1)} fusion(bf16[512,2048]{1,0:T(8,128)(2,1)} %bitcast.133, bf16[512,2048]{1,0:T(8,128)(2,1)} %convert_dynamic-update-slice_fusion), kind=kOutput, calls=%fused_computation.1 | convolution fusion | flops 4299161600 | bytes 12582912 | tf_op jit(solution)/shard_map/dot_general | solution.py:71
  477.9 10.4 %fusion.4.normed_ref = bf16[512,2048]{1,0:T(8,128)(2,1)} fusion(f32[512,2048,1]{1,0,2:T(8,128)S(1)} %copy-done.42, bf16[2048,4,512]{2,1,0:T(4,128)(2,1)} %param.19, bf16[64,4,8,512]{3,2,1,0:T(8,128)(2,1)S(1)} %bitcast.146), kind=kOutput, calls=%fused_computation.7 | convolution fusion | flops 4297064448 | bytes 16777216 | tf_op jit(solution)/shard_map/thc,dhc->td/dot_general | solution.py:1538
  488.3 119.1 %shard_map.240 = (bf16[256,2048]{1,0:T(8,128)(2,1)}, bf16[256,1024]{1,0:T(8,128)(2,1)}, f32[128,2048]{1,0:T(8,128)}, f32[8,104,128]{2,1,0:T(8,128)}, bf16[704,51...) custom-call(bf16[2048,2048]{1,0:T(8,128)(2,1)} %convolution_convert_fusion.qkv_ref, ...), custom_call_target="tpu_custom_call" | custom-call | bytes 31250000 | tf_op jit(solution)/shard_map/pallas_call | solution.py:1354
  607.5 1.1 reduce_sum.59
  608.7 3.8 reshape.193
  612.5 1.3 convert_element_type.117
  613.8 1.4 reshape.195
  615.6 2.9 add_convert_fusion.3
  618.5 3.3 convert_bitcast_fusion.1
  621.8 0.7 constant_dynamic-slice_fusion
  (128 shorter events, 4.7 us)
Async XLA Ops:
  7.2 213.3 %copy-start = (bf16[704,2048]{1,0:T(8,128)(2,1)S(1)}, bf16[704,2048]{1,0:T(8,128)(2,1)}, u32[]{:S(2)}) copy-start(bf16[704,2048]{1,0:T(8,128)(2,1)} %param.27) | copy-start | bytes 8650756
  7.2 127.4 %all-gather.2.cloned.1.call-start = ((), (), s32[]{:S(2)}) async-start(), calls=%async_computation.2 | async-start | bytes 4718592 | tf_op jit(solution)/shard_map/all_gather | solution.py:1406
  7.9 409.2 %reduce-scatter.3.cloned.1.call-start = ((), (), s32[]{:S(2)}) async-start(), calls=%async_computation.3 | async-start | bytes 4718592 | tf_op jit(solution)/shard_map/reduce_scatter | solution.py:1410
  8.7 36.9 %copy-start.25 = (f32[2048]{0:T(1024)}, f32[2048]{0:T(1024)S(1)}, u32[]{:S(2)}) copy-start(f32[2048]{0:T(1024)S(1)} %convert_element_type.92) | copy-start | bytes 24580
  10.0 35.7 %copy-start.30 = (f32[128]{0:T(128)}, f32[128]{0:T(128)S(1)}, u32[]{:S(2)}) copy-start(f32[128]{0:T(128)S(1)} %add_rsqrt_fusion.1) | copy-start | bytes 1540
  12.2 0.9 copy-start.11
  37.0 11.6 %copy-start.28 = (s32[512,4]{0,1:T(4,128)S(1)}, s32[512,4]{0,1:T(4,128)}, u32[]{:S(2)}) copy-start(s32[512,4]{0,1:T(4,128)} %param.28) | copy-start | bytes 24580
  37.0 12.3 %copy-start.29 = (s32[512,4]{0,1:T(4,128)S(1)}, s32[512,4]{0,1:T(4,128)}, u32[]{:S(2)}) copy-start(s32[512,4]{0,1:T(4,128)} %param.29) | copy-start | bytes 24580
  45.7 2.9 copy-start.34
  45.7 12.9 %collective-permute-start = (bf16[4,8,512]{2,1,0:T(8,128)(2,1)S(1)}, bf16[4,8,512]{2,1,0:T(8,128)(2,1)S(1)}, u32[]{:S(2)}, u32[]{:S(2)}) collective-permute-start(bf16[4,8,512]{2,1,0:T(8,128)(2,1)S(1)} %slice.40), channel_id=1, source_target_pairs={{0,1},{1,2},{2,3},{3,4},{4,5},{5,6},{6,7},{8,9},{9,10},{10,11},{11... | collective-permute-start | bytes 98312 | tf_op jit(solution)/shard_map/ppermute | solution.py:28
  49.3 8.1 %copy-start.27 = (bf16[4,4,512]{2,1,0:T(4,128)(2,1)S(1)}, bf16[4,4,512]{2,1,0:T(4,128)(2,1)}, u32[]{:S(2)}) copy-start(bf16[4,4,512]{2,1,0:T(4,128)(2,1)} %param.20) | copy-start | bytes 49156
  49.3 8.7 %copy-start.41 = (bf16[256]{0:T(256)(128)(2,1)S(1)}, bf16[256]{0:T(256)(128)(2,1)}, u32[]{:S(2)}) copy-start(bf16[256]{0:T(256)(128)(2,1)} %param.22) | copy-start | bytes 1540
  49.3 9.2 %copy-start.32 = (bf16[2048]{0:T(1024)(128)(2,1)S(1)}, bf16[2048]{0:T(1024)(128)(2,1)}, u32[]{:S(2)}) copy-start(bf16[2048]{0:T(1024)(128)(2,1)} %param.24) | copy-start | bytes 12292
  140.8 16.9 %copy-start.5 = (bf16[128,2048]{1,0:T(8,128)(2,1)S(1)}, bf16[128,2048]{1,0:T(8,128)(2,1)}, u32[]{:S(2)}) copy-start(bf16[128,2048]{1,0:T(8,128)(2,1)} %param.16) | copy-start | bytes 1572868
  159.2 132.7 %copy-start.2 = (f32[128,2048]{1,0:T(8,128)}, f32[128,2048]{1,0:T(8,128)S(1)}, u32[]{:S(2)}) copy-start(f32[128,2048]{1,0:T(8,128)S(1)} %get-tuple-element.147) | copy-start | bytes 3145732
  159.2 52.8 %copy-start.36 = (bf16[2048,704]{0,1:T(8,128)(2,1)S(1)}, bf16[2048,704]{0,1:T(8,128)(2,1)}, u32[]{:S(2)}) copy-start(bf16[2048,704]{0,1:T(8,128)(2,1)} %param.25) | copy-start | bytes 8650756
  211.9 5.3 copy-start.4
  211.9 5.3 copy-start.38
  217.2 3.2 copy-start.9
  220.5 5.3 copy-start.37
  225.8 3.6 copy-start.15
  225.8 3.6 copy-start.14
  234.8 57.1 %copy-start.12 = (bf16[128,2048]{1,0:T(8,128)(2,1)S(1)}, bf16[128,2048]{1,0:T(8,128)(2,1)}, u32[]{:S(2)}) copy-start(bf16[128,2048]{1,0:T(8,128)(2,1)} %param.17) | copy-start | bytes 1572868
  290.2 4.2 copy-start.13
  299.5 1.2 copy-start.7
  299.5 160.4 %reduce-scatter.5.cloned.1.call-start = ((), (), s32[]{:S(2)}) async-start(), calls=%async_computation.4 | async-start | bytes 2621440 | tf_op jit(solution)/shard_map/reduce_scatter | solution.py:1509
  299.6 114.8 %collective-permute-start.1 = (bf16[512,1024]{1,0:T(8,128)(2,1)}, bf16[512,1024]{1,0:T(8,128)(2,1)S(1)}, u32[]{:S(2)}, u32[]{:S(2)}) collective-permute-start(bf16[512,1024]{1,0:T(8,128)(2,1)} %get-tuple-element.78), channel_id=1, source_target_pairs={{0,1},{1,0},{2,3},{3,2},{4,5},{5,4},{6,7},{7,6},{8,9},{9,8},{10,11... | collective-permute-start | bytes 3145736 | tf_op jit(solution)/shard_map/ppermute | solution.py:1397
  300.8 0.9 copy-start.10
  342.8 70.1 %copy-start.22 = (bf16[4,128,2048]{2,1,0:T(8,128)(2,1)S(1)}, bf16[4,128,2048]{2,1,0:T(8,128)(2,1)}, u32[]{:S(2)}) copy-start(bf16[4,128,2048]{2,1,0:T(8,128)(2,1)} %get-tuple-element.84) | copy-start | bytes 6291460
  353.3 59.8 %copy-start.40 = (bf16[512,1024]{1,0:T(8,128)(2,1)S(1)}, bf16[512,1024]{1,0:T(8,128)(2,1)}, u32[]{:S(2)}) copy-start(bf16[512,1024]{1,0:T(8,128)(2,1)} %get-tuple-element.78) | copy-start | bytes 3145732
  413.1 1.3 copy-start.19
  417.1 2.6 copy-start.33
  417.1 2.6 copy-start.16
  419.7 1.3 copy-start.17
  419.7 1.5 copy-start.18
  421.3 2.9 copy-start.35
  428.6 28.9 %copy-start.3 = (f32[128,2048]{1,0:T(8,128)S(1)}, f32[128,2048]{1,0:T(8,128)}, u32[]{:S(2)}) copy-start(f32[128,2048]{1,0:T(8,128)} %copy-done.2) | copy-start | bytes 3145732
  457.5 9.1 %copy-start.24 = (f32[8,2048]{1,0:T(8,128)S(1)}, f32[8,2048]{1,0:T(8,128)}, u32[]{:S(2)}) copy-start(f32[8,2048]{1,0:T(8,128)} %get-tuple-element.101) | copy-start | bytes 196612
  460.8 5.8 collective-permute-start.2
  467.7 10.2 %copy-start.39 = (bf16[512,2048]{1,0:T(8,128)(2,1)S(1)}, bf16[512,2048]{1,0:T(8,128)(2,1)}, u32[]{:S(2)}) copy-start(bf16[512,2048]{1,0:T(8,128)(2,1)} %convert_dynamic-update-slice_fusion) | copy-start | bytes 6291460
  467.7 10.2 %copy-start.42 = (f32[512,2048,1]{1,0,2:T(8,128)S(1)}, f32[512,2048,1]{1,0,2:T(8,128)}, u32[]{:S(2)}) copy-start(f32[512,2048,1]{1,0,2:T(8,128)} %fusion.5) | copy-start | bytes 12582916
  607.5 5.0 copy-start.20
  607.5 6.3 %copy-start.21 = (bf16[256,1024]{1,0:T(8,128)(2,1)S(1)}, bf16[256,1024]{1,0:T(8,128)(2,1)}, u32[]{:S(2)}) copy-start(bf16[256,1024]{1,0:T(8,128)(2,1)} %get-tuple-element.115) | copy-start | bytes 1572868
  608.6 6.6 %copy-start.23 = (f32[104,128]{1,0:T(8,128)}, f32[104,128]{1,0:T(8,128)S(1)}, u32[]{:S(2)}) copy-start(f32[104,128]{1,0:T(8,128)S(1)} %reduce_sum.59) | copy-start | bytes 159748
  608.6 6.6 %copy-start.6 = (bf16[128,2048]{1,0:T(8,128)(2,1)S(1)}, bf16[128,2048]{1,0:T(8,128)(2,1)}, u32[]{:S(2)}) copy-start(bf16[128,2048]{1,0:T(8,128)(2,1)} %param.16) | copy-start | bytes 1572868
  608.7 6.6 %copy-start.8 = (f32[128,2048]{1,0:T(8,128)S(1)}, f32[128,2048]{1,0:T(8,128)}, u32[]{:S(2)}) copy-start(f32[128,2048]{1,0:T(8,128)} %get-tuple-element.112) | copy-start | bytes 3145732
  608.7 6.6 %copy-start.26 = (f32[2048]{0:T(1024)S(1)}, f32[2048]{0:T(1024)}, u32[]{:S(2)}) copy-start(f32[2048]{0:T(1024)} %copy-done.25) | copy-start | bytes 24580
  608.7 6.6 %copy-start.31 = (f32[128]{0:T(128)S(1)}, f32[128]{0:T(128)}, u32[]{:S(2)}) copy-start(f32[128]{0:T(128)} %copy-done.30) | copy-start | bytes 1540
  615.3 3.2 slice-start
  615.6 8.0 %copy-start.1 = (bf16[704,2048]{1,0:T(8,128)(2,1)S(1)}, bf16[704,2048]{1,0:T(8,128)(2,1)}, u32[]{:S(2)}) copy-start(bf16[704,2048]{1,0:T(8,128)(2,1)} %param.27) | copy-start | bytes 8650756
Sparse Core Ops, SparseCore 0:
  10.2 76.7 all-gather.1
  299.7 98.6 reduce-scatter.2
  418.5 41.3 reduce-scatter.4

commit v7 on v6

--- a/solution.py
+++ b/solution.py
@@ -1016,41 +1016,29 @@
     return out.reshape(count * rows, width)
 
 
-def gathered_sided(value, half, number, pieces=4, half_pieces=2):
+def gathered_crossed(value, half, number, pieces=4):
     count = lax.axis_size("head")
     rows, width = value.shape
 
-    def body(own_ref, half_ref, out_ref, beside_ref, landing, *sems):
+    def body(own_ref, half_ref, out_ref, landed_ref, local, send, arrive, crossing):
         head, line, side = seq_places()
         beside = (head, line * SIDE + 1 - side)
         greet(head_partners() + [(beside, None)])
-
-        def half_steps():
-            copy = remote(half_ref, landing, sems[6].at[0], sems[6].at[1], beside)
-            copy.start()
-            yield
-            yield
-            copy.wait()
-            yield from gather_head(landing, beside_ref, *sems[3:6], half_pieces)
-
-        run_together([half_steps(), gather_head(own_ref, out_ref, *sems[:3], pieces)])
-
-    out, beside = link_call(
+        cross = remote(half_ref, landed_ref, crossing.at[0], crossing.at[1], beside)
+        cross.start()
+        run_together([gather_head(own_ref, out_ref, local, send, arrive, pieces)])
+        cross.wait()
+
+    out, landed = link_call(
         body,
         number,
         [ANY, ANY],
         [ANY, ANY],
-        [
-            shaped((count, rows, width), value.dtype),
-            shaped((count, rows, half.shape[1]), value.dtype),
-        ],
-        [pltpu.VMEM(half.shape, half.dtype)]
-        + [DMA((1,)), DMA((3, pieces)), DMA((3, pieces))]
-        + [DMA((1,)), DMA((3, half_pieces)), DMA((3, half_pieces))]
-        + [DMA((2,))],
+        [shaped((count, rows, width), value.dtype), shaped(half.shape, half.dtype)],
+        [DMA((1,)), DMA((3, pieces)), DMA((3, pieces)), DMA((2,))],
         60_000_000,
     )(value, half)
-    return out.reshape(count * rows, width), beside.reshape(count * rows, half.shape[1])
+    return out.reshape(count * rows, width), landed
 
 
 def gathered_seq(value, number):
@@ -1249,38 +1237,52 @@
     return outs[0], list(outs[1:])
 
 
-def gathered_swapped(ends, d_gate, number):
-    total = lax.axis_size("seq")
+def gathered_more(ends, half, number, swap=None):
+    total, heads = lax.axis_size("seq"), lax.axis_size("head")
     count = total // SIDE
-
-    def body(ends_ref, gate_ref, ends_out, gate_out, *rest):
+    swaps = [] if swap is None else [swap]
+
+    def body(ends_ref, half_ref, *rest):
         head, line, side = seq_places()
         beside = (head, line * SIDE + 1 - side)
-        greet(seq_partners(count))
-
-        def swap_steps():
+        swap_refs, rest = rest[: len(swaps)], rest[len(swaps) :]
+        ends_out, half_out, rest = rest[0], rest[1], rest[2:]
+        swap_outs, rest = rest[: len(swaps)], rest[len(swaps) :]
+        greet(head_partners() + seq_partners(count))
+
+        def swap_steps(source, target):
             yield
             yield
-            copy = remote(gate_ref, gate_out, rest[5].at[0], rest[5].at[1], beside)
+            copy = remote(source, target, rest[8].at[0], rest[8].at[1], beside)
             copy.start()
             for _ in range(count):
                 yield
             copy.wait()
 
-        run_together([gather_seq(ends_ref, ends_out, *rest[:5], count), swap_steps()])
-
-    return link_call(
+        run_together(
+            [
+                gather_seq(ends_ref, ends_out, *rest[:5], count),
+                gather_head(half_ref, half_out, *rest[5:8], 1),
+            ]
+            + [swap_steps(*refs) for refs in zip(swap_refs, swap_outs)]
+        )
+
+    outs = link_call(
         body,
         number,
-        [ANY] * 2,
-        [ANY] * 2,
+        [ANY] * (2 + len(swaps)),
+        [ANY] * (2 + len(swaps)),
         [
             shaped((total,) + ends.shape, ends.dtype),
-            shaped(d_gate.shape, d_gate.dtype),
-        ],
-        [DMA((1,))] + [DMA((2 * count,)) for _ in range(4)] + [DMA((2,))],
+            shaped((heads,) + half.shape, half.dtype),
+        ]
+        + [shaped(value.shape, value.dtype) for value in swaps],
+        [DMA((1,))]
+        + [DMA((2 * count,)) for _ in range(4)]
+        + [DMA((1,)), DMA((3, 1)), DMA((3, 1)), DMA((2,))],
         150_000_000,
-    )(ends, d_gate)
+    )(ends, half, *swaps)
+    return [outs[0], outs[1].reshape(-1, half.shape[1])] + list(outs[2:])
 
 
 def scattered_last(qkv, gate, normed, hat, mlp, small, gain_rows, number, pieces=4, gate_pieces=2):
@@ -1448,7 +1450,7 @@
     scale_own = rms_scale(input_f)
     hat_own = input_f * scale_own
     normed_own = (hat_own * gain_first).astype(bf16)
-    normed_first, normed_side = gathered_sided(
+    normed_first, normed_half = gathered_crossed(
         normed_own, side_columns(normed_own, 1 - side, slice_rows), 1
     )
     mixed_in = jnp.einsum(
@@ -1459,7 +1461,8 @@
     solve, score, fresh, reach, inner_part, turn, local_states, piece_end = run_local_forward(
         mixed_in, tail_in, taps, columns, run_rows, heads
     )
-    ends = gathered_seq(piece_end.reshape(-1, DV + DK), 2).reshape(-1, heads, DK, DV + DK)
+    ends, normed_side = gathered_more(piece_end.reshape(-1, DV + DK), normed_half, 2)
+    ends = ends.reshape(-1, heads, DK, DV + DK)
     gate_pre = jnp.einsum("td,dhv->htv", normed_first, gate_weight, preferred_element_type=f32)
     states, core, branch = run_finish_forward(
         ends, local_states, reach, inner_part, gate_pre, gain_head
@@ -1471,6 +1474,7 @@
     hat_two = middle * scale_two
     normed_two = (hat_two * gain_second).astype(bf16)
 
+    normed_two, branch_side = lax.optimization_barrier((normed_two, branch_side))
     rows_out = gathered_seq(normed_two, 4).reshape(-1, width)
     cot_f = out_cot.astype(f32)
     gate_units, up_units = mlp_gate.T, mlp_up.T
@@ -1495,15 +1499,17 @@
     )
     mlp_out = scattered(mlp_part, "seq")
     d_mix = d_middle.astype(bf16)
-    d_mix_all, d_mix_side = gathered_sided(d_mix, side_columns(d_mix, 1 - side, slice_rows), 6)
+    d_mix_all, d_mix_half = gathered_crossed(d_mix, side_columns(d_mix, 1 - side, slice_rows), 6)
     d_branch = mm_nt(d_mix_all, out_flat)
+    d_core, d_gate_low, gain_out_part, local_grads, grad_end = run_local_backward(
+        d_branch, core, gate_pre, gain_head, reach, turn
+    )
+    grad_ends, d_mix_side, d_gate_side = gathered_more(
+        grad_end.reshape(-1, DV), d_mix_half, 7, d_gate_low
+    )
     out_half = (
         mm_tn(side_columns(d_mix_all, side, slice_rows), branch) + mm_tn(d_mix_side, branch_side)
     ).astype(bf16)
-    d_core, d_gate_low, gain_out_part, local_grads, grad_end = run_local_backward(
-        d_branch, core, gate_pre, gain_head, reach, turn
-    )
-    grad_ends, d_gate_side = gathered_swapped(grad_end.reshape(-1, DV), d_gate_low, 7)
     out_half, grad_ends, mlp_out = lax.optimization_barrier((out_half, grad_ends, mlp_out))
     output = (middle + mlp_out).astype(bf16)
     grad_out_s = lax.psum_scatter(

time: 641 us -> 633 us (0.988)
  Pallas kernels: 475 us -> 464 us
    pallas_call x2 -> x1, Pallas kernels: 93.8 us -> 51.7 us  [gathered_seq(): link_call(body, number, [ANY], ANY, shaped((total, rows, width), value.dt...]
    pallas_call x3 -> x4, Pallas kernels: 118 us -> 154 us  [the longest x2 114 us: gathered_more(): link_call(body, number, [ANY] * (2 + len(swaps)), [ANY] * (2 + len(swaps)...]
  transfers between devices with their start and end apart: 6 -> 6, of which waited for: 2 -> 2; matrix products, arithmetic and copies ran while one was open for 8% -> 10% of each run, Pallas kernels for 37% -> 39%
where the time goes in v7:
time: 633 us; the launch traced here: 624 us
  Pallas kernels  464 us (73%)
  matrix products  90 us (14%)
  other arithmetic  26.8 us (4%)
  local copies, waits for them, and re-layouts  16.7 us (3%)
  between operations  14.7 us (2%)
    pallas_call x1, Pallas kernels, scattered_last(): link_call(body, number, [ANY] * 3 + [IN_VMEM] * 2 + [ANY] * len(mlp), [IN...  119 us
    pallas_call x2, Pallas kernels, gathered_more(): link_call(body, number, [ANY] * (2 + len(swaps)), [ANY] * (2 + len(swaps)...  114 us
    pallas_call x1, Pallas kernels, gathered_seq(): link_call(body, number, [ANY], ANY, shaped((total, rows, width), value.dt...  51.7 us
    pallas_call x1, Pallas kernels, scattered_seq_products(): link_call(body, number, [ANY] * (1 + n_left + n_right), [IN_VMEM] + [ANY]...  50.4 us
    pallas_call x2, Pallas kernels, gathered_crossed(): link_call(body, number, [ANY, ANY], [ANY, ANY], [shaped((count, rows, wid...  40 us
    dot_general x8, matrix products, mm_tn(): lax.dot_general(left, right, (((0,), (0,)), ((), ())), preferred_element_...  32.3 us
    pallas_call x1, Pallas kernels, run_finish_backward(): kernel_call(finish_backward, heads, [whole(ends.shape), whole(grad_ends.s...  27.5 us
    pallas_call x1, Pallas kernels, run_local_forward(): kernel_call(local_forward, heads, [by_head((rows, INNER)), by_head((8, IN...  22.9 us
  transfers between devices with their start and end apart: 6, of which 2 were waited for; matrix products, arithmetic and copies ran while one was open for 10% of the time, Pallas kernels for 39%

profile of v7, /device:TPU:0, one launch (start us, length us, event | category | flops | bytes accessed | tf_op | source)
XLA Modules:
  0.0 623.6 jit_solution(7519609951313134858)
XLA Ops:
  7.2 0.7 all-gather.2.cloned.1.call-update
  8.0 0.8 convert_element_type.92
  8.7 1.2 fusion.27
  10.0 2.2 convert_multiply_fusion
  12.2 0.8 pad_maximum_fusion.half_ref
  13.1 20.2 %shard_map.229 = (bf16[4,128,2048]{2,1,0:T(8,128)(2,1)}, bf16[128,1024]{1,0:T(8,128)(2,1)}) custom-call(bf16[128,2048]{1,0:T(8,128)(2,1)} %copy-done.11, bf16[128,1024]{1,0:T(8,128)(2,1)} %pad_maximum_fusion.half_ref), custom_call_target="tpu_custom_call" | custom-call | bytes 7500000 | tf_op jit(solution)/shard_map/pallas_call | solution.py:1032
  33.3 8.7 %convert_bitcast_fusion.mixed_ref = bf16[4,512,512]{2,1,0:T(8,128)(2,1)S(1)} fusion(bf16[512,2048,1]{1,0,2:T(8,128)(2,1)} %bitcast.128, bf16[2048,4,512]{2,1,0:T(4,128)(2,1)} %param.19), kind=kOutput, calls=%fused_computation.33 | convolution fusion | flops 4296015872 | bytes 12582912 | tf_op jit(solution)/shard_map/td,dhc->htc/dot_general | solution.py:1456
  42.0 3.4 collective-permute-start
  46.2 6.9 %fusion.24.gate_ref = f32[4,512,256]{2,1,0:T(8,128)} fusion(bf16[512,2048,1]{1,0,2:T(8,128)(2,1)} %bitcast.129, bf16[2048,4,256]{2,1,0:T(4,128)(2,1)} %param.21), kind=kOutput, calls=%fused_computation.34 | convolution fusion | flops 2147483648 | bytes 8388608 | tf_op jit(solution)/shard_map/td,dhv->htv/dot_general | solution.py:1466
  53.2 0.7 pad.14.clone.columns_ref
  54.6 0.6 copy.48
  55.8 0.7 convert_select_fusion.tail_ref
  56.5 22.9 %shard_map.230 = (bf16[4,2,256,256]{3,2,1,0:T(8,128)(2,1)}, bf16[4,2,256,256]{3,2,1,0:T(8,128)(2,1)}, bf16[4,512,384]{2,1,0:T(8,128)(2,1)}, bf16[4,512,128]{2,1,...) custom-call(bf16[4,512,512]{2,1,0:T(8,128)(2,1)} %copy-done.36, ...), custom_call_target="tpu_custom_call" | custom-call | flops 12000000000 | bytes 20000000 | tf_op jit(solution)/shard_map/pallas_call | solution.py:485
  79.4 49.8 %shard_map.231 = (bf16[8,512,384]{2,1,0:T(8,128)(2,1)}, bf16[4,128,1024]{2,1,0:T(8,128)(2,1)}) custom-call(bf16[512,384]{1,0:T(8,128)(2,1)} %bitcast.134, bf16[128,1024]{1,0:T(8,128)(2,1)} %get-tuple-element.79.half_ref), custom_call_target="tpu_custom_call" | custom-call | bytes 18750000 | tf_op jit(solution)/shard_map/pallas_call | solution.py:1270
  129.2 10.3 %shard_map.232 = (bf16[4,8,128,256]{3,2,1,0:T(8,128)(2,1)}, f32[512,1024]{1,0:T(8,128)}, bf16[512,1024]{1,0:T(8,128)(2,1)}) custom-call(bf16[8,4,128,384]{3,2,1,0:T(8,128)(2,1)} %bitcast.143, bf16[4,8,128,384]{3,2,1,0:T(8,128)(2,1)} %get-tuple-element.81.local_ref, bf16[4,512,128]{2,1,0:T(8,128)(2,1)} %get-tuple-element.82.reach_ref, ...), custom_call_target="tpu_custom_call" | custom-call | flops 3000000000 | bytes 20000000 | tf_op jit(solution)/shard_map/pallas_call | solution.py:528
  139.6 1.1 collective-permute-start.1
  140.7 6.2 convolution_convert_fusion.2.source
  146.9 17.2 %shard_map.233 = f32[128,2048]{1,0:T(8,128)} custom-call(bf16[512,2048]{1,0:T(8,128)(2,1)} %convolution_convert_fusion.2.source), custom_call_target="tpu_custom_call" | custom-call | bytes 7500000 | tf_op jit(solution)/shard_map/pallas_call | solution.py:1105
  164.1 1.4 multiply_reduce_fusion.3
  165.6 1.1 multiply_convert_fusion.own_ref
  166.7 51.7 %shard_map.234 = bf16[8,128,2048]{2,1,0:T(8,128)(2,1)} custom-call(bf16[128,2048]{1,0:T(8,128)(2,1)} %multiply_convert_fusion.own_ref), custom_call_target="tpu_custom_call" | custom-call | bytes 15000000 | tf_op jit(solution)/shard_map/pallas_call | solution.py:1055
  218.4 6.0 fusion.57
  224.5 3.2 fusion.58
  227.7 5.3 fusion.13
  233.0 3.5 fusion.59
  236.6 5.4 add_convert_fusion.source
  242.0 50.4 %shard_map.235 = (f32[128,2048]{1,0:T(8,128)}, bf16[704,2048]{1,0:T(8,128)(2,1)}, bf16[704,2048]{1,0:T(8,128)(2,1)}, bf16[704,2048]{1,0:T(8,128)(2,1)}) custom-call(bf16[1024,2048]{1,0:T(8,128)(2,1)} %add_convert_fusion.source, bf16[704,1024]{1,0:T(8,128)(2,1)} %copy-done.15, bf16[704,1024]{1,0:T(8,128)(2,1)} %copy-done.14, ...), custom_call_target="tpu_custom_call" | custom-call | bytes 15000000 | tf_op jit(solution)/shard_map/pallas_call | solution.py:1220
  292.4 1.7 multiply_reduce_fusion.1
  294.1 2.5 multiply_add_fusion
  296.6 5.1 convolution_convert_fusion.1
  301.9 1.0 copy-done.7
  303.0 0.8 pad_maximum_fusion.1.half_ref
  303.8 19.8 %shard_map.236 = (bf16[4,128,2048]{2,1,0:T(8,128)(2,1)}, bf16[128,1024]{1,0:T(8,128)(2,1)}) custom-call(bf16[128,2048]{1,0:T(8,128)(2,1)} %copy-done.10, bf16[128,1024]{1,0:T(8,128)(2,1)} %pad_maximum_fusion.1.half_ref), custom_call_target="tpu_custom_call" | custom-call | bytes 7500000 | tf_op jit(solution)/shard_map/pallas_call | solution.py:1032
  323.7 6.5 %fusion.60.d_branch_ref = f32[512,1024]{1,0:T(8,128)} fusion(bf16[512,2048]{1,0:T(8,128)(2,1)} %bitcast.132, bf16[1024,2048]{1,0:T(8,128)(2,1)} %bitcast.142), kind=kOutput, calls=%fused_computation.122 | convolution fusion | flops 2147483648 | bytes 8388608 | tf_op jit(solution)/shard_map/dot_general | solution.py:67
  330.2 10.6 %shard_map.237 = (bf16[512,1024]{1,0:T(8,128)(2,1)}, bf16[512,1024]{1,0:T(8,128)(2,1)}, f32[1,256]{1,0:T(1,128)}, bf16[4,8,128,384]{3,2,1,0:T(8,128)(2,1)}, bf16[4,128,256]{2,1,0:T(8,128)(2,1)}) custom-call(f32[512,1024]{1,0:T(8,128)} %fusion.60.d_branch_ref, f32[512,1024]{1,0:T(8,128)} %get-tuple-element.93.core_ref, f32[4,512,256]{2,1,0:T(8,128)} %fusion.24.gate_ref, ...), custom_call_target="tpu_custom_call" | custom-call | flops 4000000000 | bytes 20000000 | tf_op jit(solution)/shard_map/pallas_call | solution.py:554
  340.8 64.3 %shard_map.238 = (bf16[8,512,256]{2,1,0:T(8,128)(2,1)}, bf16[4,128,1024]{2,1,0:T(8,128)(2,1)}, bf16[512,1024]{1,0:T(8,128)(2,1)}) custom-call(bf16[512,256]{1,0:T(8,128)(2,1)} %bitcast.135, bf16[128,1024]{1,0:T(8,128)(2,1)} %get-tuple-element.96.half_ref, bf16[512,1024]{1,0:T(8,128)(2,1)} %get-tuple-element.97.rest_0_), custom_call_target="tpu_custom_call" | custom-call | bytes 18750000 | tf_op jit(solution)/shard_map/pallas_call | solution.py:1270
  405.3 1.3 fusion.30
  406.9 2.7 add_convert_fusion.2
  409.6 1.2 convert_element_type.110
  410.9 1.3 constant_dynamic-slice_fusion.4
  412.2 1.3 fusion.38
  413.7 2.7 add_convert_fusion.1.gate_ref
  416.5 4.4 fusion.5
  420.9 27.5 %shard_map.239 = (bf16[512,2048]{1,0:T(8,128)(2,1)}, f32[8,2048]{1,0:T(8,128)}, f32[8,2048]{1,0:T(8,128)}, f32[4,2048]{1,0:T(4,128)}) custom-call(bf16[8,4,128,384]{3,2,1,0:T(8,128)(2,1)} %bitcast.144, bf16[8,4,128,256]{3,2,1,0:T(8,128)(2,1)} %bitcast.145, bf16[4,512,512]{2,1,0:T(8,128)(2,1)} %copy-done.36, f32[4,8,512]{2,1,0:T(8,128)} %convert_select_fusion.tail_ref, ...), custom_call_target="tpu_custom_call" | custom-call | flops 12000000000 | bytes 20000000 | tf_op jit(solution)/shard_map/pallas_call | solution.py:592
  448.4 0.8 reshape.183
  449.2 0.6 pad_maximum_fusion.2.small_ref
  449.8 0.9 add_convert_fusion.4
  450.7 2.7 reduce-scatter.5.cloned.1.call-done
  453.4 0.8 slice.37
  454.3 1.3 collective-permute-start.2
  455.5 1.1 convert_bitcast_fusion.3
  456.7 1.3 copy.44
  458.0 2.0 collective-permute-done.2
  460.4 0.6 convert_dynamic-update-slice_fusion
  461.0 10.2 %convolution_convert_fusion.qkv_ref = bf16[2048,2048]{1,0:T(8,128)(2,1)} fusion(bf16[512,2048]{1,0:T(8,128)(2,1)} %bitcast.131, bf16[512,2048]{1,0:T(8,128)(2,1)} %convert_dynamic-update-slice_fusion), kind=kOutput, calls=%fused_computation.1 | convolution fusion | flops 4299161600 | bytes 12582912 | tf_op jit(solution)/shard_map/dot_general | solution.py:71
  471.3 10.4 %fusion.4.normed_ref = bf16[512,2048]{1,0:T(8,128)(2,1)} fusion(f32[512,2048,1]{1,0,2:T(8,128)S(1)} %copy-done.43, bf16[2048,4,512]{2,1,0:T(4,128)(2,1)} %param.19, bf16[64,4,8,512]{3,2,1,0:T(8,128)(2,1)S(1)} %bitcast.146), kind=kOutput, calls=%fused_computation.7 | convolution fusion | flops 4297064448 | bytes 16777216 | tf_op jit(solution)/shard_map/thc,dhc->td/dot_general | solution.py:1544
  481.7 119.0 %shard_map.240 = (bf16[256,2048]{1,0:T(8,128)(2,1)}, bf16[256,1024]{1,0:T(8,128)(2,1)}, f32[128,2048]{1,0:T(8,128)}, f32[8,104,128]{2,1,0:T(8,128)}, bf16[704,51...) custom-call(bf16[2048,2048]{1,0:T(8,128)(2,1)} %convolution_convert_fusion.qkv_ref, ...), custom_call_target="tpu_custom_call" | custom-call | bytes 31250000 | tf_op jit(solution)/shard_map/pallas_call | solution.py:1356
  600.7 1.1 reduce_sum.59
  601.9 3.8 reshape.193
  605.7 1.3 convert_element_type.117
  607.0 1.4 reshape.195
  608.8 2.9 add_convert_fusion.3
  611.7 3.3 convert_bitcast_fusion.1
  615.0 0.7 constant_dynamic-slice_fusion
  (130 shorter events, 5.2 us)
Async XLA Ops:
  7.2 220.5 %copy-start = (bf16[704,2048]{1,0:T(8,128)(2,1)S(1)}, bf16[704,2048]{1,0:T(8,128)(2,1)}, u32[]{:S(2)}) copy-start(bf16[704,2048]{1,0:T(8,128)(2,1)} %param.27) | copy-start | bytes 8650756
  7.2 132.4 %all-gather.2.cloned.1.call-start = ((), (), s32[]{:S(2)}) async-start(), calls=%async_computation.2 | async-start | bytes 4718592 | tf_op jit(solution)/shard_map/all_gather | solution.py:1408
  7.9 401.7 %reduce-scatter.3.cloned.1.call-start = ((), (), s32[]{:S(2)}) async-start(), calls=%async_computation.3 | async-start | bytes 4718592 | tf_op jit(solution)/shard_map/reduce_scatter | solution.py:1412
  8.7 33.2 %copy-start.27 = (f32[2048]{0:T(1024)}, f32[2048]{0:T(1024)S(1)}, u32[]{:S(2)}) copy-start(f32[2048]{0:T(1024)S(1)} %convert_element_type.92) | copy-start | bytes 24580
  10.0 32.0 %copy-start.32 = (f32[128]{0:T(128)}, f32[128]{0:T(128)S(1)}, u32[]{:S(2)}) copy-start(f32[128]{0:T(128)S(1)} %add_rsqrt_fusion.1) | copy-start | bytes 1540
  12.2 0.9 copy-start.11
  33.3 12.1 %copy-start.30 = (s32[512,4]{0,1:T(4,128)S(1)}, s32[512,4]{0,1:T(4,128)}, u32[]{:S(2)}) copy-start(s32[512,4]{0,1:T(4,128)} %param.28) | copy-start | bytes 24580
  33.3 12.8 %copy-start.31 = (s32[512,4]{0,1:T(4,128)S(1)}, s32[512,4]{0,1:T(4,128)}, u32[]{:S(2)}) copy-start(s32[512,4]{0,1:T(4,128)} %param.29) | copy-start | bytes 24580
  42.0 3.4 copy-start.36
  42.0 13.7 %collective-permute-start = (bf16[4,8,512]{2,1,0:T(8,128)(2,1)S(1)}, bf16[4,8,512]{2,1,0:T(8,128)(2,1)S(1)}, u32[]{:S(2)}, u32[]{:S(2)}) collective-permute-start(bf16[4,8,512]{2,1,0:T(8,128)(2,1)S(1)} %slice.40), channel_id=1, source_target_pairs={{0,1},{1,2},{2,3},{3,4},{4,5},{5,6},{6,7},{8,9},{9,10},{10,11},{11... | collective-permute-start | bytes 98312 | tf_op jit(solution)/shard_map/ppermute | solution.py:28
  46.1 8.4 %copy-start.29 = (bf16[4,4,512]{2,1,0:T(4,128)(2,1)S(1)}, bf16[4,4,512]{2,1,0:T(4,128)(2,1)}, u32[]{:S(2)}) copy-start(bf16[4,4,512]{2,1,0:T(4,128)(2,1)} %param.20) | copy-start | bytes 49156
  46.1 9.0 %copy-start.42 = (bf16[256]{0:T(256)(128)(2,1)S(1)}, bf16[256]{0:T(256)(128)(2,1)}, u32[]{:S(2)}) copy-start(bf16[256]{0:T(256)(128)(2,1)} %param.22) | copy-start | bytes 1540
  46.2 9.6 %copy-start.34 = (bf16[2048]{0:T(1024)(128)(2,1)S(1)}, bf16[2048]{0:T(1024)(128)(2,1)}, u32[]{:S(2)}) copy-start(bf16[2048]{0:T(1024)(128)(2,1)} %param.24) | copy-start | bytes 12292
  139.6 27.1 %collective-permute-start.1 = (bf16[512,1024]{1,0:T(8,128)(2,1)}, bf16[512,1024]{1,0:T(8,128)(2,1)S(1)}, u32[]{:S(2)}, u32[]{:S(2)}) collective-permute-start(bf16[512,1024]{1,0:T(8,128)(2,1)} %get-tuple-element.85), channel_id=1, source_target_pairs={{0,1},{1,0},{2,3},{3,2},{4,5},{5,4},{6,7},{7,6},{8,9},{9,8},{10,11... | collective-permute-start | bytes 3145736 | tf_op jit(solution)/shard_map/ppermute | solution.py:1399
  146.9 17.2 %copy-start.5 = (bf16[128,2048]{1,0:T(8,128)(2,1)S(1)}, bf16[128,2048]{1,0:T(8,128)(2,1)}, u32[]{:S(2)}) copy-start(bf16[128,2048]{1,0:T(8,128)(2,1)} %param.16) | copy-start | bytes 1572868
  165.6 128.5 %copy-start.2 = (f32[128,2048]{1,0:T(8,128)}, f32[128,2048]{1,0:T(8,128)S(1)}, u32[]{:S(2)}) copy-start(f32[128,2048]{1,0:T(8,128)S(1)} %get-tuple-element.157) | copy-start | bytes 3145732
  166.7 51.7 %copy-start.18 = (bf16[512,1024]{1,0:T(8,128)(2,1)}, bf16[512,1024]{1,0:T(8,128)(2,1)S(1)}, u32[]{:S(2)}) copy-start(bf16[512,1024]{1,0:T(8,128)(2,1)S(1)} %collective-permute-done.1) | copy-start | bytes 3145732
  218.4 6.0 copy-start.4
  218.4 6.0 copy-start.39
  224.5 3.2 copy-start.9
  227.7 5.3 copy-start.38
  233.0 3.6 copy-start.15
  233.0 3.6 copy-start.14
  242.0 52.1 %copy-start.12 = (bf16[128,2048]{1,0:T(8,128)(2,1)S(1)}, bf16[128,2048]{1,0:T(8,128)(2,1)}, u32[]{:S(2)}) copy-start(bf16[128,2048]{1,0:T(8,128)(2,1)} %param.17) | copy-start | bytes 1572868
  292.4 4.2 copy-start.13
  301.7 1.2 copy-start.7
  301.7 151.7 %reduce-scatter.5.cloned.1.call-start = ((), (), s32[]{:S(2)}) async-start(), calls=%async_computation.4 | async-start | bytes 2621440 | tf_op jit(solution)/shard_map/reduce_scatter | solution.py:1515
  303.0 0.9 copy-start.10
  330.2 75.0 %copy-start.24 = (bf16[4,128,2048]{2,1,0:T(8,128)(2,1)S(1)}, bf16[4,128,2048]{2,1,0:T(8,128)(2,1)}, u32[]{:S(2)}) copy-start(bf16[4,128,2048]{2,1,0:T(8,128)(2,1)} %get-tuple-element.92) | copy-start | bytes 6291460
  340.8 64.5 %copy-start.41 = (bf16[512,1024]{1,0:T(8,128)(2,1)S(1)}, bf16[512,1024]{1,0:T(8,128)(2,1)}, u32[]{:S(2)}) copy-start(bf16[512,1024]{1,0:T(8,128)(2,1)} %get-tuple-element.85) | copy-start | bytes 3145732
  405.3 1.3 copy-start.19
  405.3 1.5 copy-start.21
  409.6 2.6 copy-start.35
  409.6 2.6 copy-start.16
  412.2 1.3 copy-start.17
  412.2 1.5 copy-start.20
  413.7 2.7 copy-start.37
  420.9 28.9 %copy-start.3 = (f32[128,2048]{1,0:T(8,128)S(1)}, f32[128,2048]{1,0:T(8,128)}, u32[]{:S(2)}) copy-start(f32[128,2048]{1,0:T(8,128)} %copy-done.2) | copy-start | bytes 3145732
  449.8 10.2 %copy-start.26 = (f32[8,2048]{1,0:T(8,128)S(1)}, f32[8,2048]{1,0:T(8,128)}, u32[]{:S(2)}) copy-start(f32[8,2048]{1,0:T(8,128)} %get-tuple-element.111) | copy-start | bytes 196612
  454.3 5.8 collective-permute-start.2
  461.0 10.2 %copy-start.40 = (bf16[512,2048]{1,0:T(8,128)(2,1)S(1)}, bf16[512,2048]{1,0:T(8,128)(2,1)}, u32[]{:S(2)}) copy-start(bf16[512,2048]{1,0:T(8,128)(2,1)} %convert_dynamic-update-slice_fusion) | copy-start | bytes 6291460
  461.0 10.2 %copy-start.43 = (f32[512,2048,1]{1,0,2:T(8,128)S(1)}, f32[512,2048,1]{1,0,2:T(8,128)}, u32[]{:S(2)}) copy-start(f32[512,2048,1]{1,0,2:T(8,128)} %fusion.5) | copy-start | bytes 12582916
  600.7 5.0 copy-start.22
  600.7 6.3 %copy-start.23 = (bf16[256,1024]{1,0:T(8,128)(2,1)S(1)}, bf16[256,1024]{1,0:T(8,128)(2,1)}, u32[]{:S(2)}) copy-start(bf16[256,1024]{1,0:T(8,128)(2,1)} %get-tuple-element.125) | copy-start | bytes 1572868
  601.9 6.6 %copy-start.25 = (f32[104,128]{1,0:T(8,128)}, f32[104,128]{1,0:T(8,128)S(1)}, u32[]{:S(2)}) copy-start(f32[104,128]{1,0:T(8,128)S(1)} %reduce_sum.59) | copy-start | bytes 159748
  601.9 6.6 %copy-start.6 = (bf16[128,2048]{1,0:T(8,128)(2,1)S(1)}, bf16[128,2048]{1,0:T(8,128)(2,1)}, u32[]{:S(2)}) copy-start(bf16[128,2048]{1,0:T(8,128)(2,1)} %param.16) | copy-start | bytes 1572868
  601.9 6.6 %copy-start.8 = (f32[128,2048]{1,0:T(8,128)S(1)}, f32[128,2048]{1,0:T(8,128)}, u32[]{:S(2)}) copy-start(f32[128,2048]{1,0:T(8,128)} %get-tuple-element.122) | copy-start | bytes 3145732
  601.9 6.6 %copy-start.28 = (f32[2048]{0:T(1024)S(1)}, f32[2048]{0:T(1024)}, u32[]{:S(2)}) copy-start(f32[2048]{0:T(1024)} %copy-done.27) | copy-start | bytes 24580
  601.9 6.6 %copy-start.33 = (f32[128]{0:T(128)S(1)}, f32[128]{0:T(128)}, u32[]{:S(2)}) copy-start(f32[128]{0:T(128)} %copy-done.32) | copy-start | bytes 1540
  608.5 3.2 slice-start
  608.8 8.0 %copy-start.1 = (bf16[704,2048]{1,0:T(8,128)(2,1)S(1)}, bf16[704,2048]{1,0:T(8,128)(2,1)}, u32[]{:S(2)}) copy-start(bf16[704,2048]{1,0:T(8,128)(2,1)} %param.27) | copy-start | bytes 8650756
Sparse Core Ops, SparseCore 0:
  10.2 76.2 all-gather.1
  301.8 103.8 reduce-scatter.2
  411.0 42.3 reduce-scatter.4

commit v8 on v7

--- a/solution.py
+++ b/solution.py
@@ -1504,9 +1504,9 @@
     d_core, d_gate_low, gain_out_part, local_grads, grad_end = run_local_backward(
         d_branch, core, gate_pre, gain_head, reach, turn
     )
-    grad_ends, d_mix_side, d_gate_side = gathered_more(
-        grad_end.reshape(-1, DV), d_mix_half, 7, d_gate_low
-    )
+    grad_ends, d_mix_side = gathered_more(grad_end.reshape(-1, DV), d_mix_half, 7)
+    d_gate_low, grad_ends = lax.optimization_barrier((d_gate_low, grad_ends))
+    d_gate_side = swapped(d_gate_low)
     out_half = (
         mm_tn(side_columns(d_mix_all, side, slice_rows), branch) + mm_tn(d_mix_side, branch_side)
     ).astype(bf16)

time: 633 us -> 637 us (level)
  waiting for transfers between devices: 5.45 us -> 38 us
  Pallas kernels: 464 us -> 433 us
    pallas_call x2, Pallas kernels: 114 us -> 81 us  [gathered_more(): link_call(body, number, [ANY] * (2 + len(swaps)), [ANY] * (2 + len(swaps)...]
    reduce_scatter x1, waiting for transfers between devices: 0.01 us -> 18.8 us  [scattered(): lax.psum_scatter(value.astype(bf16), axis, scatter_dimension=dimension, t...]
    ppermute x1 -> x2, waiting for transfers between devices: 0.01 us -> 16.4 us  [swapped(): lax.ppermute(value, 'seq', [(place, place ^ 1) for place in range(count)])]
  transfers between devices with their start and end apart: 6 -> 7, of which waited for: 2 -> 3; matrix products, arithmetic and copies ran while one was open for 10% -> 10% of each run, Pallas kernels for 39% -> 33%
where the time goes in v8:
time: 637 us; the launch traced here: 630 us
  Pallas kernels  433 us (68%)
  matrix products  91.3 us (14%)
  waiting for transfers between devices  38 us (6%)
  other arithmetic  26.7 us (4%)
  local copies, waits for them, and re-layouts  16.9 us (3%)
  between operations  14.7 us (2%)
  starting transfers between devices  8.9 us (1%)
    pallas_call x1, Pallas kernels, scattered_last(): link_call(body, number, [ANY] * 3 + [IN_VMEM] * 2 + [ANY] * len(mlp), [IN...  118 us
    pallas_call x2, Pallas kernels, gathered_more(): link_call(body, number, [ANY] * (2 + len(swaps)), [ANY] * (2 + len(swaps)...  81 us
    pallas_call x1, Pallas kernels, scattered_seq_products(): link_call(body, number, [ANY] * (1 + n_left + n_right), [IN_VMEM] + [ANY]...  56.7 us
    pallas_call x1, Pallas kernels, gathered_seq(): link_call(body, number, [ANY], ANY, shaped((total, rows, width), value.dt...  50.5 us
    pallas_call x2, Pallas kernels, gathered_crossed(): link_call(body, number, [ANY, ANY], [ANY, ANY], [shaped((count, rows, wid...  38.7 us
    dot_general x8, matrix products, mm_tn(): lax.dot_general(left, right, (((0,), (0,)), ((), ())), preferred_element_...  33.6 us
    pallas_call x1, Pallas kernels, run_finish_backward(): kernel_call(finish_backward, heads, [whole(ends.shape), whole(grad_ends.s...  27.5 us
    pallas_call x1, Pallas kernels, run_local_forward(): kernel_call(local_forward, heads, [by_head((rows, INNER)), by_head((8, IN...  22.9 us
  transfers between devices with their start and end apart: 7, of which 3 were waited for; matrix products, arithmetic and copies ran while one was open for 10% of the time, Pallas kernels for 33%

profile of v8, /device:TPU:0, one launch (start us, length us, event | category | flops | bytes accessed | tf_op | source)
XLA Modules:
  0.0 629.9 jit_solution(4441412983704774260)
XLA Ops:
  7.2 0.7 all-gather.2.cloned.1.call-update
  8.0 0.8 convert_element_type.92
  8.7 1.2 fusion.27
  10.0 2.2 convert_multiply_fusion
  12.2 0.8 pad_maximum_fusion.half_ref
  13.1 20.2 %shard_map.229 = (bf16[4,128,2048]{2,1,0:T(8,128)(2,1)}, bf16[128,1024]{1,0:T(8,128)(2,1)}) custom-call(bf16[128,2048]{1,0:T(8,128)(2,1)} %copy-done.11, bf16[128,1024]{1,0:T(8,128)(2,1)} %pad_maximum_fusion.half_ref), custom_call_target="tpu_custom_call" | custom-call | bytes 7500000 | tf_op jit(solution)/shard_map/pallas_call | solution.py:1032
  33.3 8.7 %convert_bitcast_fusion.mixed_ref = bf16[4,512,512]{2,1,0:T(8,128)(2,1)S(1)} fusion(bf16[512,2048,1]{1,0,2:T(8,128)(2,1)} %bitcast.127, bf16[2048,4,512]{2,1,0:T(4,128)(2,1)} %param.19), kind=kOutput, calls=%fused_computation.33 | convolution fusion | flops 4296015872 | bytes 12582912 | tf_op jit(solution)/shard_map/td,dhc->htc/dot_general | solution.py:1456
  42.0 3.4 collective-permute-start
  46.2 6.9 %fusion.24.gate_ref = f32[4,512,256]{2,1,0:T(8,128)} fusion(bf16[512,2048,1]{1,0,2:T(8,128)(2,1)} %bitcast.128, bf16[2048,4,256]{2,1,0:T(4,128)(2,1)} %param.21), kind=kOutput, calls=%fused_computation.34 | convolution fusion | flops 2147483648 | bytes 8388608 | tf_op jit(solution)/shard_map/td,dhv->htv/dot_general | solution.py:1466
  53.2 0.7 pad.14.clone.columns_ref
  55.8 0.7 convert_select_fusion.tail_ref
  56.5 22.9 %shard_map.230 = (bf16[4,2,256,256]{3,2,1,0:T(8,128)(2,1)}, bf16[4,2,256,256]{3,2,1,0:T(8,128)(2,1)}, bf16[4,512,384]{2,1,0:T(8,128)(2,1)}, bf16[4,512,128]{2,1,...) custom-call(bf16[4,512,512]{2,1,0:T(8,128)(2,1)} %copy-done.34, ...), custom_call_target="tpu_custom_call" | custom-call | flops 12000000000 | bytes 20000000 | tf_op jit(solution)/shard_map/pallas_call | solution.py:485
  79.4 44.2 %shard_map.231 = (bf16[8,512,384]{2,1,0:T(8,128)(2,1)}, bf16[4,128,1024]{2,1,0:T(8,128)(2,1)}) custom-call(bf16[512,384]{1,0:T(8,128)(2,1)} %bitcast.133, bf16[128,1024]{1,0:T(8,128)(2,1)} %get-tuple-element.80.half_ref), custom_call_target="tpu_custom_call" | custom-call | bytes 18750000 | tf_op jit(solution)/shard_map/pallas_call | solution.py:1270
  123.6 10.3 %shard_map.232 = (bf16[4,8,128,256]{3,2,1,0:T(8,128)(2,1)}, f32[512,1024]{1,0:T(8,128)}, bf16[512,1024]{1,0:T(8,128)(2,1)}) custom-call(bf16[8,4,128,384]{3,2,1,0:T(8,128)(2,1)} %bitcast.142, bf16[4,8,128,384]{3,2,1,0:T(8,128)(2,1)} %get-tuple-element.82.local_ref, bf16[4,512,128]{2,1,0:T(8,128)(2,1)} %get-tuple-element.83.reach_ref, ...), custom_call_target="tpu_custom_call" | custom-call | flops 3000000000 | bytes 20000000 | tf_op jit(solution)/shard_map/pallas_call | solution.py:528
  133.9 2.6 collective-permute-start.1
  136.5 6.2 convolution_convert_fusion.2.source
  142.7 17.0 %shard_map.233 = f32[128,2048]{1,0:T(8,128)} custom-call(bf16[512,2048]{1,0:T(8,128)(2,1)} %convolution_convert_fusion.2.source), custom_call_target="tpu_custom_call" | custom-call | bytes 7500000 | tf_op jit(solution)/shard_map/pallas_call | solution.py:1105
  159.7 1.4 multiply_reduce_fusion.3
  161.2 1.1 multiply_convert_fusion.own_ref
  162.3 50.5 %shard_map.234 = bf16[8,128,2048]{2,1,0:T(8,128)(2,1)} custom-call(bf16[128,2048]{1,0:T(8,128)(2,1)} %multiply_convert_fusion.own_ref), custom_call_target="tpu_custom_call" | custom-call | bytes 15000000 | tf_op jit(solution)/shard_map/pallas_call | solution.py:1055
  212.8 6.0 fusion.57
  218.9 3.2 fusion.58
  222.1 5.3 fusion.13
  227.4 3.5 fusion.59
  231.0 5.4 add_convert_fusion.source
  236.4 56.7 %shard_map.235 = (f32[128,2048]{1,0:T(8,128)}, bf16[704,2048]{1,0:T(8,128)(2,1)}, bf16[704,2048]{1,0:T(8,128)(2,1)}, bf16[704,2048]{1,0:T(8,128)(2,1)}) custom-call(bf16[1024,2048]{1,0:T(8,128)(2,1)} %add_convert_fusion.source, bf16[704,1024]{1,0:T(8,128)(2,1)} %copy-done.15, bf16[704,1024]{1,0:T(8,128)(2,1)} %copy-done.14, ...), custom_call_target="tpu_custom_call" | custom-call | bytes 15000000 | tf_op jit(solution)/shard_map/pallas_call | solution.py:1220
  293.1 1.7 multiply_reduce_fusion.1
  294.8 2.5 multiply_add_fusion
  297.3 5.1 convolution_convert_fusion.1
  302.5 1.1 copy-done.7
  303.8 0.8 pad_maximum_fusion.1.half_ref
  304.6 18.5 %shard_map.236 = (bf16[4,128,2048]{2,1,0:T(8,128)(2,1)}, bf16[128,1024]{1,0:T(8,128)(2,1)}) custom-call(bf16[128,2048]{1,0:T(8,128)(2,1)} %copy-done.10, bf16[128,1024]{1,0:T(8,128)(2,1)} %pad_maximum_fusion.1.half_ref), custom_call_target="tpu_custom_call" | custom-call | bytes 7500000 | tf_op jit(solution)/shard_map/pallas_call | solution.py:1032
  323.1 6.5 %fusion.60.d_branch_ref = f32[512,1024]{1,0:T(8,128)} fusion(bf16[512,2048]{1,0:T(8,128)(2,1)} %bitcast.131, bf16[1024,2048]{1,0:T(8,128)(2,1)} %bitcast.141), kind=kOutput, calls=%fused_computation.122 | convolution fusion | flops 2147483648 | bytes 8388608 | tf_op jit(solution)/shard_map/dot_general | solution.py:67
  329.6 10.6 %shard_map.237 = (bf16[512,1024]{1,0:T(8,128)(2,1)}, bf16[512,1024]{1,0:T(8,128)(2,1)}, f32[1,256]{1,0:T(1,128)}, bf16[4,8,128,384]{3,2,1,0:T(8,128)(2,1)}, bf16[4,128,256]{2,1,0:T(8,128)(2,1)}) custom-call(f32[512,1024]{1,0:T(8,128)} %fusion.60.d_branch_ref, f32[512,1024]{1,0:T(8,128)} %get-tuple-element.94.core_ref, f32[4,512,256]{2,1,0:T(8,128)} %fusion.24.gate_ref, ...), custom_call_target="tpu_custom_call" | custom-call | flops 4000000000 | bytes 20000000 | tf_op jit(solution)/shard_map/pallas_call | solution.py:554
  340.2 36.8 %shard_map.238 = (bf16[8,512,256]{2,1,0:T(8,128)(2,1)}, bf16[4,128,1024]{2,1,0:T(8,128)(2,1)}) custom-call(bf16[512,256]{1,0:T(8,128)(2,1)} %bitcast.134, bf16[128,1024]{1,0:T(8,128)(2,1)} %get-tuple-element.97.half_ref), custom_call_target="tpu_custom_call" | custom-call | bytes 18750000 | tf_op jit(solution)/shard_map/pallas_call | solution.py:1270
  377.1 1.3 fusion.30
  378.7 2.7 add_convert_fusion.2
  381.4 18.8 %reduce-scatter.3.cloned.1.call-done = bf16[128,2048]{1,0:T(8,128)(2,1)} async-done(((bf16[1024,2048]{1,0:T(8,128)(2,1)}), bf16[128,2048]{1,0:T(8,128)(2,1)}) %reduce-scatter.3.cloned.1.call-update) | async-done | bytes 524304 | tf_op jit(solution)/shard_map/reduce_scatter | solution.py:1412
  400.2 1.1 convert_element_type.110
  401.4 1.3 constant_dynamic-slice_fusion.4
  402.7 1.5 collective-permute-start.3
  404.2 2.7 fusion.38
  407.0 4.4 fusion.5
  411.4 16.4 %collective-permute-done.3 = bf16[512,1024]{1,0:T(8,128)(2,1)S(1)} collective-permute-done((bf16[512,1024]{1,0:T(8,128)(2,1)}, bf16[512,1024]{1,0:T(8,128)(2,1)S(1)}, u32[]{:S(2)}, u32[]{:S(2)}) %collective-permute-start.3) | collective-permute-done | bytes 1048608 | tf_op jit(solution)/shard_map/ppermute | solution.py:1399
  427.9 2.6 add_convert_fusion.1.gate_ref
  430.5 27.5 %shard_map.239 = (bf16[512,2048]{1,0:T(8,128)(2,1)}, f32[8,2048]{1,0:T(8,128)}, f32[8,2048]{1,0:T(8,128)}, f32[4,2048]{1,0:T(4,128)}) custom-call(bf16[8,4,128,384]{3,2,1,0:T(8,128)(2,1)} %bitcast.143, bf16[8,4,128,256]{3,2,1,0:T(8,128)(2,1)} %bitcast.144, bf16[4,512,512]{2,1,0:T(8,128)(2,1)} %copy-done.34, f32[4,8,512]{2,1,0:T(8,128)} %convert_select_fusion.tail_ref, ...), custom_call_target="tpu_custom_call" | custom-call | flops 12000000000 | bytes 20000000 | tf_op jit(solution)/shard_map/pallas_call | solution.py:592
  458.0 0.8 reshape.183
  458.8 0.6 pad_maximum_fusion.2.small_ref
  459.4 0.9 add_convert_fusion.4
  460.3 0.8 slice.37
  461.2 1.3 collective-permute-start.2
  462.5 1.1 convert_bitcast_fusion.3
  463.6 1.3 copy.44
  464.9 2.0 collective-permute-done.2
  468.1 10.2 %convolution_convert_fusion.qkv_ref = bf16[2048,2048]{1,0:T(8,128)(2,1)} fusion(bf16[512,2048]{1,0:T(8,128)(2,1)} %bitcast.130, bf16[512,2048]{1,0:T(8,128)(2,1)} %convert_dynamic-update-slice_fusion), kind=kOutput, calls=%fused_computation.1 | convolution fusion | flops 4299161600 | bytes 12582912 | tf_op jit(solution)/shard_map/dot_general | solution.py:71
  478.3 10.4 %fusion.4.normed_ref = bf16[512,2048]{1,0:T(8,128)(2,1)} fusion(f32[512,2048,1]{1,0,2:T(8,128)S(1)} %copy-done.42, bf16[2048,4,512]{2,1,0:T(4,128)(2,1)} %param.19, bf16[64,4,8,512]{3,2,1,0:T(8,128)(2,1)S(1)} %bitcast.145), kind=kOutput, calls=%fused_computation.7 | convolution fusion | flops 4297064448 | bytes 16777216 | tf_op jit(solution)/shard_map/thc,dhc->td/dot_general | solution.py:1544
  488.7 118.2 %shard_map.240 = (bf16[256,2048]{1,0:T(8,128)(2,1)}, bf16[256,1024]{1,0:T(8,128)(2,1)}, f32[128,2048]{1,0:T(8,128)}, f32[8,104,128]{2,1,0:T(8,128)}, bf16[704,51...) custom-call(bf16[2048,2048]{1,0:T(8,128)(2,1)} %convolution_convert_fusion.qkv_ref, ...), custom_call_target="tpu_custom_call" | custom-call | bytes 31250000 | tf_op jit(solution)/shard_map/pallas_call | solution.py:1356
  607.0 1.1 reduce_sum.59
  608.2 3.8 reshape.193
  612.0 1.3 convert_element_type.117
  613.3 1.4 reshape.195
  615.1 2.9 add_convert_fusion.3
  618.0 3.3 convert_bitcast_fusion.1
  621.3 0.7 constant_dynamic-slice_fusion
  (130 shorter events, 6.3 us)
Async XLA Ops:
  7.2 214.9 %copy-start = (bf16[704,2048]{1,0:T(8,128)(2,1)S(1)}, bf16[704,2048]{1,0:T(8,128)(2,1)}, u32[]{:S(2)}) copy-start(bf16[704,2048]{1,0:T(8,128)(2,1)} %param.27) | copy-start | bytes 8650756
  7.2 126.8 %all-gather.2.cloned.1.call-start = ((), (), s32[]{:S(2)}) async-start(), calls=%async_computation.2 | async-start | bytes 4718592 | tf_op jit(solution)/shard_map/all_gather | solution.py:1408
  7.9 392.3 %reduce-scatter.3.cloned.1.call-start = ((), (), s32[]{:S(2)}) async-start(), calls=%async_computation.3 | async-start | bytes 4718592 | tf_op jit(solution)/shard_map/reduce_scatter | solution.py:1412
  8.7 33.2 %copy-start.25 = (f32[2048]{0:T(1024)}, f32[2048]{0:T(1024)S(1)}, u32[]{:S(2)}) copy-start(f32[2048]{0:T(1024)S(1)} %convert_element_type.92) | copy-start | bytes 24580
  10.0 32.0 %copy-start.30 = (f32[128]{0:T(128)}, f32[128]{0:T(128)S(1)}, u32[]{:S(2)}) copy-start(f32[128]{0:T(128)S(1)} %add_rsqrt_fusion.1) | copy-start | bytes 1540
  12.2 0.9 copy-start.11
  33.3 12.1 %copy-start.28 = (s32[512,4]{0,1:T(4,128)S(1)}, s32[512,4]{0,1:T(4,128)}, u32[]{:S(2)}) copy-start(s32[512,4]{0,1:T(4,128)} %param.28) | copy-start | bytes 24580
  33.3 12.8 %copy-start.29 = (s32[512,4]{0,1:T(4,128)S(1)}, s32[512,4]{0,1:T(4,128)}, u32[]{:S(2)}) copy-start(s32[512,4]{0,1:T(4,128)} %param.29) | copy-start | bytes 24580
  42.0 3.4 copy-start.34
  42.0 13.7 %collective-permute-start = (bf16[4,8,512]{2,1,0:T(8,128)(2,1)S(1)}, bf16[4,8,512]{2,1,0:T(8,128)(2,1)S(1)}, u32[]{:S(2)}, u32[]{:S(2)}) collective-permute-start(bf16[4,8,512]{2,1,0:T(8,128)(2,1)S(1)} %slice.40), channel_id=1, source_target_pairs={{0,1},{1,2},{2,3},{3,4},{4,5},{5,6},{6,7},{8,9},{9,10},{10,11},{11... | collective-permute-start | bytes 98312 | tf_op jit(solution)/shard_map/ppermute | solution.py:28
  46.1 8.4 %copy-start.27 = (bf16[4,4,512]{2,1,0:T(4,128)(2,1)S(1)}, bf16[4,4,512]{2,1,0:T(4,128)(2,1)}, u32[]{:S(2)}) copy-start(bf16[4,4,512]{2,1,0:T(4,128)(2,1)} %param.20) | copy-start | bytes 49156
  46.1 9.0 %copy-start.41 = (bf16[256]{0:T(256)(128)(2,1)S(1)}, bf16[256]{0:T(256)(128)(2,1)}, u32[]{:S(2)}) copy-start(bf16[256]{0:T(256)(128)(2,1)} %param.22) | copy-start | bytes 1540
  46.2 9.6 %copy-start.32 = (bf16[2048]{0:T(1024)(128)(2,1)S(1)}, bf16[2048]{0:T(1024)(128)(2,1)}, u32[]{:S(2)}) copy-start(bf16[2048]{0:T(1024)(128)(2,1)} %param.24) | copy-start | bytes 12292
  133.9 28.3 %collective-permute-start.1 = (bf16[512,1024]{1,0:T(8,128)(2,1)}, bf16[512,1024]{1,0:T(8,128)(2,1)S(1)}, u32[]{:S(2)}, u32[]{:S(2)}) collective-permute-start(bf16[512,1024]{1,0:T(8,128)(2,1)} %get-tuple-element.86), channel_id=1, source_target_pairs={{0,1},{1,0},{2,3},{3,2},{4,5},{5,4},{6,7},{7,6},{8,9},{9,8},{10,11... | collective-permute-start | bytes 3145736 | tf_op jit(solution)/shard_map/ppermute | solution.py:1399
  142.7 17.0 %copy-start.5 = (bf16[128,2048]{1,0:T(8,128)(2,1)S(1)}, bf16[128,2048]{1,0:T(8,128)(2,1)}, u32[]{:S(2)}) copy-start(bf16[128,2048]{1,0:T(8,128)(2,1)} %param.16) | copy-start | bytes 1572868
  161.1 133.7 %copy-start.2 = (f32[128,2048]{1,0:T(8,128)}, f32[128,2048]{1,0:T(8,128)S(1)}, u32[]{:S(2)}) copy-start(f32[128,2048]{1,0:T(8,128)S(1)} %get-tuple-element.159) | copy-start | bytes 3145732
  162.3 50.6 %copy-start.17 = (bf16[512,1024]{1,0:T(8,128)(2,1)}, bf16[512,1024]{1,0:T(8,128)(2,1)S(1)}, u32[]{:S(2)}) copy-start(bf16[512,1024]{1,0:T(8,128)(2,1)S(1)} %collective-permute-done.1) | copy-start | bytes 3145732
  212.8 6.0 copy-start.4
  212.8 6.0 copy-start.37
  218.9 3.2 copy-start.9
  222.1 5.3 copy-start.36
  227.4 3.6 copy-start.15
  227.4 3.6 copy-start.14
  236.4 58.4 %copy-start.12 = (bf16[128,2048]{1,0:T(8,128)(2,1)S(1)}, bf16[128,2048]{1,0:T(8,128)(2,1)}, u32[]{:S(2)}) copy-start(bf16[128,2048]{1,0:T(8,128)(2,1)} %param.17) | copy-start | bytes 1572868
  293.1 4.2 copy-start.13
  302.4 1.2 copy-start.7
  302.5 157.9 %reduce-scatter.5.cloned.1.call-start = ((), (), s32[]{:S(2)}) async-start(), calls=%async_computation.4 | async-start | bytes 2621440 | tf_op jit(solution)/shard_map/reduce_scatter | solution.py:1515
  303.7 0.9 copy-start.10
  329.6 47.3 %copy-start.22 = (bf16[4,128,2048]{2,1,0:T(8,128)(2,1)S(1)}, bf16[4,128,2048]{2,1,0:T(8,128)(2,1)}, u32[]{:S(2)}) copy-start(bf16[4,128,2048]{2,1,0:T(8,128)(2,1)} %get-tuple-element.93) | copy-start | bytes 6291460
  329.6 47.5 %copy-start.39 = (bf16[512,1024]{1,0:T(8,128)(2,1)S(1)}, bf16[512,1024]{1,0:T(8,128)(2,1)}, u32[]{:S(2)}) copy-start(bf16[512,1024]{1,0:T(8,128)(2,1)} %get-tuple-element.86) | copy-start | bytes 3145732
  377.1 1.3 copy-start.18
  377.1 1.5 copy-start.19
  381.4 22.8 %copy-start.33 = (f32[1,256]{1,0:T(1,128)S(1)}, f32[1,256]{1,0:T(1,128)}, u32[]{:S(2)}) copy-start(f32[1,256]{1,0:T(1,128)} %get-tuple-element.119) | copy-start | bytes 3076
  402.7 25.2 %collective-permute-start.3 = (bf16[512,1024]{1,0:T(8,128)(2,1)}, bf16[512,1024]{1,0:T(8,128)(2,1)S(1)}, u32[]{:S(2)}, u32[]{:S(2)}) collective-permute-start(bf16[512,1024]{1,0:T(8,128)(2,1)} %get-tuple-element.117), channel_id=1, source_target_pairs={{0,1},{1,0},{2,3},{3,2},{4,5},{5,4},{6,7},{7,6},{8,9},{9,8},{10,11... | collective-permute-start | bytes 3145736 | tf_op jit(solution)/shard_map/ppermute | solution.py:1399
  404.2 2.7 copy-start.35
  404.2 2.8 copy-start.40
  407.0 20.9 %copy-start.16 = (bf16[4,128,1024]{2,1,0:T(8,128)(2,1)S(1)}, bf16[4,128,1024]{2,1,0:T(8,128)(2,1)}, u32[]{:S(2)}) copy-start(bf16[4,128,1024]{2,1,0:T(8,128)(2,1)} %get-tuple-element.118) | copy-start | bytes 3145732
  430.5 28.9 %copy-start.3 = (f32[128,2048]{1,0:T(8,128)S(1)}, f32[128,2048]{1,0:T(8,128)}, u32[]{:S(2)}) copy-start(f32[128,2048]{1,0:T(8,128)} %copy-done.2) | copy-start | bytes 3145732
  459.4 7.6 %copy-start.24 = (f32[8,2048]{1,0:T(8,128)S(1)}, f32[8,2048]{1,0:T(8,128)}, u32[]{:S(2)}) copy-start(f32[8,2048]{1,0:T(8,128)} %get-tuple-element.113) | copy-start | bytes 196612
  461.2 5.8 collective-permute-start.2
  468.1 10.2 %copy-start.38 = (bf16[512,2048]{1,0:T(8,128)(2,1)S(1)}, bf16[512,2048]{1,0:T(8,128)(2,1)}, u32[]{:S(2)}) copy-start(bf16[512,2048]{1,0:T(8,128)(2,1)} %convert_dynamic-update-slice_fusion) | copy-start | bytes 6291460
  468.1 10.2 %copy-start.42 = (f32[512,2048,1]{1,0,2:T(8,128)S(1)}, f32[512,2048,1]{1,0,2:T(8,128)}, u32[]{:S(2)}) copy-start(f32[512,2048,1]{1,0,2:T(8,128)} %fusion.5) | copy-start | bytes 12582916
  607.0 5.0 copy-start.20
  607.0 6.3 %copy-start.21 = (bf16[256,1024]{1,0:T(8,128)(2,1)S(1)}, bf16[256,1024]{1,0:T(8,128)(2,1)}, u32[]{:S(2)}) copy-start(bf16[256,1024]{1,0:T(8,128)(2,1)} %get-tuple-element.127) | copy-start | bytes 1572868
  608.1 6.6 %copy-start.23 = (f32[104,128]{1,0:T(8,128)}, f32[104,128]{1,0:T(8,128)S(1)}, u32[]{:S(2)}) copy-start(f32[104,128]{1,0:T(8,128)S(1)} %reduce_sum.59) | copy-start | bytes 159748
  608.2 6.6 %copy-start.6 = (bf16[128,2048]{1,0:T(8,128)(2,1)S(1)}, bf16[128,2048]{1,0:T(8,128)(2,1)}, u32[]{:S(2)}) copy-start(bf16[128,2048]{1,0:T(8,128)(2,1)} %param.16) | copy-start | bytes 1572868
  608.2 6.6 %copy-start.8 = (f32[128,2048]{1,0:T(8,128)S(1)}, f32[128,2048]{1,0:T(8,128)}, u32[]{:S(2)}) copy-start(f32[128,2048]{1,0:T(8,128)} %get-tuple-element.124) | copy-start | bytes 3145732
  608.2 6.6 %copy-start.26 = (f32[2048]{0:T(1024)S(1)}, f32[2048]{0:T(1024)}, u32[]{:S(2)}) copy-start(f32[2048]{0:T(1024)} %copy-done.25) | copy-start | bytes 24580
  608.2 6.6 %copy-start.31 = (f32[128]{0:T(128)S(1)}, f32[128]{0:T(128)}, u32[]{:S(2)}) copy-start(f32[128]{0:T(128)} %copy-done.30) | copy-start | bytes 1540
  614.8 3.2 slice-start
  615.1 8.0 %copy-start.1 = (bf16[704,2048]{1,0:T(8,128)(2,1)S(1)}, bf16[704,2048]{1,0:T(8,128)(2,1)}, u32[]{:S(2)}) copy-start(bf16[704,2048]{1,0:T(8,128)(2,1)} %param.27) | copy-start | bytes 8650756
Sparse Core Ops, SparseCore 0:
  10.2 77.4 all-gather.1
  302.6 97.5 reduce-scatter.2
  402.6 43.6 reduce-scatter.4

commit v9 on v8

--- a/solution.py
+++ b/solution.py
@@ -1510,17 +1510,6 @@
     out_half = (
         mm_tn(side_columns(d_mix_all, side, slice_rows), branch) + mm_tn(d_mix_side, branch_side)
     ).astype(bf16)
-    out_half, grad_ends, mlp_out = lax.optimization_barrier((out_half, grad_ends, mlp_out))
-    output = (middle + mlp_out).astype(bf16)
-    grad_out_s = lax.psum_scatter(
-        out_half,
-        "seq",
-        scatter_dimension=0,
-        axis_index_groups=[
-            [place * SIDE + across for place in range(seq_count // SIDE)] for across in range(SIDE)
-        ],
-        tiled=True,
-    )
     grad_ends = grad_ends.reshape(-1, heads, DK, DV)
     d_mixed, d_tail, d_lead, grad_conv = run_finish_backward(
         ends,
@@ -1537,7 +1526,19 @@
         d_core,
         local_grads,
     )
-    d_lead, grad_out_s = lax.optimization_barrier((d_lead, grad_out_s))
+    out_half, mlp_out, d_lead, d_gate_side = lax.optimization_barrier(
+        (out_half, mlp_out, d_lead, d_gate_side)
+    )
+    output = (middle + mlp_out).astype(bf16)
+    grad_out_s = lax.psum_scatter(
+        out_half,
+        "seq",
+        scatter_dimension=0,
+        axis_index_groups=[
+            [place * SIDE + across for place in range(seq_count // SIDE)] for across in range(SIDE)
+        ],
+        tiled=True,
+    )
     from_next = passed_along(d_lead[:lead_rows], "seq", -1)
     d_tail = d_tail.at[8 - lead_rows :].add(from_next).astype(bf16)
     d_mixed = lax.dynamic_update_slice(d_mixed, d_tail, (span_rows - 8, 0))
@@ -1558,6 +1559,7 @@
         + mm_tn(normed_side, d_gate_side)
     ).astype(bf16)
 
+    grad_qkv, grad_out_s = lax.optimization_barrier((grad_qkv, grad_out_s))
     gains = jnp.concatenate([jnp.zeros_like(gain_two_part), gain_two_part, gain_out_part.reshape(-1)])
     gain_rows = -(-gains.shape[0] // 1024) * 8
     gains = jnp.pad(gains, (0, gain_rows * 128 - gains.shape[0])).reshape(gain_rows, 128)

time: 637 us -> 629 us (0.987)
  waiting for transfers between devices: 38 us -> 21.6 us
    reduce_scatter x1, waiting for transfers between devices: 18.8 us -> 0.01 us  [scattered(): lax.psum_scatter(value.astype(bf16), axis, scatter_dimension=dimension, t...]
    reduce_scatter x1, waiting for transfers between devices: 0.01 us -> 16.5 us  [on_device(): lax.psum_scatter(out_half, 'seq', scatter_dimension=0, axis_index_groups=...]
    ppermute x2, waiting for transfers between devices: 16.4 us -> 4.32 us  [swapped(): lax.ppermute(value, 'seq', [(place, place ^ 1) for place in range(count)])]
  transfers between devices with their start and end apart: 7 -> 7, of which waited for: 3 -> 2; matrix products, arithmetic and copies ran while one was open for 10% -> 14% of each run, Pallas kernels for 33% -> 34%
where the time goes in v9:
time: 629 us; the launch traced here: 619 us
  Pallas kernels  433 us (69%)
  matrix products  95 us (15%)
  other arithmetic  28.2 us (4%)
  waiting for transfers between devices  21.6 us (3%)
  local copies, waits for them, and re-layouts  18.3 us (3%)
  between operations  14.6 us (2%)
  starting transfers between devices  8.39 us (1%)
    pallas_call x1, Pallas kernels, scattered_last(): link_call(body, number, [ANY] * 3 + [IN_VMEM] * 2 + [ANY] * len(mlp), [IN...  118 us
    pallas_call x2, Pallas kernels, gathered_more(): link_call(body, number, [ANY] * (2 + len(swaps)), [ANY] * (2 + len(swaps)...  80.9 us
    pallas_call x1, Pallas kernels, scattered_seq_products(): link_call(body, number, [ANY] * (1 + n_left + n_right), [IN_VMEM] + [ANY]...  56.7 us
    pallas_call x1, Pallas kernels, gathered_seq(): link_call(body, number, [ANY], ANY, shaped((total, rows, width), value.dt...  50.5 us
    pallas_call x2, Pallas kernels, gathered_crossed(): link_call(body, number, [ANY, ANY], [ANY, ANY], [shaped((count, rows, wid...  38.8 us
    dot_general x8, matrix products, mm_tn(): lax.dot_general(left, right, (((0,), (0,)), ((), ())), preferred_element_...  35 us
    pallas_call x1, Pallas kernels, run_finish_backward(): kernel_call(finish_backward, heads, [whole(ends.shape), whole(grad_ends.s...  27.4 us
    pallas_call x1, Pallas kernels, run_local_forward(): kernel_call(local_forward, heads, [by_head((rows, INNER)), by_head((8, IN...  22.9 us
  transfers between devices with their start and end apart: 7, of which 2 were waited for; matrix products, arithmetic and copies ran while one was open for 14% of the time, Pallas kernels for 34%

profile of v9, /device:TPU:0, one launch (start us, length us, event | category | flops | bytes accessed | tf_op | source)
XLA Modules:
  0.0 619.4 jit_solution(1992047676807790787)
XLA Ops:
  7.2 0.7 all-gather.2.cloned.1.call-update
  8.0 0.8 convert_element_type.92
  8.7 1.2 fusion.27
  10.0 2.2 convert_multiply_fusion
  12.2 0.8 pad_maximum_fusion.half_ref
  13.1 20.2 %shard_map.229 = (bf16[4,128,2048]{2,1,0:T(8,128)(2,1)}, bf16[128,1024]{1,0:T(8,128)(2,1)}) custom-call(bf16[128,2048]{1,0:T(8,128)(2,1)} %copy-done.11, bf16[128,1024]{1,0:T(8,128)(2,1)} %pad_maximum_fusion.half_ref), custom_call_target="tpu_custom_call" | custom-call | bytes 7500000 | tf_op jit(solution)/shard_map/pallas_call | solution.py:1032
  33.3 8.7 %convert_bitcast_fusion.mixed_ref = bf16[4,512,512]{2,1,0:T(8,128)(2,1)S(1)} fusion(bf16[512,2048,1]{1,0,2:T(8,128)(2,1)} %bitcast.127, bf16[2048,4,512]{2,1,0:T(4,128)(2,1)} %param.19), kind=kOutput, calls=%fused_computation.33 | convolution fusion | flops 4296015872 | bytes 12582912 | tf_op jit(solution)/shard_map/td,dhc->htc/dot_general | solution.py:1456
  42.0 3.4 collective-permute-start
  46.2 6.9 %fusion.24.gate_ref = f32[4,512,256]{2,1,0:T(8,128)} fusion(bf16[512,2048,1]{1,0,2:T(8,128)(2,1)} %bitcast.128, bf16[2048,4,256]{2,1,0:T(4,128)(2,1)} %param.21), kind=kOutput, calls=%fused_computation.34 | convolution fusion | flops 2147483648 | bytes 8388608 | tf_op jit(solution)/shard_map/td,dhv->htv/dot_general | solution.py:1466
  53.2 0.7 pad.14.clone.columns_ref
  54.6 0.6 copy.48
  55.8 0.7 convert_select_fusion.tail_ref
  56.5 22.9 %shard_map.230 = (bf16[4,2,256,256]{3,2,1,0:T(8,128)(2,1)}, bf16[4,2,256,256]{3,2,1,0:T(8,128)(2,1)}, bf16[4,512,384]{2,1,0:T(8,128)(2,1)}, bf16[4,512,128]{2,1,...) custom-call(bf16[4,512,512]{2,1,0:T(8,128)(2,1)} %copy-done.33, ...), custom_call_target="tpu_custom_call" | custom-call | flops 12000000000 | bytes 20000000 | tf_op jit(solution)/shard_map/pallas_call | solution.py:485
  79.4 44.2 %shard_map.231 = (bf16[8,512,384]{2,1,0:T(8,128)(2,1)}, bf16[4,128,1024]{2,1,0:T(8,128)(2,1)}) custom-call(bf16[512,384]{1,0:T(8,128)(2,1)} %bitcast.133, bf16[128,1024]{1,0:T(8,128)(2,1)} %get-tuple-element.81.half_ref), custom_call_target="tpu_custom_call" | custom-call | bytes 18750000 | tf_op jit(solution)/shard_map/pallas_call | solution.py:1270
  123.6 10.4 %shard_map.232 = (bf16[4,8,128,256]{3,2,1,0:T(8,128)(2,1)}, f32[512,1024]{1,0:T(8,128)}, bf16[512,1024]{1,0:T(8,128)(2,1)}) custom-call(bf16[8,4,128,384]{3,2,1,0:T(8,128)(2,1)} %bitcast.142, bf16[4,8,128,384]{3,2,1,0:T(8,128)(2,1)} %get-tuple-element.83.local_ref, bf16[4,512,128]{2,1,0:T(8,128)(2,1)} %get-tuple-element.84.reach_ref, ...), custom_call_target="tpu_custom_call" | custom-call | flops 3000000000 | bytes 20000000 | tf_op jit(solution)/shard_map/pallas_call | solution.py:528
  134.0 2.6 collective-permute-start.1
  136.6 6.2 %convolution_convert_fusion.2.source = bf16[512,2048]{1,0:T(8,128)(2,1)} fusion(bf16[512,1024]{1,0:T(8,128)(2,1)} %get-tuple-element.87, bf16[1024,2048]{1,0:T(8,128)(2,1)} %bitcast.140), kind=kOutput, calls=%fused_computation.15 | convolution fusion | flops 2148532224 | bytes 7340032 | tf_op jit(solution)/shard_map/dot_general | solution.py:63
  142.8 16.9 %shard_map.233 = f32[128,2048]{1,0:T(8,128)} custom-call(bf16[512,2048]{1,0:T(8,128)(2,1)} %convolution_convert_fusion.2.source), custom_call_target="tpu_custom_call" | custom-call | bytes 7500000 | tf_op jit(solution)/shard_map/pallas_call | solution.py:1105
  159.7 1.4 multiply_reduce_fusion.3
  161.1 1.1 multiply_convert_fusion.own_ref
  162.3 50.5 %shard_map.234 = bf16[8,128,2048]{2,1,0:T(8,128)(2,1)} custom-call(bf16[128,2048]{1,0:T(8,128)(2,1)} %multiply_convert_fusion.own_ref), custom_call_target="tpu_custom_call" | custom-call | bytes 15000000 | tf_op jit(solution)/shard_map/pallas_call | solution.py:1055
  212.9 6.0 fusion.57
  218.9 3.2 fusion.58
  222.2 5.3 fusion.13
  227.5 3.5 fusion.59
  231.0 5.4 add_convert_fusion.source
  236.4 56.7 %shard_map.235 = (f32[128,2048]{1,0:T(8,128)}, bf16[704,2048]{1,0:T(8,128)(2,1)}, bf16[704,2048]{1,0:T(8,128)(2,1)}, bf16[704,2048]{1,0:T(8,128)(2,1)}) custom-call(bf16[1024,2048]{1,0:T(8,128)(2,1)} %add_convert_fusion.source, bf16[704,1024]{1,0:T(8,128)(2,1)} %copy-done.15, bf16[704,1024]{1,0:T(8,128)(2,1)} %copy-done.14, ...), custom_call_target="tpu_custom_call" | custom-call | bytes 15000000 | tf_op jit(solution)/shard_map/pallas_call | solution.py:1220
  293.1 1.7 multiply_reduce_fusion.1
  294.8 2.5 multiply_add_fusion
  297.3 5.1 convolution_convert_fusion.1
  302.5 1.4 constant_dynamic-slice_fusion.4
  304.1 0.7 pad_maximum_fusion.1.half_ref
  304.9 18.6 %shard_map.236 = (bf16[4,128,2048]{2,1,0:T(8,128)(2,1)}, bf16[128,1024]{1,0:T(8,128)(2,1)}) custom-call(bf16[128,2048]{1,0:T(8,128)(2,1)} %copy-done.10, bf16[128,1024]{1,0:T(8,128)(2,1)} %pad_maximum_fusion.1.half_ref), custom_call_target="tpu_custom_call" | custom-call | bytes 7500000 | tf_op jit(solution)/shard_map/pallas_call | solution.py:1032
  323.5 5.3 fusion.60.d_branch_ref
  328.8 10.4 %shard_map.237 = (bf16[512,1024]{1,0:T(8,128)(2,1)}, bf16[512,1024]{1,0:T(8,128)(2,1)}, f32[1,256]{1,0:T(1,128)}, bf16[4,8,128,384]{3,2,1,0:T(8,128)(2,1)}, bf16[4,128,256]{2,1,0:T(8,128)(2,1)}) custom-call(f32[512,1024]{1,0:T(8,128)} %fusion.60.d_branch_ref, f32[512,1024]{1,0:T(8,128)} %get-tuple-element.95.core_ref, f32[4,512,256]{2,1,0:T(8,128)} %fusion.24.gate_ref, ...), custom_call_target="tpu_custom_call" | custom-call | flops 4000000000 | bytes 20000000 | tf_op jit(solution)/shard_map/pallas_call | solution.py:554
  339.2 36.7 %shard_map.238 = (bf16[8,512,256]{2,1,0:T(8,128)(2,1)}, bf16[4,128,1024]{2,1,0:T(8,128)(2,1)}) custom-call(bf16[512,256]{1,0:T(8,128)(2,1)} %bitcast.134, bf16[128,1024]{1,0:T(8,128)(2,1)} %get-tuple-element.98.half_ref), custom_call_target="tpu_custom_call" | custom-call | bytes 18750000 | tf_op jit(solution)/shard_map/pallas_call | solution.py:1270
  375.9 27.4 %shard_map.239 = (bf16[512,2048]{1,0:T(8,128)(2,1)}, f32[8,2048]{1,0:T(8,128)}, f32[8,2048]{1,0:T(8,128)}, f32[4,2048]{1,0:T(4,128)}) custom-call(bf16[8,4,128,384]{3,2,1,0:T(8,128)(2,1)} %bitcast.143, bf16[8,4,128,256]{3,2,1,0:T(8,128)(2,1)} %bitcast.145, bf16[4,512,512]{2,1,0:T(8,128)(2,1)} %copy-done.33, f32[4,8,512]{2,1,0:T(8,128)} %convert_select_fusion.tail_ref, ...), custom_call_target="tpu_custom_call" | custom-call | flops 12000000000 | bytes 20000000 | tf_op jit(solution)/shard_map/pallas_call | solution.py:592
  403.3 0.8 reshape.183
  404.1 0.6 collective-permute-start.2
  404.7 0.6 pad_maximum_fusion.2.small_ref
  405.4 1.3 constant_dynamic-slice_fusion.8
  406.7 2.6 fusion.30
  409.3 3.3 fusion.38
  412.6 2.7 add_convert_fusion.2
  415.3 7.0 %fusion.5 = f32[512,2048,1]{1,0,2:T(8,128)} fusion(bf16[2048,4,256]{2,1,0:T(4,128)(2,1)} %param.21, bf16[64,4,8,256]{3,2,1,0:T(8,128)(2,1)} %bitcast.146), kind=kOutput, calls=%fused_computation.11 | convolution fusion | flops 2147483648 | bytes 9437184 | tf_op jit(solution)/shard_map/thv,dhv->td/dot_general | solution.py:1550
  422.3 2.2 convert_element_type.110
  424.5 4.3 collective-permute-done.2
  428.8 1.7 collective-permute-start.3
  430.6 2.1 add_convert_fusion.4
  432.7 5.5 add_convert_fusion.1.gate_ref
  438.5 0.6 convert_dynamic-update-slice_fusion
  439.1 11.3 %fusion.4.normed_ref = bf16[512,2048]{1,0:T(8,128)(2,1)} fusion(f32[512,2048,1]{1,0,2:T(8,128)} %fusion.5, bf16[2048,4,512]{2,1,0:T(4,128)(2,1)} %param.19, bf16[64,4,8,512]{3,2,1,0:T(8,128)(2,1)} %bitcast.144), kind=kOutput, calls=%fused_computation.7 | convolution fusion | flops 4297064448 | bytes 16777216 | tf_op jit(solution)/shard_map/thc,dhc->td/dot_general | solution.py:1545
  450.5 6.9 %convolution_convert_fusion.qkv_ref = bf16[2048,2048]{1,0:T(8,128)(2,1)} fusion(bf16[512,2048]{1,0:T(8,128)(2,1)S(1)} %bitcast.130, bf16[512,2048]{1,0:T(8,128)(2,1)S(1)} %copy-done.37), kind=kOutput, calls=%fused_computation.1 | convolution fusion | flops 4299161600 | bytes 12582912 | tf_op jit(solution)/shard_map/dot_general | solution.py:71
  457.4 16.5 %reduce-scatter.5.cloned.1.call-done = bf16[256,1024]{1,0:T(8,128)(2,1)} async-done(((bf16[1024,1024]{1,0:T(8,128)(2,1)}), bf16[256,1024]{1,0:T(8,128)(2,1)}) %reduce-scatter.5.cloned.1.call-update) | async-done | bytes 524304 | tf_op jit(solution)/shard_map/reduce_scatter | solution.py:1533
  473.9 118.4 %shard_map.240 = (bf16[256,2048]{1,0:T(8,128)(2,1)}, bf16[256,1024]{1,0:T(8,128)(2,1)}, f32[128,2048]{1,0:T(8,128)}, f32[8,104,128]{2,1,0:T(8,128)}, bf16[704,51...) custom-call(bf16[2048,2048]{1,0:T(8,128)(2,1)} %convolution_convert_fusion.qkv_ref, ...), custom_call_target="tpu_custom_call" | custom-call | bytes 31250000 | tf_op jit(solution)/shard_map/pallas_call | solution.py:1356
  592.3 1.0 reduce_sum.59
  593.5 3.8 reshape.193
  597.3 2.4 convert_element_type.117
  599.7 2.5 reshape.195
  602.6 1.2 add_convert_fusion.3
  603.8 1.1 convert_bitcast_fusion.3
  604.9 2.7 copy.44
  607.5 3.3 convert_bitcast_fusion.1
  610.8 0.7 constant_dynamic-slice_fusion
  (124 shorter events, 4.5 us)
Async XLA Ops:
  7.2 214.9 %copy-start = (bf16[704,2048]{1,0:T(8,128)(2,1)S(1)}, bf16[704,2048]{1,0:T(8,128)(2,1)}, u32[]{:S(2)}) copy-start(bf16[704,2048]{1,0:T(8,128)(2,1)} %param.27) | copy-start | bytes 8650756
  7.2 126.8 %all-gather.2.cloned.1.call-start = ((), (), s32[]{:S(2)}) async-start(), calls=%async_computation.2 | async-start | bytes 4718592 | tf_op jit(solution)/shard_map/all_gather | solution.py:1408
  7.9 414.4 %reduce-scatter.3.cloned.1.call-start = ((), (), s32[]{:S(2)}) async-start(), calls=%async_computation.3 | async-start | bytes 4718592 | tf_op jit(solution)/shard_map/reduce_scatter | solution.py:1412
  8.7 33.2 %copy-start.23 = (f32[2048]{0:T(1024)}, f32[2048]{0:T(1024)S(1)}, u32[]{:S(2)}) copy-start(f32[2048]{0:T(1024)S(1)} %convert_element_type.92) | copy-start | bytes 24580
  10.0 32.0 %copy-start.29 = (f32[128]{0:T(128)}, f32[128]{0:T(128)S(1)}, u32[]{:S(2)}) copy-start(f32[128]{0:T(128)S(1)} %add_rsqrt_fusion.1) | copy-start | bytes 1540
  12.2 0.9 copy-start.11
  33.3 12.1 %copy-start.27 = (s32[512,4]{0,1:T(4,128)S(1)}, s32[512,4]{0,1:T(4,128)}, u32[]{:S(2)}) copy-start(s32[512,4]{0,1:T(4,128)} %param.28) | copy-start | bytes 24580
  33.3 12.8 %copy-start.28 = (s32[512,4]{0,1:T(4,128)S(1)}, s32[512,4]{0,1:T(4,128)}, u32[]{:S(2)}) copy-start(s32[512,4]{0,1:T(4,128)} %param.29) | copy-start | bytes 24580
  42.0 3.4 copy-start.33
  42.0 13.8 %collective-permute-start = (bf16[4,8,512]{2,1,0:T(8,128)(2,1)S(1)}, bf16[4,8,512]{2,1,0:T(8,128)(2,1)S(1)}, u32[]{:S(2)}, u32[]{:S(2)}) collective-permute-start(bf16[4,8,512]{2,1,0:T(8,128)(2,1)S(1)} %slice.40), channel_id=1, source_target_pairs={{0,1},{1,2},{2,3},{3,4},{4,5},{5,6},{6,7},{8,9},{9,10},{10,11},{11... | collective-permute-start | bytes 98312 | tf_op jit(solution)/shard_map/ppermute | solution.py:28
  46.1 8.4 %copy-start.26 = (bf16[4,4,512]{2,1,0:T(4,128)(2,1)S(1)}, bf16[4,4,512]{2,1,0:T(4,128)(2,1)}, u32[]{:S(2)}) copy-start(bf16[4,4,512]{2,1,0:T(4,128)(2,1)} %param.20) | copy-start | bytes 49156
  46.1 9.0 %copy-start.39 = (bf16[256]{0:T(256)(128)(2,1)S(1)}, bf16[256]{0:T(256)(128)(2,1)}, u32[]{:S(2)}) copy-start(bf16[256]{0:T(256)(128)(2,1)} %param.22) | copy-start | bytes 1540
  46.2 9.6 %copy-start.31 = (bf16[2048]{0:T(1024)(128)(2,1)S(1)}, bf16[2048]{0:T(1024)(128)(2,1)}, u32[]{:S(2)}) copy-start(bf16[2048]{0:T(1024)(128)(2,1)} %param.24) | copy-start | bytes 12292
  134.0 28.3 %collective-permute-start.1 = (bf16[512,1024]{1,0:T(8,128)(2,1)}, bf16[512,1024]{1,0:T(8,128)(2,1)S(1)}, u32[]{:S(2)}, u32[]{:S(2)}) collective-permute-start(bf16[512,1024]{1,0:T(8,128)(2,1)} %get-tuple-element.87), channel_id=1, source_target_pairs={{0,1},{1,0},{2,3},{3,2},{4,5},{5,4},{6,7},{7,6},{8,9},{9,8},{10,11... | collective-permute-start | bytes 3145736 | tf_op jit(solution)/shard_map/ppermute | solution.py:1399
  142.8 16.9 %copy-start.5 = (bf16[128,2048]{1,0:T(8,128)(2,1)S(1)}, bf16[128,2048]{1,0:T(8,128)(2,1)}, u32[]{:S(2)}) copy-start(bf16[128,2048]{1,0:T(8,128)(2,1)} %param.16) | copy-start | bytes 1572868
  161.1 133.7 %copy-start.2 = (f32[128,2048]{1,0:T(8,128)}, f32[128,2048]{1,0:T(8,128)S(1)}, u32[]{:S(2)}) copy-start(f32[128,2048]{1,0:T(8,128)S(1)} %get-tuple-element.161) | copy-start | bytes 3145732
  162.3 50.6 %copy-start.16 = (bf16[512,1024]{1,0:T(8,128)(2,1)}, bf16[512,1024]{1,0:T(8,128)(2,1)S(1)}, u32[]{:S(2)}) copy-start(bf16[512,1024]{1,0:T(8,128)(2,1)S(1)} %collective-permute-done.1) | copy-start | bytes 3145732
  212.9 6.0 copy-start.4
  212.9 6.0 copy-start.36
  218.9 3.2 copy-start.9
  222.1 5.3 copy-start.35
  227.4 3.6 copy-start.15
  227.5 3.6 copy-start.14
  236.4 58.4 %copy-start.12 = (bf16[128,2048]{1,0:T(8,128)(2,1)S(1)}, bf16[128,2048]{1,0:T(8,128)(2,1)}, u32[]{:S(2)}) copy-start(bf16[128,2048]{1,0:T(8,128)(2,1)} %param.17) | copy-start | bytes 1572868
  293.1 4.2 copy-start.13
  302.4 1.6 copy-start.7
  302.4 171.5 %reduce-scatter.5.cloned.1.call-start = ((), (), s32[]{:S(2)}) async-start(), calls=%async_computation.4 | async-start | bytes 2621440 | tf_op jit(solution)/shard_map/reduce_scatter | solution.py:1533
  302.5 21.0 %copy-start.34 = (bf16[4,256,2048]{2,1,0:T(8,128)(2,1)S(1)}, bf16[4,256,2048]{2,1,0:T(8,128)(2,1)}, u32[]{:S(2)}) copy-start(bf16[4,256,2048]{2,1,0:T(8,128)(2,1)} %param.23) | copy-start | bytes 12582916
  304.0 0.9 copy-start.10
  375.9 28.8 %copy-start.32 = (f32[1,256]{1,0:T(1,128)S(1)}, f32[1,256]{1,0:T(1,128)}, u32[]{:S(2)}) copy-start(f32[1,256]{1,0:T(1,128)} %get-tuple-element.121) | copy-start | bytes 3076
  404.1 24.7 %collective-permute-start.2 = (bf16[512,1024]{1,0:T(8,128)(2,1)}, bf16[512,1024]{1,0:T(8,128)(2,1)}, u32[]{:S(2)}, u32[]{:S(2)}) collective-permute-start(bf16[512,1024]{1,0:T(8,128)(2,1)} %get-tuple-element.112), channel_id=1, source_target_pairs={{0,1},{1,0},{2,3},{3,2},{4,5},{5,4},{6,7},{7,6},{8,9},{9,8},{10,11... | collective-permute-start | bytes 3145736 | tf_op jit(solution)/shard_map/ppermute | solution.py:1399
  406.6 2.6 copy-start.38
  409.3 3.3 copy-start.17
  409.3 3.3 copy-start.18
  415.3 13.5 %copy-start.25 = (f32[8,2048]{1,0:T(8,128)S(1)}, f32[8,2048]{1,0:T(8,128)}, u32[]{:S(2)}) copy-start(f32[8,2048]{1,0:T(8,128)} %get-tuple-element.116) | copy-start | bytes 196612
  422.3 8.3 %copy-start.3 = (f32[128,2048]{1,0:T(8,128)S(1)}, f32[128,2048]{1,0:T(8,128)}, u32[]{:S(2)}) copy-start(f32[128,2048]{1,0:T(8,128)} %copy-done.2) | copy-start | bytes 3145732
  428.8 9.4 %collective-permute-start.3 = (f32[3,2048]{1,0:T(4,128)S(1)}, f32[3,2048]{1,0:T(4,128)S(1)}, u32[]{:S(2)}, u32[]{:S(2)}) collective-permute-start(f32[3,2048]{1,0:T(4,128)S(1)} %slice.37), channel_id=1, source_target_pairs={{1,0},{2,1},{3,2},{4,3},{5,4},{6,5},{7,6},{9,8},{10,9},{11,10},{12... | collective-permute-start | bytes 73736 | tf_op jit(solution)/shard_map/ppermute | solution.py:28
  432.7 5.5 copy-start.22
  439.1 11.4 %copy-start.20 = (bf16[4,128,2048]{2,1,0:T(8,128)(2,1)S(1)}, bf16[4,128,2048]{2,1,0:T(8,128)(2,1)}, u32[]{:S(2)}) copy-start(bf16[4,128,2048]{2,1,0:T(8,128)(2,1)} %get-tuple-element.79) | copy-start | bytes 6291460
  439.1 11.4 %copy-start.37 = (bf16[512,2048]{1,0:T(8,128)(2,1)S(1)}, bf16[512,2048]{1,0:T(8,128)(2,1)}, u32[]{:S(2)}) copy-start(bf16[512,2048]{1,0:T(8,128)(2,1)} %convert_dynamic-update-slice_fusion) | copy-start | bytes 6291460
  593.4 8.8 %copy-start.21 = (f32[104,128]{1,0:T(8,128)}, f32[104,128]{1,0:T(8,128)S(1)}, u32[]{:S(2)}) copy-start(f32[104,128]{1,0:T(8,128)S(1)} %reduce_sum.59) | copy-start | bytes 159748
  593.4 8.8 %copy-start.6 = (bf16[128,2048]{1,0:T(8,128)(2,1)S(1)}, bf16[128,2048]{1,0:T(8,128)(2,1)}, u32[]{:S(2)}) copy-start(bf16[128,2048]{1,0:T(8,128)(2,1)} %param.16) | copy-start | bytes 1572868
  593.4 8.8 %copy-start.8 = (f32[128,2048]{1,0:T(8,128)S(1)}, f32[128,2048]{1,0:T(8,128)}, u32[]{:S(2)}) copy-start(f32[128,2048]{1,0:T(8,128)} %get-tuple-element.126) | copy-start | bytes 3145732
  593.4 8.8 %copy-start.24 = (f32[2048]{0:T(1024)S(1)}, f32[2048]{0:T(1024)}, u32[]{:S(2)}) copy-start(f32[2048]{0:T(1024)} %copy-done.23) | copy-start | bytes 24580
  593.4 8.8 %copy-start.30 = (f32[128]{0:T(128)S(1)}, f32[128]{0:T(128)}, u32[]{:S(2)}) copy-start(f32[128]{0:T(128)} %copy-done.29) | copy-start | bytes 1540
  599.7 4.1 copy-start.19
  602.2 1.5 slice-start
  603.8 8.9 %copy-start.1 = (bf16[704,2048]{1,0:T(8,128)(2,1)S(1)}, bf16[704,2048]{1,0:T(8,128)(2,1)}, u32[]{:S(2)}) copy-start(bf16[704,2048]{1,0:T(8,128)(2,1)} %param.27) | copy-start | bytes 8650756
Sparse Core Ops, SparseCore 0:
  10.2 77.4 all-gather.1
  302.5 96.6 reduce-scatter.2
  430.7 43.1 reduce-scatter.4
